TPU v7x, 32 devices: a whole 2x2x4 slice. The times are simulated.
32 devices in a mesh: dev: 32 (over z, y, x, core).
Axes of the slice: x: 2, y: 2, z: 4, core: 2. Of those that a mesh axis runs over, the one named last changes fastest.
Arguments:
- tokens: bfloat16 [24576, 1024], P('dev'), may hold values from -6 to 6
- seq_ids: int32 [24576], P('dev'), may hold values from 0 to 32, as said below
- positions: int32 [24576], P('dev'), may hold values from 0 to 1406, as said below
- w_qkv: bfloat16 [1024, 3072], P('dev'), may hold values from -0.1875 to 0.1875
- w_out: bfloat16 [1024, 1024], P('dev'), may hold values from -1.5 to 1.5
- w_in: bfloat16 [1024, 5248], P('dev'), may hold values from -0.1875 to 0.1875
- w_down: bfloat16 [2624, 1024], P(None, 'dev'), may hold values from -0.15625 to 0.15625
- gain_attn: bfloat16 [1024], P('dev'), may hold values from 0.099609375 to 1.8984375
- gain_mlp: bfloat16 [1024], P('dev'), may hold values from 0.099609375 to 1.8984375
- cotangent: bfloat16 [24576, 1024], P('dev'), may hold values from -6 to 6
Outputs:
- layer_out: bfloat16 [24576, 1024], P('dev')
- tokens_grad: bfloat16 [24576, 1024], P('dev')
- qkv_grad: float32 [1024, 3072], P('dev')
- out_grad: float32 [1024, 1024], P('dev')
- in_grad: float32 [1024, 5248], P('dev')
- down_grad: float32 [2624, 1024], P(None, 'dev')
- attn_gain_grad: float32 [1024], P('dev')
- mlp_gain_grad: float32 [1024], P('dev')
Inputs may be any that keep to these rules, and one draw needn't show every extreme that they name: `seq_ids`: sequence numbers rise along the tokens from 0; every device's rows hold exactly one sequence start, at least 64 rows from either end of its rows, so the first and last 64 rows of a device lie in one sequence together with the 64 rows beyond them on the neighbouring device. `positions`: position within the sequence: 0 at a sequence's first token, rising by one.
All inputs are finite; a program needn't handle non-finite values.
Results may differ from a plain program's by a relative error of at most 0.017.
Values may be sent and summed in bfloat16 or wider, within the bound.
A program may use at most 256 MiB of HBM per device.

v0:
```python
import math

import jax
import jax.numpy as jnp
from jax import lax
from jax.sharding import PartitionSpec as P

HDIM = 64
HALF = 64


epsilon = 1e-05
masked_score = -1e30


def padded(cells, sides, width):
    for axis, dim in sides:
        count = lax.axis_size(axis)
        ends = count - 1
        head = lax.slice_in_dim(cells, 0, width, axis=dim)
        tail = lax.slice_in_dim(cells, cells.shape[dim] - width, cells.shape[dim], axis=dim)
        cells = jnp.concatenate(
            [
                lax.ppermute(tail, axis, [(i, (i + 1) % count) for i in range(ends)]),
                cells,
                lax.ppermute(head, axis, [((i + 1) % count, i) for i in range(ends)]),
            ],
            axis=dim,
        )
    return cells


def passed_along(value, axis, steps):
    count = lax.axis_size(axis)
    leading, last = (max(0, -steps), min(count, count - steps))
    return lax.ppermute(value, axis, [(source, source + steps) for source in range(leading, last)])


def layer_norm(values):
    centred = values - jnp.mean(values, axis=-1, keepdims=True)
    inverse_std = lax.rsqrt(jnp.mean(centred * centred, axis=-1, keepdims=True) + epsilon)
    return (centred * inverse_std, inverse_std)


def norm_back(grad_normed, normed, inverse_std):
    mean_grad = jnp.mean(grad_normed, axis=-1, keepdims=True)
    mean_mixed = jnp.mean(grad_normed * normed, axis=-1, keepdims=True)
    return inverse_std * (grad_normed - mean_grad - normed * mean_mixed)


def rope_tables(positions, head_size):
    half_size = head_size // 2
    inverse_freq = 10000.0 ** (-(jnp.arange(half_size).astype(jnp.float32) * 2.0 / head_size))
    angles = positions.astype(jnp.float32)[:, None] * inverse_freq[None, :]
    angles = jnp.concatenate([angles, angles], axis=-1)
    return (jnp.cos(angles)[:, None, :], jnp.sin(angles)[:, None, :])


def rotate_half(values):
    half_size = values.shape[-1] // 2
    return jnp.concatenate([-values[..., half_size:], values[..., :half_size]], axis=-1)


def unrotate_half(values):
    half_size = values.shape[-1] // 2
    return jnp.concatenate([values[..., half_size:], -values[..., :half_size]], axis=-1)


def apply_rope(values, cosine, sine_table):
    return values * cosine + rotate_half(values) * sine_table


def rope_back(grads_in, cosine, sine_table):
    return grads_in * cosine + unrotate_half(grads_in * sine_table)


def contract_rows(first_mat, second_mat):
    return lax.dot_general(
        first_mat, second_mat, (((0,), (0,)), ((), ())), preferred_element_type=jnp.float32
    )


def contract_cols(first_mat, second_mat):
    return lax.dot_general(
        first_mat, second_mat, (((1,), (1,)), ((), ())), preferred_element_type=jnp.float32
    )


def geglu(gate_part, up_part):
    return jax.nn.gelu(gate_part, approximate=False) * up_part


def local(tokens, seq_ids, positions, w_qkv, w_out, w_in, w_down, gain_attn, gain_mlp, cotangent):
    tok_rows, model_width = tokens.shape
    hidden_units = w_down.shape[0]
    head_count = model_width // HDIM
    dev_count = lax.axis_size("dev")
    dev_index = lax.axis_index("dev")
    query_block = math.gcd(tok_rows, 512)
    window_rows = query_block + 2 * HALF
    score_scale = 1.0 / math.sqrt(HDIM)
    block_total = tok_rows // query_block
    cosine, sine_table = rope_tables(positions, HDIM)
    key_ids = jnp.concatenate(
        [
            jnp.full((HALF,), seq_ids[0], jnp.int32),
            seq_ids,
            jnp.full((HALF,), seq_ids[-1], jnp.int32),
        ]
    )
    key_live = jnp.concatenate(
        [
            jnp.full((HALF,), dev_index > 0, jnp.bool_),
            jnp.ones((tok_rows,), jnp.bool_),
            jnp.full((HALF,), dev_index < dev_count - 1, jnp.bool_),
        ]
    )
    offsets = jnp.arange(query_block)[:, None] - jnp.arange(window_rows)[None, :] + HALF
    nearby = jnp.abs(offsets) <= HALF
    gathered = (
        lax.all_gather(w_qkv, "dev", axis=0, tiled=True),
        lax.all_gather(w_out, "dev", axis=0, tiled=True),
        lax.all_gather(w_in, "dev", axis=0, tiled=True),
        lax.all_gather(gain_attn, "dev", axis=0, tiled=True),
        lax.all_gather(gain_mlp, "dev", axis=0, tiled=True),
    )
    full_down = lax.all_gather(w_down, "dev", axis=1, tiled=True)
    full_qkv, full_out, full_in, full_gain_attn, full_gain_mlp = gathered
    inputs = tokens.astype(jnp.float32)
    normed_attn, inv_attn = layer_norm(inputs)
    h_attn = (normed_attn * full_gain_attn.astype(jnp.float32)).astype(jnp.bfloat16)
    projected = jnp.dot(h_attn, full_qkv, preferred_element_type=jnp.float32).reshape(
        tok_rows, 3, head_count, HDIM
    )
    queries = apply_rope(projected[:, 0], cosine, sine_table).astype(jnp.bfloat16)
    keys_own = (
        apply_rope(projected[:, 1], cosine, sine_table)
        .astype(jnp.bfloat16)
        .reshape(tok_rows, model_width)
    )
    values_own = projected[:, 2].astype(jnp.bfloat16).reshape(tok_rows, model_width)
    key_values = padded(jnp.concatenate([keys_own, values_own], axis=1), (("dev", 0),), HALF)

    def block_scores(block_start):
        query_tile = queries[block_start : block_start + query_block]
        window = key_values[block_start : block_start + window_rows]
        key_tile = window[:, :model_width].reshape(window_rows, head_count, HDIM)
        value_tile = window[:, model_width:].reshape(window_rows, head_count, HDIM)
        query_ids = seq_ids[block_start : block_start + query_block]
        allowed = (
            nearby
            & (query_ids[:, None] == key_ids[None, block_start : block_start + window_rows])
            & key_live[None, block_start : block_start + window_rows]
        )
        scores = (
            jnp.einsum("qhd,khd->hqk", query_tile, key_tile, preferred_element_type=jnp.float32)
            * score_scale
        )
        scores = jnp.where(allowed[None], scores, masked_score)
        return (query_tile, key_tile, value_tile, scores)

    log_totals = []
    block_outputs = []
    for block_number in range(block_total):
        block_start = block_number * query_block
        query_tile, key_tile, value_tile, scores = block_scores(block_start)
        row_peak = jnp.max(scores, axis=-1, keepdims=True)
        exponent = jnp.exp(scores - row_peak)
        row_total = jnp.sum(exponent, axis=-1, keepdims=True)
        attn_probs = (exponent / row_total).astype(jnp.bfloat16)
        log_totals.append(row_peak + jnp.log(row_total))
        block_outputs.append(
            jnp.einsum(
                "hqk,khd->qhd", attn_probs, value_tile, preferred_element_type=jnp.float32
            ).reshape(query_block, model_width)
        )
    mixed = jnp.concatenate(block_outputs, axis=0).astype(jnp.bfloat16)
    residual = inputs + jnp.dot(mixed, full_out, preferred_element_type=jnp.float32)
    normed_mlp, inv_mlp = layer_norm(residual)
    h_mlp = (normed_mlp * full_gain_mlp.astype(jnp.float32)).astype(jnp.bfloat16)
    gate_up = jnp.dot(h_mlp, full_in, preferred_element_type=jnp.float32)
    gate_part = gate_up[:, :hidden_units]
    up_part = gate_up[:, hidden_units:]
    activated = geglu(gate_part, up_part).astype(jnp.bfloat16)
    layer_out = (
        residual + jnp.dot(activated, full_down, preferred_element_type=jnp.float32)
    ).astype(jnp.bfloat16)
    full_qkv, full_out, full_in, full_gain_attn, full_gain_mlp = (
        lax.all_gather(w_qkv, "dev", axis=0, tiled=True),
        lax.all_gather(w_out, "dev", axis=0, tiled=True),
        lax.all_gather(w_in, "dev", axis=0, tiled=True),
        lax.all_gather(gain_attn, "dev", axis=0, tiled=True),
        lax.all_gather(gain_mlp, "dev", axis=0, tiled=True),
    )
    full_down = lax.all_gather(w_down, "dev", axis=1, tiled=True)
    d_activated = contract_cols(cotangent, full_down)
    _, geglu_back = jax.vjp(geglu, gate_part, up_part)
    d_gate, d_up = geglu_back(d_activated)
    d_gate_up = jnp.concatenate([d_gate, d_up], axis=1).astype(jnp.bfloat16)
    d_h_mlp = contract_cols(d_gate_up, full_in)
    mlp_gain_grad = jnp.sum(d_h_mlp * normed_mlp, axis=0)
    d_residual = cotangent.astype(jnp.float32) + norm_back(
        d_h_mlp * full_gain_mlp.astype(jnp.float32), normed_mlp, inv_mlp
    )
    d_branch = d_residual.astype(jnp.bfloat16)
    d_mixed = contract_cols(d_branch, full_out).astype(jnp.bfloat16)
    d_query_list = []
    d_window = jnp.zeros((tok_rows + 2 * HALF, 2 * model_width), jnp.float32)
    for block_number in range(block_total):
        block_start = block_number * query_block
        query_tile, key_tile, value_tile, scores = block_scores(block_start)
        attn_probs = jnp.exp(scores - log_totals[block_number])
        grad_tile = d_mixed[block_start : block_start + query_block].reshape(
            query_block, head_count, HDIM
        )
        d_probs = jnp.einsum(
            "qhd,khd->hqk", grad_tile, value_tile, preferred_element_type=jnp.float32
        )
        d_scores = (
            attn_probs * (d_probs - jnp.sum(attn_probs * d_probs, axis=-1, keepdims=True))
        ).astype(jnp.bfloat16)
        d_query_list.append(
            jnp.einsum("hqk,khd->qhd", d_scores, key_tile, preferred_element_type=jnp.float32)
            * score_scale
        )
        d_keys = (
            jnp.einsum("hqk,qhd->khd", d_scores, query_tile, preferred_element_type=jnp.float32)
            * score_scale
        )
        d_values = jnp.einsum(
            "hqk,qhd->khd",
            attn_probs.astype(jnp.bfloat16),
            grad_tile,
            preferred_element_type=jnp.float32,
        )
        window_grad = jnp.concatenate(
            [d_keys.reshape(window_rows, model_width), d_values.reshape(window_rows, model_width)],
            axis=1,
        )
        d_window = d_window.at[block_start : block_start + window_rows].add(window_grad)
    from_right = passed_along(d_window[:HALF].astype(jnp.bfloat16), "dev", -1).astype(jnp.float32)
    from_left = passed_along(d_window[tok_rows + HALF :].astype(jnp.bfloat16), "dev", 1).astype(
        jnp.float32
    )
    d_own = d_window[HALF : tok_rows + HALF]
    d_own = d_own.at[:HALF].add(from_left).at[tok_rows - HALF :].add(from_right)
    d_query_all = jnp.concatenate(d_query_list, axis=0)
    d_key_all = d_own[:, :model_width].reshape(tok_rows, head_count, HDIM)
    d_projected = jnp.concatenate(
        [
            rope_back(d_query_all, cosine, sine_table).reshape(tok_rows, model_width),
            rope_back(d_key_all, cosine, sine_table).reshape(tok_rows, model_width),
            d_own[:, model_width:],
        ],
        axis=1,
    ).astype(jnp.bfloat16)
    d_h_attn = contract_cols(d_projected, full_qkv)
    attn_gain_grad = jnp.sum(d_h_attn * normed_attn, axis=0)
    tokens_grad = (
        d_residual + norm_back(d_h_attn * full_gain_attn.astype(jnp.float32), normed_attn, inv_attn)
    ).astype(jnp.bfloat16)
    down_grad = contract_rows(activated, cotangent)
    in_grad = contract_rows(h_mlp, d_gate_up)
    out_grad = contract_rows(mixed, d_branch)
    qkv_grad = contract_rows(h_attn, d_projected)
    qkv_part, out_part, in_part, attn_gain_part, mlp_gain_part = (
        lax.psum_scatter(qkv_grad, "dev", scatter_dimension=0, tiled=True),
        lax.psum_scatter(out_grad, "dev", scatter_dimension=0, tiled=True),
        lax.psum_scatter(in_grad, "dev", scatter_dimension=0, tiled=True),
        lax.psum_scatter(attn_gain_grad, "dev", scatter_dimension=0, tiled=True),
        lax.psum_scatter(mlp_gain_grad, "dev", scatter_dimension=0, tiled=True),
    )
    down_part = lax.psum_scatter(down_grad, "dev", scatter_dimension=1, tiled=True)
    return (
        layer_out,
        tokens_grad,
        qkv_part,
        out_part,
        in_part,
        down_part,
        attn_gain_part,
        mlp_gain_part,
    )


def solution(mesh):
    return jax.shard_map(
        local,
        mesh=mesh,
        in_specs=(
            P("dev", None),
            P("dev"),
            P("dev"),
            P("dev", None),
            P("dev", None),
            P("dev", None),
            P(None, "dev"),
            P("dev"),
            P("dev"),
            P("dev", None),
        ),
        out_specs=(
            P("dev", None),
            P("dev", None),
            P("dev", None),
            P("dev", None),
            P("dev", None),
            P(None, "dev"),
            P("dev"),
            P("dev"),
        ),
        check_vma=False,
    )
```

profile of v0, /device:TPU:0, one launch (start us, length us, event | category | flops | bytes accessed | tf_op | source)
XLA Modules:
  0.0 1058.5 jit_solution(498574114154215598)
XLA Ops:
  13.9 42.2 %all-reduce.10 = (bf16[1024]{0:T(1024)(128)(2,1)S(1)}, bf16[1024]{0:T(1024)(128)(2,1)S(1)}) all-reduce(bf16[1024]{0:T(1024)(128)(2,1)S(1)} %dynamic-update-slice.15, bf16[1024]{0:T(1024)(128)(2,1)S(1)} %dynamic-update-slice.16), channel_id=1, replica_groups=mesh['dev'=32] {'dev'}, use_global_device_ids=true, to_apply=%add.5 | all-reduce | flops 2048 | bytes 8192
  61.1 21.9 %all-gather.5.cloned.1.call-done = bf16[1024,3072]{1,0:T(8,128)(2,1)} async-done(((bf16[32,3072]{1,0:T(8,128)(2,1)}), bf16[1024,3072]{1,0:T(8,128)(2,1)}) %all-gather.5.cloned.1.call-update) | async-done | bytes 6291472 | tf_op jit(solution)/shard_map/all_gather | solution.py:121
  83.1 8.2 fusion.74
  91.3 2.8 convert.40
  96.6 2.3 slice_negate_fusion.2
  98.9 3.4 fusion.43
  103.1 2.2 collective-permute-start
  107.2 2.7 collective-permute-done.1
  109.9 7.2 pad_maximum_fusion.12
  126.2 3.0 fusion.54
  129.3 3.0 fusion.52
  132.3 4.2 fusion.53
  136.5 6.6 all-gather.7.cloned.1.call-done
  143.1 4.5 fusion.86
  148.0 84.6 %all-gather.9.cloned.1.call-done = bf16[1024,5248]{1,0:T(8,128)(2,1)} async-done(((bf16[32,5248]{1,0:T(8,128)(2,1)}), bf16[1024,5248]{1,0:T(8,128)(2,1)}) %all-gather.9.cloned.1.call-update) | async-done | bytes 10747920 | tf_op jit(solution)/shard_map/all_gather | solution.py:123
  232.6 15.8 %fusion.76 = f32[768,5248]{1,0:T(8,128)} fusion(bf16[1024,5248]{1,0:T(8,128)(2,1)} %all-gather.9.cloned.1.call-done, f32[768,1024]{1,0:T(8,128)S(1)} %get-tuple-element.130, f32[1024]{0:T(1024)S(1)} %convert_element_type.106, f32[768]{0:T(1024)S(1)} %add_rsqrt_fusion, f32[768]{0:T(1024)S(1)} %broadcast_multiply_fusion.6), kind=kOutput, calls=%fused_computation.180 | convolution fusion | flops 8257536000 | bytes 30025728 | tf_op jit(solution)/shard_map/dot_general | solution.py:181
  248.4 51.5 %all-gather.11.cloned.1.call-done = bf16[2624,1024]{0,1:T(8,128)(2,1)} async-done(((bf16[2624,32]{0,1:T(8,128)(2,1)}), bf16[2624,1024]{0,1:T(8,128)(2,1)}) %all-gather.11.cloned.1.call-update) | async-done | bytes 5373968 | tf_op jit(solution)/shard_map/all_gather | solution.py:127
  300.0 29.7 %add_convert_fusion = (bf16[768,2624]{1,0:T(8,128)(2,1)}, f32[768,2624]{1,0:T(8,128)}, f32[768,2624]{1,0:T(8,128)}) fusion(f32[768,5248]{1,0:T(8,128)} %fusion.76, bf16[768,1024]{1,0:T(8,128)(2,1)} %param.29, bf16[2624,1024]{0,1:T(8,128)(2,1)} %all-gather.11.cloned.1.call-done), kind=kOutput, calls=%fused_computation.3 | convolution fusion | flops 4274307072 | bytes 43220992 | tf_op jit(solution)/shard_map/dot_general | solution.py:84
  329.7 15.2 %multiply_convert_fusion = (bf16[768,2624]{1,0:T(8,128)(2,1)}, bf16[768,2624]{1,0:T(8,128)(2,1)}) fusion(f32[768,2624]{1,0:T(8,128)} %get-tuple-element.131, f32[768,2624]{1,0:T(8,128)} %get-tuple-element.81, f32[768,5248]{1,0:T(8,128)} %fusion.76), kind=kLoop, calls=%fused_computation.2 | loop fusion | flops 12091392 | bytes 40304640 | tf_op jit(solution)/shard_map/convert.7
  344.9 16.6 %multiply_reduce_fusion.3 = (f32[1024]{0:T(1024)}, f32[768]{0:T(1024)S(1)}, f32[768]{0:T(1024)S(1)}, f32[768,1024]{1,0:T(8,128)}) fusion(f32[768,1024]{1,0:T(8,128)S(1)} %get-tuple-element.130, f32[768]{0:T(1024)S(1)} %add_rsqrt_fusion, f32[768]{0:T(1024)S(1)} %broadcast_multiply_fusion.6, f32[1024]{0:T(1024)S(1)} %convert_element_type.106, ...), kind=kOutput, calls=%fused_computation.91 | convolution fusion | flops 8276800512 | bytes 25120768 | tf_op jit(solution)/shard_map/dot_general | solution.py:84
  361.5 3.1 multiply_add_fusion
  366.2 3.8 fusion.55
  370.1 11.4 %fusion.87 = f32[2624,1024]{0,1:T(8,128)} fusion(bf16[768,2624]{1,0:T(8,128)(2,1)} %get-tuple-element.83, bf16[768,1024]{1,0:T(8,128)(2,1)} %param.29), kind=kOutput, calls=%fused_computation.190 | convolution fusion | flops 4127195136 | bytes 16351232 | tf_op jit(solution)/shard_map/dot_general | solution.py:78
  382.2 4.4 convolution_convert_fusion
  394.0 5.7 multiply_reduce_fusion.1
  403.8 3.9 multiply_reduce_fusion
  407.8 3.8 multiply_convert_fusion.2
  413.3 3.9 multiply_reduce_fusion.2
  417.3 3.7 multiply_convert_fusion.4
  421.0 2.1 convolution_multiply_fusion.2
  426.8 2.4 fusion.31
  434.6 4.3 slice.330
  440.5 3.2 collective-permute-start.2
  451.5 6.3 scatter-add.21
  457.8 2.7 slice_add_fusion.2
  460.5 6.3 scatter-add.24
  466.8 3.2 slice.392
  470.0 2.2 slice.335
  479.9 5.7 fusion.38
  485.6 12.5 %fusion.50 = f32[1024,3072]{1,0:T(8,128)} fusion(bf16[768,1024]{0,1:T(8,128)(2,1)} %slice.392, bf16[768,1024]{0,1:T(8,128)(2,1)} %get-tuple-element.108, bf16[768,1024]{0,1:T(8,128)(2,1)} %get-tuple-element.107, bf16[768,1024]{1,0:T(8,128)(2,1)S(1)} %copy-done.6, f32[1024]{0:T(1024)S(1)} %copy-done.45, f32[768]{0:T(1024)S(1)} %copy-done.47, ...), kind=kOutput, calls=%fused_computation.106 | convolution fusion | flops 4849926144 | bytes 18884608 | tf_op jit(solution)/shard_map/dot_general | solution.py:78
  498.1 17.9 %fusion.10 = f32[1024,5248]{1,0:T(8,128)} fusion(bf16[768,2624]{1,0:T(8,128)(2,1)} %get-tuple-element.82, bf16[768,2624]{1,0:T(8,128)(2,1)} %get-tuple-element.80, f32[768,1024]{1,0:T(8,128)S(1)} %get-tuple-element.130, f32[1024]{0:T(1024)S(1)} %convert_element_type.106, f32[768]{0:T(1024)S(1)} %add_rsqrt_fusion, f32[768]{0:T(1024)S(1)} %broadcast_multiply_fusion.6), kind=kOutput, calls=%fused_computation.47 | convolution fusion | flops 8273657856 | bytes 32712704 | tf_op jit(solution)/shard_map/dot_general | solution.py:78
  516.1 10.2 add_convert_fusion.1
  526.3 10.8 %fusion.27 = (f32[1024]{0:T(1024)S(1)}, f32[768]{0:T(1024)S(1)}, f32[768]{0:T(1024)S(1)}, f32[768,1024]{1,0:T(8,128)}) fusion(bf16[768,1024]{1,0:T(8,128)(2,1)S(1)} %copy-done.7, f32[768]{0:T(1024)S(1)} %copy-done.47, f32[768]{0:T(1024)S(1)} %copy-done.42, f32[1024]{0:T(1024)S(1)} %copy-done.45, bf16[1024,3072]{1,0:T(8,128)(2,1)} %all-gather.5.cloned.1.call-done, ...), kind=kOutput, calls=%fused_computation.68 | convolution fusion | flops 4853068800 | bytes 15749120 | tf_op jit(solution)/shard_map/dot_general | solution.py:84
  537.1 53.2 %all-reduce.9 = (f32[1024]{0:T(1024)S(1)}, f32[1024]{0:T(1024)S(1)}) all-reduce(f32[1024]{0:T(1024)S(1)} %get-tuple-element.70, f32[1024]{0:T(1024)S(1)} %copy-done.48), channel_id=6, replica_groups=mesh['dev'=32] {'dev'}, use_global_device_ids=true, to_apply=%region_22.23.clone | all-reduce | flops 2048 | bytes 16384
  591.5 4.5 fusion.26
  596.0 61.6 %reduce-scatter.11.cloned.1.call-done = f32[2624,32]{0,1:T(8,128)} async-done(((f32[2624,1024]{0,1:T(8,128)}), f32[2624,32]{0,1:T(8,128)}) %reduce-scatter.11.cloned.1.call-update) | async-done | bytes 335888 | tf_op jit(solution)/shard_map/reduce_scatter | solution.py:273
  657.6 161.1 %reduce-scatter.5.cloned.1.call-done = f32[32,3072]{1,0:T(8,128)} async-done(((f32[1024,3072]{1,0:T(8,128)}), f32[32,3072]{1,0:T(8,128)}) %reduce-scatter.5.cloned.1.call-update) | async-done | bytes 393232 | tf_op jit(solution)/shard_map/reduce_scatter | solution.py:267
  818.6 232.6 %reduce-scatter.9.cloned.1.call-done = f32[32,5248]{1,0:T(8,128)} async-done(((f32[1024,5248]{1,0:T(8,128)}), f32[32,5248]{1,0:T(8,128)}) %reduce-scatter.9.cloned.1.call-update) | async-done | bytes 671760 | tf_op jit(solution)/shard_map/reduce_scatter | solution.py:269
  (214 shorter events, 68.9 us)
Async XLA Ops:
  7.2 52.4 %copy-start.43 = (s32[768]{0:T(1024)S(1)}, s32[768]{0:T(1024)}, u32[]{:S(2)}) copy-start(s32[768]{0:T(1024)} %param.21) | copy-start | bytes 9220
  7.2 51.3 %copy-start.5 = (bf16[768,1024]{1,0:T(8,128)(2,1)S(1)}, bf16[768,1024]{1,0:T(8,128)(2,1)}, u32[]{:S(2)}) copy-start(bf16[768,1024]{1,0:T(8,128)(2,1)} %param.20) | copy-start | bytes 4718596
  7.2 75.9 %all-gather.5.cloned.1.call-start = ((), (), s32[]{:S(2)}) async-start(), calls=%async_computation.4 | async-start | bytes 6488064 | tf_op jit(solution)/shard_map/all_gather | solution.py:121
  7.9 135.1 %all-gather.7.cloned.1.call-start = ((), (), s32[]{:S(2)}) async-start(), calls=%async_computation.5 | async-start | bytes 2162688 | tf_op jit(solution)/shard_map/all_gather | solution.py:122
  8.7 223.9 %all-gather.9.cloned.1.call-start = ((), (), s32[]{:S(2)}) async-start(), calls=%async_computation.6 | async-start | bytes 11083776 | tf_op jit(solution)/shard_map/all_gather | solution.py:123
  9.4 290.5 %all-gather.11.cloned.1.call-start = ((), (), s32[]{:S(2)}) async-start(), calls=%async_computation.7 | async-start | bytes 5677056 | tf_op jit(solution)/shard_map/all_gather | solution.py:127
  10.0 586.0 %reduce-scatter.7.cloned.1.call-start = ((), (), s32[]{:S(2)}) async-start(), calls=%async_computation.9 | async-start | bytes 4325376 | tf_op jit(solution)/shard_map/reduce_scatter | solution.py:268
  56.1 35.2 %copy-start.44 = (f32[1024]{0:T(1024)}, f32[1024]{0:T(1024)S(1)}, u32[]{:S(2)}) copy-start(f32[1024]{0:T(1024)S(1)} %convert_element_type.96) | copy-start | bytes 12292
  58.5 32.8 %copy-start.41 = (f32[768]{0:T(1024)}, f32[768]{0:T(1024)S(1)}, u32[]{:S(2)}) copy-start(f32[768]{0:T(1024)S(1)} %broadcast_multiply_fusion.7) | copy-start | bytes 9220
  59.1 32.2 %copy-start.46 = (f32[768]{0:T(1024)}, f32[768]{0:T(1024)S(1)}, u32[]{:S(2)}) copy-start(f32[768]{0:T(1024)S(1)} %add_rsqrt_fusion.1) | copy-start | bytes 9220
  59.6 39.3 %copy-start.32 = (f32[768,64]{0,1:T(8,128)}, f32[768,64]{0,1:T(8,128)S(1)}, u32[]{:S(2)}) copy-start(f32[768,64]{0,1:T(8,128)S(1)} %get-tuple-element.114) | copy-start | bytes 589828
  59.6 42.8 %copy-start.26 = (f32[768,64]{0,1:T(8,128)}, f32[768,64]{0,1:T(8,128)S(1)}, u32[]{:S(2)}) copy-start(f32[768,64]{0,1:T(8,128)S(1)} %get-tuple-element.113) | copy-start | bytes 589828
  102.3 20.9 %copy-start.9 = (bf16[768,16,64]{0,2,1:T(8,128)(2,1)}, bf16[768,16,64]{0,2,1:T(8,128)(2,1)S(1)}, u32[]{:S(2)}) copy-start(bf16[768,16,64]{0,2,1:T(8,128)(2,1)S(1)} %get-tuple-element.111) | copy-start | bytes 4718596
  103.1 4.0 collective-permute-start
  105.3 4.6 collective-permute-start.1
  117.1 6.1 copy-start.20
  117.1 9.1 copy-start.28
  117.1 12.1 %copy-start.30 = (bf16[384,1024]{0,1:T(8,128)(2,1)}, bf16[384,1024]{0,1:T(8,128)(2,1)S(1)}, u32[]{:S(2)}) copy-start(bf16[384,1024]{0,1:T(8,128)(2,1)S(1)} %get-tuple-element.95) | copy-start | bytes 2359300
  118.5 7.7 copy-start.1
  118.5 7.7 copy-start.37
  120.2 6.1 copy-start.39
  121.5 7.8 copy-start
  124.5 7.7 copy-start.2
  361.4 4.8 copy-start.49
  361.4 4.8 copy-start.50
  361.4 4.8 copy-start.51
  370.0 287.6 %reduce-scatter.11.cloned.1.call-start = ((), (), s32[]{:S(2)}) async-start(), calls=%async_computation.11 | async-start | bytes 11354112 | tf_op jit(solution)/shard_map/reduce_scatter | solution.py:273
  381.5 437.2 %reduce-scatter.5.cloned.1.call-start = ((), (), s32[]{:S(2)}) async-start(), calls=%async_computation.8 | async-start | bytes 12976128 | tf_op jit(solution)/shard_map/reduce_scatter | solution.py:267
  394.0 5.8 slice-start.4
  394.0 5.8 slice-start.5
  407.7 5.6 slice-start.2
  407.8 5.6 slice-start.3
  434.6 9.2 copy-start.21
  438.9 7.0 copy-start.19
  439.1 18.7 %collective-permute-start.3 = (bf16[64,2048]{0,1:T(8,128)(2,1)}, bf16[64,2048]{0,1:T(8,128)(2,1)}, u32[]{:S(2)}, u32[]{:S(2)}) collective-permute-start(bf16[64,2048]{0,1:T(8,128)(2,1)} %slice.393), channel_id=1, source_target_pairs={{1,0},{2,1},{3,2},{4,3},{5,4},{6,5},{7,6},{8,7},{9,8},{10,9},{11,1... | collective-permute-start | bytes 786440 | tf_op jit(solution)/shard_map/ppermute | solution.py:36
  440.5 9.7 collective-permute-start.2
  473.5 4.2 slice-start.6
  479.9 5.7 copy-start.6
  479.9 5.7 copy-start.42
  479.9 5.7 copy-start.45
  479.9 5.7 copy-start.47
  498.1 553.2 %reduce-scatter.9.cloned.1.call-start = ((), (), s32[]{:S(2)}) async-start(), calls=%async_computation.10 | async-start | bytes 22167552 | tf_op jit(solution)/shard_map/reduce_scatter | solution.py:269
  516.0 10.2 copy-start.7
  516.0 10.2 copy-start.34
  516.0 10.2 copy-start.35
  516.1 10.2 copy-start.36
  526.3 10.8 %copy-start.48 = (f32[1024]{0:T(1024)S(1)}, f32[1024]{0:T(1024)}, u32[]{:S(2)}) copy-start(f32[1024]{0:T(1024)} %get-tuple-element.68) | copy-start | bytes 12292
  526.3 65.2 %copy-start.8 = (bf16[768,1024]{1,0:T(8,128)(2,1)S(1)}, bf16[768,1024]{1,0:T(8,128)(2,1)}, u32[]{:S(2)}) copy-start(bf16[768,1024]{1,0:T(8,128)(2,1)} %param.20) | copy-start | bytes 4718596
  (24 other events, 57.9 us)
Sparse Core Ops, SparseCore 0:
  10.9 72.1 all-gather.4
  85.9 57.0 all-gather.6
  145.9 86.6 all-gather.8
  235.4 64.5 all-gather.10
  370.1 139.8 reduce-scatter.6
  516.5 141.0 reduce-scatter.10
  664.2 154.4 reduce-scatter.4
  821.6 229.5 reduce-scatter.8
where the time goes:
time: 1070 us; the launch traced here: 1060 us
  waiting for transfers between devices  625 us (58%)
  matrix products  191 us (18%)
  blocking collectives  95.4 us (9%)
  other arithmetic  76.4 us (7%)
  local copies, waits for them, and re-layouts  46 us (4%)
  between operations  15.4 us (1%)
    reduce_scatter x1, waiting for transfers between devices, local(): lax.psum_scatter(in_grad, 'dev', scatter_dimension=0, tiled=True)  233 us
    reduce_scatter x1, waiting for transfers between devices, local(): lax.psum_scatter(qkv_grad, 'dev', scatter_dimension=0, tiled=True)  161 us
    unnamed x2, blocking collectives  95.4 us
    all_gather x1, waiting for transfers between devices, local(): lax.all_gather(w_in, 'dev', axis=0, tiled=True)  84.6 us
    reduce_scatter x1, waiting for transfers between devices, local(): lax.psum_scatter(down_grad, 'dev', scatter_dimension=1, tiled=True)  61.6 us
    dot_general x4, matrix products, contract_cols(): lax.dot_general(first_mat, second_mat, (((1,), (1,)), ((), ())), preferre...  61.5 us
    all_gather x1, waiting for transfers between devices, local(): full_down = lax.all_gather(w_down, 'dev', axis=1, tiled=True)  51.5 us
    dot_general x4, matrix products, contract_rows(): lax.dot_general(first_mat, second_mat, (((0,), (0,)), ((), ())), preferre...  45.5 us
  transfers between devices with their start and end apart: 12, of which 8 were waited for; matrix products, arithmetic and copies ran while one was open for 23% of the time, Pallas kernels for 0%

commit v1 on v0

--- a/solution.py
+++ b/solution.py
@@ -34,6 +34,101 @@
     count = lax.axis_size(axis)
     leading, last = (max(0, -steps), min(count, count - steps))
     return lax.ppermute(value, axis, [(source, source + steps) for source in range(leading, last)])
+
+
+def swapped(value, count, mask):
+    return lax.ppermute(value, "dev", [(i, i ^ mask) for i in range(count)])
+
+
+def column_halves(width):
+    middle = max(128, (width // 256) * 128)
+    return ((0, middle, (2, 4)), (middle, width, (4, 2)))
+
+
+def place_bits(dev_index):
+    return {1: dev_index % 2, 2: (dev_index // 2) % 2, 4: (dev_index // 4) % 2}
+
+
+def far_groups(count):
+    return [list(range(first, count, 8)) for first in range(8)]
+
+
+def gather_rows(shard):
+    count = lax.axis_size("dev")
+    dev_index = lax.axis_index("dev")
+    bits = place_bits(dev_index)
+    far = count // 8
+    mine_far = dev_index // 8
+    rows, width = shard.shape
+    full = jnp.zeros((far, 2, 2, 2, rows, width), shard.dtype)
+    for first, last, order in column_halves(width):
+        part = shard[:, first:last]
+        if far <= 4:
+            held = jnp.zeros((far, rows, last - first), shard.dtype)
+            held = lax.dynamic_update_slice(held, part[None], (mine_far, 0, 0))
+            for step in range(1, far):
+                moved = swapped(part, count, 8 * step)
+                held = lax.dynamic_update_slice(held, moved[None], (mine_far ^ step, 0, 0))
+        else:
+            held = lax.all_gather(part, "dev", axis=0, axis_index_groups=far_groups(count))
+        pieces = [(0, held)]
+        for mask in order + (1,):
+            pieces = pieces + [(seen | mask, swapped(piece, count, mask)) for seen, piece in pieces]
+        for seen, piece in pieces:
+            spot = {bit: bits[bit] ^ (1 if seen & bit else 0) for bit in (1, 2, 4)}
+            full = lax.dynamic_update_slice(
+                full, piece[:, None, None, None], (0, spot[4], spot[2], spot[1], 0, first)
+            )
+    return full.reshape(count * rows, width)
+
+
+def scatter_start(grad):
+    count = lax.axis_size("dev")
+    mine = place_bits(lax.axis_index("dev"))[1]
+    rows = grad.shape[0] // count
+    split = grad.astype(jnp.bfloat16).reshape(count // 2, 2, rows, grad.shape[1])
+    given = lax.dynamic_slice_in_dim(split, 1 - mine, 1, axis=1)
+    taken = swapped(given, count, 1)
+    kept = lax.dynamic_slice_in_dim(split, mine, 1, axis=1)
+    return (kept.astype(jnp.float32) + taken.astype(jnp.float32)).astype(jnp.bfloat16)
+
+
+def scatter_rest(half):
+    count = lax.axis_size("dev")
+    dev_index = lax.axis_index("dev")
+    bits = place_bits(dev_index)
+    far = count // 8
+    mine_far = dev_index // 8
+    rows, width = half.shape[2:]
+    whole = half.reshape(far, 2, 2, rows, width)
+    outs = []
+    for first, last, order in column_halves(width):
+        part = whole[..., first:last]
+        for mask in order[::-1]:
+            axis = 1 if mask == 4 or part.ndim == 4 else 2
+            given = lax.dynamic_index_in_dim(part, 1 - bits[mask], axis, keepdims=False)
+            kept = lax.dynamic_index_in_dim(part, bits[mask], axis, keepdims=False)
+            taken = swapped(given, count, mask)
+            part = (kept.astype(jnp.float32) + taken.astype(jnp.float32)).astype(jnp.bfloat16)
+        if far <= 4:
+            total = lax.dynamic_index_in_dim(part, mine_far, 0, keepdims=False).astype(jnp.float32)
+            for step in range(1, far):
+                given = lax.dynamic_index_in_dim(part, mine_far ^ step, 0, keepdims=False)
+                total = total + swapped(given, count, 8 * step).astype(jnp.float32)
+        else:
+            total = lax.psum_scatter(
+                part.reshape(far * rows, last - first),
+                "dev",
+                scatter_dimension=0,
+                tiled=True,
+                axis_index_groups=far_groups(count),
+            ).astype(jnp.float32)
+        outs.append(total)
+    return jnp.concatenate(outs, axis=1)
+
+
+def with_column(matrix, vector):
+    return jnp.concatenate([matrix, jnp.pad(vector[:, None], ((0, 0), (0, 127)))], axis=1)
 
 
 def layer_norm(values):
@@ -117,15 +212,15 @@
     )
     offsets = jnp.arange(query_block)[:, None] - jnp.arange(window_rows)[None, :] + HALF
     nearby = jnp.abs(offsets) <= HALF
-    gathered = (
-        lax.all_gather(w_qkv, "dev", axis=0, tiled=True),
-        lax.all_gather(w_out, "dev", axis=0, tiled=True),
-        lax.all_gather(w_in, "dev", axis=0, tiled=True),
-        lax.all_gather(gain_attn, "dev", axis=0, tiled=True),
-        lax.all_gather(gain_mlp, "dev", axis=0, tiled=True),
-    )
-    full_down = lax.all_gather(w_down, "dev", axis=1, tiled=True)
-    full_qkv, full_out, full_in, full_gain_attn, full_gain_mlp = gathered
+    gains = jnp.pad(jnp.stack([gain_attn, gain_mlp], axis=1), ((0, 0), (0, 126)))
+    qkv_and_gains = gather_rows(jnp.concatenate([w_qkv, gains], axis=1))
+    full_qkv = qkv_and_gains[:, : 3 * model_width]
+    full_gain_attn = qkv_and_gains[:, 3 * model_width]
+    full_gain_mlp = qkv_and_gains[:, 3 * model_width + 1]
+    out_and_in = gather_rows(jnp.concatenate([w_out, w_in], axis=1))
+    full_out = out_and_in[:, :model_width]
+    full_in = out_and_in[:, model_width:]
+    down_rows = gather_rows(w_down.T)
     inputs = tokens.astype(jnp.float32)
     normed_attn, inv_attn = layer_norm(inputs)
     h_attn = (normed_attn * full_gain_attn.astype(jnp.float32)).astype(jnp.bfloat16)
@@ -183,26 +278,28 @@
     up_part = gate_up[:, hidden_units:]
     activated = geglu(gate_part, up_part).astype(jnp.bfloat16)
     layer_out = (
-        residual + jnp.dot(activated, full_down, preferred_element_type=jnp.float32)
+        residual + contract_cols(activated, down_rows)
     ).astype(jnp.bfloat16)
-    full_qkv, full_out, full_in, full_gain_attn, full_gain_mlp = (
-        lax.all_gather(w_qkv, "dev", axis=0, tiled=True),
-        lax.all_gather(w_out, "dev", axis=0, tiled=True),
-        lax.all_gather(w_in, "dev", axis=0, tiled=True),
-        lax.all_gather(gain_attn, "dev", axis=0, tiled=True),
-        lax.all_gather(gain_mlp, "dev", axis=0, tiled=True),
-    )
-    full_down = lax.all_gather(w_down, "dev", axis=1, tiled=True)
-    d_activated = contract_cols(cotangent, full_down)
+    down_half = scatter_start(contract_rows(cotangent, activated))
+    d_activated = jnp.dot(cotangent, down_rows, preferred_element_type=jnp.float32)
     _, geglu_back = jax.vjp(geglu, gate_part, up_part)
     d_gate, d_up = geglu_back(d_activated)
     d_gate_up = jnp.concatenate([d_gate, d_up], axis=1).astype(jnp.bfloat16)
+    d_gate_up, down_half = lax.optimization_barrier((d_gate_up, down_half))
+    down_part = scatter_rest(down_half).T
+    in_grad = contract_rows(h_mlp, d_gate_up)
     d_h_mlp = contract_cols(d_gate_up, full_in)
     mlp_gain_grad = jnp.sum(d_h_mlp * normed_mlp, axis=0)
+    in_half = scatter_start(with_column(in_grad, mlp_gain_grad))
     d_residual = cotangent.astype(jnp.float32) + norm_back(
         d_h_mlp * full_gain_mlp.astype(jnp.float32), normed_mlp, inv_mlp
     )
     d_branch = d_residual.astype(jnp.bfloat16)
+    out_half = scatter_start(contract_rows(mixed, d_branch))
+    d_branch, in_half, out_half = lax.optimization_barrier((d_branch, in_half, out_half))
+    in_sums = scatter_rest(in_half)
+    in_part, mlp_gain_part = in_sums[:, : 2 * hidden_units], in_sums[:, 2 * hidden_units]
+    out_part = scatter_rest(out_half)
     d_mixed = contract_cols(d_branch, full_out).astype(jnp.bfloat16)
     d_query_list = []
     d_window = jnp.zeros((tok_rows + 2 * HALF, 2 * model_width), jnp.float32)
@@ -259,18 +356,9 @@
     tokens_grad = (
         d_residual + norm_back(d_h_attn * full_gain_attn.astype(jnp.float32), normed_attn, inv_attn)
     ).astype(jnp.bfloat16)
-    down_grad = contract_rows(activated, cotangent)
-    in_grad = contract_rows(h_mlp, d_gate_up)
-    out_grad = contract_rows(mixed, d_branch)
     qkv_grad = contract_rows(h_attn, d_projected)
-    qkv_part, out_part, in_part, attn_gain_part, mlp_gain_part = (
-        lax.psum_scatter(qkv_grad, "dev", scatter_dimension=0, tiled=True),
-        lax.psum_scatter(out_grad, "dev", scatter_dimension=0, tiled=True),
-        lax.psum_scatter(in_grad, "dev", scatter_dimension=0, tiled=True),
-        lax.psum_scatter(attn_gain_grad, "dev", scatter_dimension=0, tiled=True),
-        lax.psum_scatter(mlp_gain_grad, "dev", scatter_dimension=0, tiled=True),
-    )
-    down_part = lax.psum_scatter(down_grad, "dev", scatter_dimension=1, tiled=True)
+    qkv_sums = scatter_rest(scatter_start(with_column(qkv_grad, attn_gain_grad)))
+    qkv_part, attn_gain_part = qkv_sums[:, : 3 * model_width], qkv_sums[:, 3 * model_width]
     return (
         layer_out,
         tokens_grad,

time: 1070 us -> 793 us (0.74)
  waiting for transfers between devices: 625 us -> 254 us
  starting transfers between devices: 8.68 us -> 121 us
  blocking collectives: 95.4 us -> 0 us
  local copies, waits for them, and re-layouts: 46 us -> 131 us
  other arithmetic: 76.4 us -> 100 us
  matrix products: 191 us -> 173 us
  between operations: 15.4 us -> 3 us
    reduce_scatter x4 -> x0, waiting for transfers between devices: 455 us -> none  [the longest x1 233 us: local(): lax.psum_scatter(in_grad, 'dev', scatter_dimension=0, tiled=True)]
    ppermute x0 -> x104, waiting for transfers between devices: none -> 254 us  [swapped(): return lax.ppermute(value, 'dev', [(i, i ^ mask) for i in range(count)])]
    all_gather x4 -> x0, waiting for transfers between devices: 165 us -> none  [the longest x1 84.6 us: local(): lax.all_gather(w_in, 'dev', axis=0, tiled=True)]
    ppermute x0 -> x104, starting transfers between devices: none -> 113 us  [swapped(): return lax.ppermute(value, 'dev', [(i, i ^ mask) for i in range(count)])]
    unnamed x2 -> x0, blocking collectives: 95.4 us -> none
    dynamic_update_slice x0 -> x70, local copies, waits for them, and re-layouts: none -> 42.6 us  [the longest x48 37.5 us: gather_rows(): lax.dynamic_update_slice(full, piece[:, None, None, None], (0, spot[4], s...]
    convert_element_type x1 -> x21, other arithmetic: 0.01 us -> 24.6 us  [the longest x4 11.2 us: scatter_start(): (kept.astype(jnp.float32) + taken.astype(jnp.float32)).astype(jnp.bfloat16)]
    dot_general x4, matrix products: 61.5 us -> 40.4 us  [contract_cols(): lax.dot_general(first_mat, second_mat, (((1,), (1,)), ((), ())), preferre...]
  transfers between devices with their start and end apart: 12 -> 108, of which waited for: 8 -> 50; matrix products, arithmetic and copies ran while one was open for 23% -> 27% of each run, Pallas kernels for 0% -> 0%
where the time goes in v1:
time: 793 us; the launch traced here: 783 us
  waiting for transfers between devices  254 us (32%)
  matrix products  173 us (22%)
  local copies, waits for them, and re-layouts  131 us (17%)
  starting transfers between devices  121 us (15%)
  other arithmetic  100 us (13%)
    ppermute x104, waiting for transfers between devices, swapped(): return lax.ppermute(value, 'dev', [(i, i ^ mask) for i in range(count)])  254 us
    ppermute x104, starting transfers between devices, swapped(): return lax.ppermute(value, 'dev', [(i, i ^ mask) for i in range(count)])  113 us
    dot_general x4, matrix products, contract_cols(): lax.dot_general(first_mat, second_mat, (((1,), (1,)), ((), ())), preferre...  40.4 us
    dynamic_update_slice x48, local copies, waits for them, and re-layouts, gather_rows(): lax.dynamic_update_slice(full, piece[:, None, None, None], (0, spot[4], s...  37.5 us
    dot_general x4, matrix products, contract_rows(): lax.dot_general(first_mat, second_mat, (((0,), (0,)), ((), ())), preferre...  31.6 us
    dot_general x1, matrix products, local(): jnp.dot(cotangent, down_rows, preferred_element_type=jnp.float32)  26.8 us
    another operation x3, other arithmetic  20.6 us
    dot_general x1, matrix products, local(): gate_up = jnp.dot(h_mlp, full_in, preferred_element_type=jnp.float32)  16.4 us
  transfers between devices with their start and end apart: 108, of which 50 were waited for; matrix products, arithmetic and copies ran while one was open for 27% of the time, Pallas kernels for 0%

profile of v1, /device:TPU:0, one launch (start us, length us, event | category | flops | bytes accessed | tf_op | source)
XLA Modules:
  0.0 783.1 jit_solution(9778034214665870830)
XLA Ops:
  58.2 9.1 %collective-permute-done.11 = bf16[32,1664]{1,0:T(8,128)(2,1)S(1)} collective-permute-done((bf16[32,1664]{1,0:T(8,128)(2,1)S(1)}, bf16[32,1664]{1,0:T(8,128)(2,1)S(1)}, u32[]{:S(2)}, u32[]{:S(2)}) %collective-permute-start.11) | collective-permute-done | bytes 106528 | tf_op jit(solution)/shard_map/ppermute | solution.py:40
  69.0 5.3 collective-permute-done.22
  78.3 4.9 collective-permute-done.23
  85.8 5.9 broadcast_in_dim.379
  98.1 6.4 collective-permute-done.45
  108.2 11.7 %collective-permute-done.3 = bf16[4,32,1536]{2,1,0:T(8,128)(2,1)S(1)} collective-permute-done((bf16[4,32,1536]{2,1,0:T(8,128)(2,1)S(1)}, bf16[4,32,1536]{2,1,0:T(8,128)(2,1)S(1)}, u32[]{:S(2)}, u32[]{:S(2)}) %collective-permute-start.3) | collective-permute-done | bytes 393248 | tf_op jit(solution)/shard_map/ppermute | solution.py:40
  121.4 8.9 %collective-permute-done.4 = bf16[4,32,1536]{2,1,0:T(8,128)(2,1)S(1)} collective-permute-done((bf16[4,32,1536]{2,1,0:T(8,128)(2,1)S(1)}, bf16[4,32,1536]{2,1,0:T(8,128)(2,1)S(1)}, u32[]{:S(2)}, u32[]{:S(2)}) %collective-permute-start.4) | collective-permute-done | bytes 393248 | tf_op jit(solution)/shard_map/ppermute | solution.py:40
  131.7 6.6 collective-permute-done.47
  143.9 10.0 %collective-permute-done.5 = bf16[4,32,1536]{2,1,0:T(8,128)(2,1)S(1)} collective-permute-done((bf16[4,32,1536]{2,1,0:T(8,128)(2,1)S(1)}, bf16[4,32,1536]{2,1,0:T(8,128)(2,1)S(1)}, u32[]{:S(2)}, u32[]{:S(2)}) %collective-permute-start.5) | collective-permute-done | bytes 393248 | tf_op jit(solution)/shard_map/ppermute | solution.py:40
  161.2 12.0 %collective-permute-done.25 = bf16[4,32,3072]{2,1,0:T(8,128)(2,1)S(1)} collective-permute-done((bf16[4,32,3072]{2,1,0:T(8,128)(2,1)}, bf16[4,32,3072]{2,1,0:T(8,128)(2,1)S(1)}, u32[]{:S(2)}, u32[]{:S(2)}) %collective-permute-start.25) | collective-permute-done | bytes 786464 | tf_op jit(solution)/shard_map/ppermute | solution.py:40
  174.2 5.5 collective-permute-done.26
  187.1 14.0 %collective-permute-done.57 = bf16[4,32,1344]{2,1,0:T(8,128)(2,1)} collective-permute-done((bf16[4,32,1344]{2,1,0:T(8,128)(2,1)S(1)}, bf16[4,32,1344]{2,1,0:T(8,128)(2,1)}, u32[]{:S(2)}, u32[]{:S(2)}) %collective-permute-start.57) | collective-permute-done | bytes 344096 | tf_op jit(solution)/shard_map/ppermute | solution.py:40
  213.7 26.0 %collective-permute-done.15 = bf16[4,32,1664]{2,1,0:T(8,128)(2,1)S(1)} collective-permute-done((bf16[4,32,1664]{2,1,0:T(8,128)(2,1)S(1)}, bf16[4,32,1664]{2,1,0:T(8,128)(2,1)S(1)}, u32[]{:S(2)}, u32[]{:S(2)}) %collective-permute-start.15) | collective-permute-done | bytes 426016 | tf_op jit(solution)/shard_map/ppermute | solution.py:40
  247.6 8.5 %fusion.17 = f32[768,3072]{0,1:T(8,128)S(1)} fusion(bf16[1024,3200]{1,0:T(8,128)(2,1)} %bitcast.40, bf16[768,1024]{1,0:T(8,128)(2,1)S(1)} %copy-done.3, f32[1024]{0:T(1024)S(1)} %get-tuple-element.79, f32[768]{0:T(1024)S(1)} %add_rsqrt_fusion.1, f32[768]{0:T(1024)S(1)} %broadcast_multiply_fusion.7), kind=kOutput, calls=%fused_computation.68 | convolution fusion | flops 4835770368 | bytes 17311744 | tf_op jit(solution)/shard_map/dot_general | solution.py:227
  273.3 9.3 %collective-permute-start.35 = (bf16[4,32,3200]{2,1,0:T(8,128)(2,1)}, bf16[4,32,3200]{2,1,0:T(8,128)(2,1)S(1)}, u32[]{:S(2)}, u32[]{:S(2)}) collective-permute-start(bf16[4,32,3200]{2,1,0:T(8,128)(2,1)} %bitcast_dynamic-update-slice_fusion.48), channel_id=1, source_target_pairs={{0,4},{1,5},{2,6},{3,7},{4,0},{5,1},{6,2},{7,3},{8,12},{9,13},{10,... | collective-permute-start | bytes 2457608 | tf_op jit(solution)/shard_map/ppermute | solution.py:40
  282.8 7.6 pad_maximum_fusion.10
  308.8 9.8 %collective-permute-done.27 = bf16[4,32,3072]{2,1,0:T(8,128)(2,1)S(1)} collective-permute-done((bf16[4,32,3072]{2,1,0:T(8,128)(2,1)S(1)}, bf16[4,32,3072]{2,1,0:T(8,128)(2,1)S(1)}, u32[]{:S(2)}, u32[]{:S(2)}) %collective-permute-start.27) | collective-permute-done | bytes 786464 | tf_op jit(solution)/shard_map/ppermute | solution.py:40
  322.1 17.4 %collective-permute-done.37 = bf16[4,32,3200]{2,1,0:T(8,128)(2,1)S(1)} collective-permute-done((bf16[4,32,3200]{2,1,0:T(8,128)(2,1)S(1)}, bf16[4,32,3200]{2,1,0:T(8,128)(2,1)S(1)}, u32[]{:S(2)}, u32[]{:S(2)}) %collective-permute-start.37) | collective-permute-done | bytes 819232 | tf_op jit(solution)/shard_map/ppermute | solution.py:40
  349.1 16.4 %fusion.2 = f32[768,5248]{1,0:T(8,128)} fusion(bf16[1024,6272]{1,0:T(8,128)(2,1)} %bitcast.585, f32[768,1024]{1,0:T(8,128)S(1)} %get-tuple-element.180, f32[1024]{0:T(1024)S(1)} %get-tuple-element.78, f32[768]{0:T(1024)S(1)} %add_rsqrt_fusion, f32[768]{0:T(1024)S(1)} %broadcast_multiply_fusion.6), kind=kOutput, calls=%fused_computation.9 | convolution fusion | flops 8257536000 | bytes 30025728 | tf_op jit(solution)/shard_map/dot_general | solution.py:276
  365.6 26.8 %add_convert_fusion.1 = (bf16[768,2624]{1,0:T(8,128)(2,1)}, f32[768,2624]{1,0:T(8,128)S(1)}, f32[2624,768]{0,1:T(8,128)}) fusion(f32[768,5248]{1,0:T(8,128)} %fusion.2, bf16[768,1024]{1,0:T(8,128)(2,1)S(1)} %copy-done.42, bf16[1024,2624]{1,0:T(8,128)(2,1)} %bitcast.140), kind=kOutput, calls=%fused_computation.17 | convolution fusion | flops 4274307072 | bytes 43220992 | tf_op jit(solution)/shard_map/dot_general | solution.py:284
  392.4 13.1 %fusion.5 = (bf16[768,2624]{1,0:T(8,128)(2,1)}, bf16[768,2624]{1,0:T(8,128)(2,1)}) fusion(f32[2624,768]{0,1:T(8,128)} %get-tuple-element.181, f32[768,2624]{1,0:T(8,128)S(1)} %get-tuple-element.91, f32[768,5248]{1,0:T(8,128)} %fusion.2), kind=kLoop, calls=%fused_computation.16 | loop fusion | flops 12091392 | bytes 40304640 | tf_op jit(solution)/shard_map/convert.47
  405.5 8.8 %fusion.23 = bf16[1024,2624]{0,1:T(8,128)(2,1)} fusion(bf16[768,2624]{1,0:T(8,128)(2,1)} %get-tuple-element.97, bf16[768,1024]{1,0:T(8,128)(2,1)S(1)} %copy-done.42), kind=kOutput, calls=%fused_computation.75 | convolution fusion | flops 4129882112 | bytes 10977280 | tf_op jit(solution)/shard_map/dot_general | solution.py:173
  414.3 8.0 %copy.133 = bf16[1024,2624]{1,0:T(8,128)(2,1)} copy(bf16[1024,2624]{0,1:T(8,128)(2,1)} %fusion.23) | data formatting | bytes 10747904 | tf_op jit(solution)/shard_map/convert_element_type | solution.py:89
  426.4 9.0 %pad_maximum_fusion = bf16[768,5248]{1,0:T(8,128)(2,1)} fusion(bf16[768,2624]{1,0:T(8,128)(2,1)} %get-tuple-element.96, bf16[768,2624]{1,0:T(8,128)(2,1)} %get-tuple-element.90), kind=kLoop, calls=%fused_computation.32 | loop fusion | flops 16121856 | bytes 16121856 | tf_op jit(solution)/shard_map/concatenate | solution.py:287
  435.4 10.6 %add_convert_fusion.4 = bf16[768,1024]{1,0:T(8,128)(2,1)} fusion(f32[768,1024]{1,0:T(8,128)} %copy-done.7, bf16[768,2624]{1,0:T(8,128)(2,1)} %get-tuple-element.97, bf16[1024,2624]{1,0:T(8,128)(2,1)} %bitcast.140), kind=kOutput, calls=%fused_computation.128 | convolution fusion | flops 4128768000 | bytes 14123008 | tf_op jit(solution)/shard_map/dot_general | solution.py:179
  450.8 15.6 %multiply_reduce_fusion.3 = (bf16[1024]{0:T(1024)(128)(2,1)S(1)}, f32[768]{0:T(1024)S(1)}, f32[768]{0:T(1024)S(1)}, f32[768,1024]{1,0:T(8,128)}) fusion(f32[768,1024]{1,0:T(8,128)S(1)} %copy-done.8, f32[768]{0:T(1024)S(1)} %add_rsqrt_fusion, f32[768]{0:T(1024)S(1)} %broadcast_multiply_fusion.6, f32[1024]{0:T(1024)S(1)} %get-tuple-element.78, ...), kind=kOutput, calls=%fused_computation.124 | convolution fusion | flops 8260678656 | bytes 25118720 | tf_op jit(solution)/shard_map/dot_general | solution.py:179
  466.5 13.4 %convolution_convert_fusion = bf16[1024,5248]{1,0:T(8,128)(2,1)S(1)} fusion(bf16[768,5248]{1,0:T(8,128)(2,1)} %pad_maximum_fusion, f32[768,1024]{1,0:T(8,128)S(1)} %copy-done.8, f32[1024]{0:T(1024)S(1)} %get-tuple-element.78, f32[768]{0:T(1024)S(1)} %add_rsqrt_fusion, f32[768]{0:T(1024)S(1)} %broadcast_multiply_fusion.6), kind=kOutput, calls=%fused_computation.3 | convolution fusion | flops 8262909952 | bytes 21964800 | tf_op jit(solution)/shard_map/dot_general | solution.py:173
  490.9 6.9 collective-permute-done.98
  503.3 4.7 collective-permute-done.99
  526.3 6.4 add_convert_fusion
  537.9 5.2 fusion.47
  554.7 5.4 fusion.45
  571.5 4.3 fusion.49
  587.5 4.4 slice.429
  607.0 9.0 %collective-permute-start.88 = (bf16[4,2,32,2688]{3,2,0,1:T(8,128)(2,1)}, bf16[4,2,32,2688]{3,2,0,1:T(8,128)(2,1)}, u32[]{:S(2)}, u32[]{:S(2)}) collective-permute-start(bf16[4,2,32,2688]{3,2,0,1:T(8,128)(2,1)} %bitcast.552), channel_id=1, source_target_pairs={{0,4},{1,5},{2,6},{3,7},{4,0},{5,1},{6,2},{7,3},{8,12},{9,13},{10,... | collective-permute-start | bytes 4128776 | tf_op jit(solution)/shard_map/ppermute | solution.py:40
  616.3 5.9 scatter-add.21
  623.9 6.4 scatter-add.24
  639.7 4.7 fusion.54
  644.3 10.2 %fusion.43 = (bf16[1024]{0:T(1024)(128)(2,1)S(1)}, f32[768]{0:T(1024)S(1)}, f32[768]{0:T(1024)S(1)}, f32[768,1024]{1,0:T(8,128)S(1)}) fusion(bf16[768,1024]{1,0:T(8,128)(2,1)S(1)} %copy-done.4, f32[768]{0:T(1024)S(1)} %copy-done.60, f32[768]{0:T(1024)S(1)} %copy-done.55, f32[1024]{0:T(1024)S(1)} %copy-done.58, bf16[1024,3200]{1,0:T(8,128)(2,1)} %bitcast.40, ...), kind=kOutput, calls=%fused_computation.99 | convolution fusion | flops 4853068800 | bytes 15747072 | tf_op jit(solution)/shard_map/dot_general | solution.py:179
  654.6 7.6 convolution_convert_fusion.1
  689.6 11.8 %collective-permute-done.94 = bf16[4,32,2688]{2,1,0:T(8,128)(2,1)S(1)} collective-permute-done((bf16[4,32,2688]{2,1,0:T(8,128)(2,1)S(1)}, bf16[4,32,2688]{2,1,0:T(8,128)(2,1)S(1)}, u32[]{:S(2)}, u32[]{:S(2)}) %collective-permute-start.94) | collective-permute-done | bytes 688160 | tf_op jit(solution)/shard_map/ppermute | solution.py:40
  708.4 5.9 collective-permute-done.95
  714.2 5.1 collective-permute-start.91
  719.3 8.2 %collective-permute-done.96 = bf16[32,2688]{1,0:T(8,128)(2,1)S(1)} collective-permute-done((bf16[32,2688]{1,0:T(8,128)(2,1)S(1)}, bf16[32,2688]{1,0:T(8,128)(2,1)S(1)}, u32[]{:S(2)}, u32[]{:S(2)}) %collective-permute-start.96) | collective-permute-done | bytes 172064 | tf_op jit(solution)/shard_map/ppermute | solution.py:40
  727.7 5.1 collective-permute-done.91
  736.6 14.7 %collective-permute-done.68 = bf16[4,2,32,1536]{3,2,0,1:T(8,128)(2,1)S(1)} collective-permute-done((bf16[4,2,32,1536]{3,2,0,1:T(8,128)(2,1)S(1)}, bf16[4,2,32,1536]{3,2,0,1:T(8,128)(2,1)S(1)}, u32[]{:S(2)}, u32[]{:S(2)}) %collective-permute-start.68) | collective-permute-done | bytes 786464 | tf_op jit(solution)/shard_map/ppermute | solution.py:40
  751.7 5.7 collective-permute-done.73
  771.3 7.5 collective-permute-done.71
  (603 shorter events, 334.6 us)
Async XLA Ops:
  1.7 26.7 %collective-permute-start.43 = (bf16[32,1280]{1,0:T(8,128)(2,1)S(1)}, bf16[32,1280]{1,0:T(8,128)(2,1)S(1)}, u32[]{:S(2)}, u32[]{:S(2)}) collective-permute-start(bf16[32,1280]{1,0:T(8,128)(2,1)S(1)} %slice.420), channel_id=1, source_target_pairs={{0,16},{1,17},{2,18},{3,19},{4,20},{5,21},{6,22},{7,23},{8,24},{9,... | collective-permute-start | bytes 245768 | tf_op jit(solution)/shard_map/ppermute | solution.py:40
  5.7 22.6 %collective-permute-start.42 = (bf16[32,1280]{1,0:T(8,128)(2,1)S(1)}, bf16[32,1280]{1,0:T(8,128)(2,1)S(1)}, u32[]{:S(2)}, u32[]{:S(2)}) collective-permute-start(bf16[32,1280]{1,0:T(8,128)(2,1)S(1)} %slice.420), channel_id=1, source_target_pairs={{0,8},{1,9},{2,10},{3,11},{4,12},{5,13},{6,14},{7,15},{8,0},{9,1},... | collective-permute-start | bytes 245768 | tf_op jit(solution)/shard_map/ppermute | solution.py:40
  7.3 22.7 %collective-permute-start.44 = (bf16[32,1280]{1,0:T(8,128)(2,1)S(1)}, bf16[32,1280]{1,0:T(8,128)(2,1)S(1)}, u32[]{:S(2)}, u32[]{:S(2)}) collective-permute-start(bf16[32,1280]{1,0:T(8,128)(2,1)S(1)} %slice.420), channel_id=1, source_target_pairs={{0,24},{1,25},{2,26},{3,27},{4,28},{5,29},{6,30},{7,31},{8,16},{9,... | collective-permute-start | bytes 245768 | tf_op jit(solution)/shard_map/ppermute | solution.py:40
  8.2 28.6 %collective-permute-start.53 = (bf16[32,1344]{1,0:T(8,128)(2,1)S(1)}, bf16[32,1344]{1,0:T(8,128)(2,1)S(1)}, u32[]{:S(2)}, u32[]{:S(2)}) collective-permute-start(bf16[32,1344]{1,0:T(8,128)(2,1)S(1)} %slice.421), channel_id=1, source_target_pairs={{0,16},{1,17},{2,18},{3,19},{4,20},{5,21},{6,22},{7,23},{8,24},{9,... | collective-permute-start | bytes 258056 | tf_op jit(solution)/shard_map/ppermute | solution.py:40
  10.1 26.7 %collective-permute-start.52 = (bf16[32,1344]{1,0:T(8,128)(2,1)S(1)}, bf16[32,1344]{1,0:T(8,128)(2,1)S(1)}, u32[]{:S(2)}, u32[]{:S(2)}) collective-permute-start(bf16[32,1344]{1,0:T(8,128)(2,1)S(1)} %slice.421), channel_id=1, source_target_pairs={{0,8},{1,9},{2,10},{3,11},{4,12},{5,13},{6,14},{7,15},{8,0},{9,1},... | collective-permute-start | bytes 258056 | tf_op jit(solution)/shard_map/ppermute | solution.py:40
  36.8 59.5 %collective-permute-start.33 = (bf16[32,3200]{1,0:T(8,128)(2,1)S(1)}, bf16[32,3200]{1,0:T(8,128)(2,1)S(1)}, u32[]{:S(2)}, u32[]{:S(2)}) collective-permute-start(bf16[32,3200]{1,0:T(8,128)(2,1)S(1)} %slice.365), channel_id=1, source_target_pairs={{0,16},{1,17},{2,18},{3,19},{4,20},{5,21},{6,22},{7,23},{8,24},{9,... | collective-permute-start | bytes 614408 | tf_op jit(solution)/shard_map/ppermute | solution.py:40
  38.3 55.6 %collective-permute-start.32 = (bf16[32,3200]{1,0:T(8,128)(2,1)S(1)}, bf16[32,3200]{1,0:T(8,128)(2,1)S(1)}, u32[]{:S(2)}, u32[]{:S(2)}) collective-permute-start(bf16[32,3200]{1,0:T(8,128)(2,1)S(1)} %slice.365), channel_id=1, source_target_pairs={{0,8},{1,9},{2,10},{3,11},{4,12},{5,13},{6,14},{7,15},{8,0},{9,1},... | collective-permute-start | bytes 614408 | tf_op jit(solution)/shard_map/ppermute | solution.py:40
  41.3 55.7 %collective-permute-start.34 = (bf16[32,3200]{1,0:T(8,128)(2,1)S(1)}, bf16[32,3200]{1,0:T(8,128)(2,1)S(1)}, u32[]{:S(2)}, u32[]{:S(2)}) collective-permute-start(bf16[32,3200]{1,0:T(8,128)(2,1)S(1)} %slice.365), channel_id=1, source_target_pairs={{0,24},{1,25},{2,26},{3,27},{4,28},{5,29},{6,30},{7,31},{8,16},{9,... | collective-permute-start | bytes 614408 | tf_op jit(solution)/shard_map/ppermute | solution.py:40
  44.3 23.0 %collective-permute-start.11 = (bf16[32,1664]{1,0:T(8,128)(2,1)S(1)}, bf16[32,1664]{1,0:T(8,128)(2,1)S(1)}, u32[]{:S(2)}, u32[]{:S(2)}) collective-permute-start(bf16[32,1664]{1,0:T(8,128)(2,1)S(1)} %get-tuple-element.93), channel_id=1, source_target_pairs={{0,16},{1,17},{2,18},{3,19},{4,20},{5,21},{6,22},{7,23},{8,24},{9,... | collective-permute-start | bytes 319496 | tf_op jit(solution)/shard_map/ppermute | solution.py:40
  83.2 56.0 %collective-permute-start.48 = (bf16[4,32,1280]{2,1,0:T(8,128)(2,1)S(1)}, bf16[4,32,1280]{2,1,0:T(8,128)(2,1)S(1)}, u32[]{:S(2)}, u32[]{:S(2)}) collective-permute-start(bf16[4,32,1280]{2,1,0:T(8,128)(2,1)S(1)} %bitcast_dynamic-update-slice_fusion.68), channel_id=1, source_target_pairs={{0,1},{1,0},{2,3},{3,2},{4,5},{5,4},{6,7},{7,6},{8,9},{9,8},{10,11... | collective-permute-start | bytes 983048 | tf_op jit(solution)/shard_map/ppermute | solution.py:40
  83.9 22.1 %collective-permute-start.46 = (bf16[4,32,1280]{2,1,0:T(8,128)(2,1)S(1)}, bf16[4,32,1280]{2,1,0:T(8,128)(2,1)S(1)}, u32[]{:S(2)}, u32[]{:S(2)}) collective-permute-start(bf16[4,32,1280]{2,1,0:T(8,128)(2,1)S(1)} %bitcast_dynamic-update-slice_fusion.68), channel_id=1, source_target_pairs={{0,4},{1,5},{2,6},{3,7},{4,0},{5,1},{6,2},{7,3},{8,12},{9,13},{10,... | collective-permute-start | bytes 983048 | tf_op jit(solution)/shard_map/ppermute | solution.py:40
  96.3 106.6 %collective-permute-start.58 = (bf16[4,32,1344]{2,1,0:T(8,128)(2,1)S(1)}, bf16[4,32,1344]{2,1,0:T(8,128)(2,1)S(1)}, u32[]{:S(2)}, u32[]{:S(2)}) collective-permute-start(bf16[4,32,1344]{2,1,0:T(8,128)(2,1)S(1)} %bitcast_dynamic-update-slice_fusion.64), channel_id=1, source_target_pairs={{0,1},{1,0},{2,3},{3,2},{4,5},{5,4},{6,7},{7,6},{8,9},{9,8},{10,11... | collective-permute-start | bytes 1032200 | tf_op jit(solution)/shard_map/ppermute | solution.py:40
  97.0 87.5 %collective-permute-start.56 = (bf16[4,32,1344]{2,1,0:T(8,128)(2,1)S(1)}, bf16[4,32,1344]{2,1,0:T(8,128)(2,1)S(1)}, u32[]{:S(2)}, u32[]{:S(2)}) collective-permute-start(bf16[4,32,1344]{2,1,0:T(8,128)(2,1)S(1)} %bitcast_dynamic-update-slice_fusion.64), channel_id=1, source_target_pairs={{0,2},{1,3},{2,0},{3,1},{4,6},{5,7},{6,4},{7,5},{8,10},{9,11},{10,... | collective-permute-start | bytes 1032200 | tf_op jit(solution)/shard_map/ppermute | solution.py:40
  104.5 78.7 %collective-permute-start.55 = (bf16[4,32,1344]{2,1,0:T(8,128)(2,1)S(1)}, bf16[4,32,1344]{2,1,0:T(8,128)(2,1)S(1)}, u32[]{:S(2)}, u32[]{:S(2)}) collective-permute-start(bf16[4,32,1344]{2,1,0:T(8,128)(2,1)S(1)} %bitcast_dynamic-update-slice_fusion.64), channel_id=1, source_target_pairs={{0,4},{1,5},{2,6},{3,7},{4,0},{5,1},{6,2},{7,3},{8,12},{9,13},{10,... | collective-permute-start | bytes 1032200 | tf_op jit(solution)/shard_map/ppermute | solution.py:40
  138.3 18.2 %collective-permute-start.6 = (bf16[4,32,1536]{2,1,0:T(8,128)(2,1)S(1)}, bf16[4,32,1536]{2,1,0:T(8,128)(2,1)S(1)}, u32[]{:S(2)}, u32[]{:S(2)}) collective-permute-start(bf16[4,32,1536]{2,1,0:T(8,128)(2,1)S(1)} %bitcast_dynamic-update-slice_fusion.60), channel_id=1, source_target_pairs={{0,1},{1,0},{2,3},{3,2},{4,5},{5,4},{6,7},{7,6},{8,9},{9,8},{10,11... | collective-permute-start | bytes 1179656 | tf_op jit(solution)/shard_map/ppermute | solution.py:40
  153.9 19.3 %collective-permute-start.25 = (bf16[4,32,3072]{2,1,0:T(8,128)(2,1)}, bf16[4,32,3072]{2,1,0:T(8,128)(2,1)S(1)}, u32[]{:S(2)}, u32[]{:S(2)}) collective-permute-start(bf16[4,32,3072]{2,1,0:T(8,128)(2,1)} %bitcast_dynamic-update-slice_fusion.52), channel_id=1, source_target_pairs={{0,2},{1,3},{2,0},{3,1},{4,6},{5,7},{6,4},{7,5},{8,10},{9,11},{10,... | collective-permute-start | bytes 2359304 | tf_op jit(solution)/shard_map/ppermute | solution.py:40
  160.0 19.8 %collective-permute-start.26 = (bf16[4,32,3072]{2,1,0:T(8,128)(2,1)}, bf16[4,32,3072]{2,1,0:T(8,128)(2,1)S(1)}, u32[]{:S(2)}, u32[]{:S(2)}) collective-permute-start(bf16[4,32,3072]{2,1,0:T(8,128)(2,1)} %bitcast_dynamic-update-slice_fusion.52), channel_id=1, source_target_pairs={{0,4},{1,5},{2,6},{3,7},{4,0},{5,1},{6,2},{7,3},{8,12},{9,13},{10,... | collective-permute-start | bytes 2359304 | tf_op jit(solution)/shard_map/ppermute | solution.py:40
  173.2 67.3 %collective-permute-start.16 = (bf16[4,32,1664]{2,1,0:T(8,128)(2,1)S(1)}, bf16[4,32,1664]{2,1,0:T(8,128)(2,1)S(1)}, u32[]{:S(2)}, u32[]{:S(2)}) collective-permute-start(bf16[4,32,1664]{2,1,0:T(8,128)(2,1)S(1)} %bitcast_dynamic-update-slice_fusion.56), channel_id=1, source_target_pairs={{0,1},{1,0},{2,3},{3,2},{4,5},{5,4},{6,7},{7,6},{8,9},{9,8},{10,11... | collective-permute-start | bytes 1277960 | tf_op jit(solution)/shard_map/ppermute | solution.py:40
  181.4 29.8 %collective-permute-start.14 = (bf16[4,32,1664]{2,1,0:T(8,128)(2,1)S(1)}, bf16[4,32,1664]{2,1,0:T(8,128)(2,1)S(1)}, u32[]{:S(2)}, u32[]{:S(2)}) collective-permute-start(bf16[4,32,1664]{2,1,0:T(8,128)(2,1)S(1)} %bitcast_dynamic-update-slice_fusion.56), channel_id=1, source_target_pairs={{0,2},{1,3},{2,0},{3,1},{4,6},{5,7},{6,4},{7,5},{8,10},{9,11},{10,... | collective-permute-start | bytes 1277960 | tf_op jit(solution)/shard_map/ppermute | solution.py:40
  183.2 26.9 %collective-permute-start.13 = (bf16[4,32,1664]{2,1,0:T(8,128)(2,1)S(1)}, bf16[4,32,1664]{2,1,0:T(8,128)(2,1)S(1)}, u32[]{:S(2)}, u32[]{:S(2)}) collective-permute-start(bf16[4,32,1664]{2,1,0:T(8,128)(2,1)S(1)} %bitcast_dynamic-update-slice_fusion.56), channel_id=1, source_target_pairs={{0,4},{1,5},{2,6},{3,7},{4,0},{5,1},{6,2},{7,3},{8,12},{9,13},{10,... | collective-permute-start | bytes 1277960 | tf_op jit(solution)/shard_map/ppermute | solution.py:40
  184.5 16.6 %collective-permute-start.57 = (bf16[4,32,1344]{2,1,0:T(8,128)(2,1)S(1)}, bf16[4,32,1344]{2,1,0:T(8,128)(2,1)}, u32[]{:S(2)}, u32[]{:S(2)}) collective-permute-start(bf16[4,32,1344]{2,1,0:T(8,128)(2,1)S(1)} %collective-permute-done.55), channel_id=1, source_target_pairs={{0,2},{1,3},{2,0},{3,1},{4,6},{5,7},{6,4},{7,5},{8,10},{9,11},{10,... | collective-permute-start | bytes 1032200 | tf_op jit(solution)/shard_map/ppermute | solution.py:40
  201.1 117.7 %collective-permute-start.28 = (bf16[4,32,3072]{2,1,0:T(8,128)(2,1)}, bf16[4,32,3072]{2,1,0:T(8,128)(2,1)}, u32[]{:S(2)}, u32[]{:S(2)}) collective-permute-start(bf16[4,32,3072]{2,1,0:T(8,128)(2,1)} %bitcast_dynamic-update-slice_fusion.52), channel_id=1, source_target_pairs={{0,1},{1,0},{2,3},{3,2},{4,5},{5,4},{6,7},{7,6},{8,9},{9,8},{10,11... | collective-permute-start | bytes 2359304 | tf_op jit(solution)/shard_map/ppermute | solution.py:40
  208.1 134.3 %collective-permute-start.38 = (bf16[4,32,3200]{2,1,0:T(8,128)(2,1)}, bf16[4,32,3200]{2,1,0:T(8,128)(2,1)}, u32[]{:S(2)}, u32[]{:S(2)}) collective-permute-start(bf16[4,32,3200]{2,1,0:T(8,128)(2,1)} %bitcast_dynamic-update-slice_fusion.48), channel_id=1, source_target_pairs={{0,1},{1,0},{2,3},{3,2},{4,5},{5,4},{6,7},{7,6},{8,9},{9,8},{10,11... | collective-permute-start | bytes 2457608 | tf_op jit(solution)/shard_map/ppermute | solution.py:40
  210.1 111.0 %collective-permute-start.36 = (bf16[4,32,3200]{2,1,0:T(8,128)(2,1)}, bf16[4,32,3200]{2,1,0:T(8,128)(2,1)}, u32[]{:S(2)}, u32[]{:S(2)}) collective-permute-start(bf16[4,32,3200]{2,1,0:T(8,128)(2,1)} %bitcast_dynamic-update-slice_fusion.48), channel_id=1, source_target_pairs={{0,2},{1,3},{2,0},{3,1},{4,6},{5,7},{6,4},{7,5},{8,10},{9,11},{10,... | collective-permute-start | bytes 2457608 | tf_op jit(solution)/shard_map/ppermute | solution.py:40
  211.2 28.5 %collective-permute-start.15 = (bf16[4,32,1664]{2,1,0:T(8,128)(2,1)S(1)}, bf16[4,32,1664]{2,1,0:T(8,128)(2,1)S(1)}, u32[]{:S(2)}, u32[]{:S(2)}) collective-permute-start(bf16[4,32,1664]{2,1,0:T(8,128)(2,1)S(1)} %collective-permute-done.13), channel_id=1, source_target_pairs={{0,2},{1,3},{2,0},{3,1},{4,6},{5,7},{6,4},{7,5},{8,10},{9,11},{10,... | collective-permute-start | bytes 1277960 | tf_op jit(solution)/shard_map/ppermute | solution.py:40
  242.4 27.7 %collective-permute-start.61 = (bf16[4,32,1344]{2,1,0:T(8,128)(2,1)}, bf16[4,32,1344]{2,1,0:T(8,128)(2,1)}, u32[]{:S(2)}, u32[]{:S(2)}) collective-permute-start(bf16[4,32,1344]{2,1,0:T(8,128)(2,1)} %collective-permute-done.57), channel_id=1, source_target_pairs={{0,1},{1,0},{2,3},{3,2},{4,5},{5,4},{6,7},{7,6},{8,9},{9,8},{10,11... | collective-permute-start | bytes 1032200 | tf_op jit(solution)/shard_map/ppermute | solution.py:40
  273.3 45.9 %collective-permute-start.35 = (bf16[4,32,3200]{2,1,0:T(8,128)(2,1)}, bf16[4,32,3200]{2,1,0:T(8,128)(2,1)S(1)}, u32[]{:S(2)}, u32[]{:S(2)}) collective-permute-start(bf16[4,32,3200]{2,1,0:T(8,128)(2,1)} %bitcast_dynamic-update-slice_fusion.48), channel_id=1, source_target_pairs={{0,4},{1,5},{2,6},{3,7},{4,0},{5,1},{6,2},{7,3},{8,12},{9,13},{10,... | collective-permute-start | bytes 2457608 | tf_op jit(solution)/shard_map/ppermute | solution.py:40
  282.7 35.8 %collective-permute-start.27 = (bf16[4,32,3072]{2,1,0:T(8,128)(2,1)S(1)}, bf16[4,32,3072]{2,1,0:T(8,128)(2,1)S(1)}, u32[]{:S(2)}, u32[]{:S(2)}) collective-permute-start(bf16[4,32,3072]{2,1,0:T(8,128)(2,1)S(1)} %copy-done.46), channel_id=1, source_target_pairs={{0,4},{1,5},{2,6},{3,7},{4,0},{5,1},{6,2},{7,3},{8,12},{9,13},{10,... | collective-permute-start | bytes 2359304 | tf_op jit(solution)/shard_map/ppermute | solution.py:40
  319.2 20.3 %collective-permute-start.37 = (bf16[4,32,3200]{2,1,0:T(8,128)(2,1)S(1)}, bf16[4,32,3200]{2,1,0:T(8,128)(2,1)S(1)}, u32[]{:S(2)}, u32[]{:S(2)}) collective-permute-start(bf16[4,32,3200]{2,1,0:T(8,128)(2,1)S(1)} %collective-permute-done.35), channel_id=1, source_target_pairs={{0,2},{1,3},{2,0},{3,1},{4,6},{5,7},{6,4},{7,5},{8,10},{9,11},{10,... | collective-permute-start | bytes 2457608 | tf_op jit(solution)/shard_map/ppermute | solution.py:40
  320.8 18.7 %collective-permute-start.31 = (bf16[4,32,3072]{2,1,0:T(8,128)(2,1)S(1)}, bf16[4,32,3072]{2,1,0:T(8,128)(2,1)S(1)}, u32[]{:S(2)}, u32[]{:S(2)}) collective-permute-start(bf16[4,32,3072]{2,1,0:T(8,128)(2,1)S(1)} %collective-permute-done.27), channel_id=1, source_target_pairs={{0,1},{1,0},{2,3},{3,2},{4,5},{5,4},{6,7},{7,6},{8,9},{9,8},{10,11... | collective-permute-start | bytes 2359304 | tf_op jit(solution)/shard_map/ppermute | solution.py:40
  321.0 22.6 %collective-permute-start.39 = (bf16[4,32,3200]{2,1,0:T(8,128)(2,1)S(1)}, bf16[4,32,3200]{2,1,0:T(8,128)(2,1)S(1)}, u32[]{:S(2)}, u32[]{:S(2)}) collective-permute-start(bf16[4,32,3200]{2,1,0:T(8,128)(2,1)S(1)} %collective-permute-done.35), channel_id=1, source_target_pairs={{0,1},{1,0},{2,3},{3,2},{4,5},{5,4},{6,7},{7,6},{8,9},{9,8},{10,11... | collective-permute-start | bytes 2457608 | tf_op jit(solution)/shard_map/ppermute | solution.py:40
  321.9 21.8 %collective-permute-start.40 = (bf16[4,32,3200]{2,1,0:T(8,128)(2,1)}, bf16[4,32,3200]{2,1,0:T(8,128)(2,1)S(1)}, u32[]{:S(2)}, u32[]{:S(2)}) collective-permute-start(bf16[4,32,3200]{2,1,0:T(8,128)(2,1)} %collective-permute-done.36), channel_id=1, source_target_pairs={{0,1},{1,0},{2,3},{3,2},{4,5},{5,4},{6,7},{7,6},{8,9},{9,8},{10,11... | collective-permute-start | bytes 2457608 | tf_op jit(solution)/shard_map/ppermute | solution.py:40
  425.9 20.2 %collective-permute-start.62 = (bf16[16,1,32,2624]{3,2,1,0:T(8,128)(2,1)}, bf16[16,1,32,2624]{3,2,1,0:T(8,128)(2,1)}, u32[]{:S(2)}, u32[]{:S(2)}) collective-permute-start(bf16[16,1,32,2624]{3,2,1,0:T(8,128)(2,1)} %constant_dynamic-slice_fusion.16), channel_id=1, source_target_pairs={{0,1},{1,0},{2,3},{3,2},{4,5},{5,4},{6,7},{7,6},{8,9},{9,8},{10,11... | collective-permute-start | bytes 8060936 | tf_op jit(solution)/shard_map/ppermute | solution.py:40
  480.9 17.0 %collective-permute-start.98 = (bf16[4,2,32,1280]{3,2,0,1:T(8,128)(2,1)}, bf16[4,2,32,1280]{3,2,0,1:T(8,128)(2,1)}, u32[]{:S(2)}, u32[]{:S(2)}) collective-permute-start(bf16[4,2,32,1280]{3,2,0,1:T(8,128)(2,1)} %bitcast.554), channel_id=1, source_target_pairs={{0,4},{1,5},{2,6},{3,7},{4,0},{5,1},{6,2},{7,3},{8,12},{9,13},{10,... | collective-permute-start | bytes 1966088 | tf_op jit(solution)/shard_map/ppermute | solution.py:40
  482.8 18.1 %collective-permute-start.103 = (bf16[4,2,32,1344]{3,2,1,0:T(8,128)(2,1)}, bf16[4,2,32,1344]{3,2,1,0:T(8,128)(2,1)}, u32[]{:S(2)}, u32[]{:S(2)}) collective-permute-start(bf16[4,2,32,1344]{3,2,1,0:T(8,128)(2,1)} %dynamic-slice_bitcast_fusion.3), channel_id=1, source_target_pairs={{0,2},{1,3},{2,0},{3,1},{4,6},{5,7},{6,4},{7,5},{8,10},{9,11},{10,... | collective-permute-start | bytes 2064392 | tf_op jit(solution)/shard_map/ppermute | solution.py:40
  483.7 42.5 %collective-permute-start.63 = (bf16[16,1,32,5376]{3,2,0,1:T(8,128)(2,1)S(1)}, bf16[16,1,32,5376]{3,2,0,1:T(8,128)(2,1)}, u32[]{:S(2)}, u32[]{:S(2)}) collective-permute-start(bf16[16,1,32,5376]{3,2,0,1:T(8,128)(2,1)S(1)} %fusion.20), channel_id=1, source_target_pairs={{0,1},{1,0},{2,3},{3,2},{4,5},{5,4},{6,7},{7,6},{8,9},{9,8},{10,11... | collective-permute-start | bytes 16515080 | tf_op jit(solution)/shard_map/ppermute | solution.py:40
  490.9 21.0 %collective-permute-start.64 = (bf16[16,1,32,1024]{3,2,0,1:T(8,128)(2,1)S(1)}, bf16[16,1,32,1024]{3,2,0,1:T(8,128)(2,1)S(1)}, u32[]{:S(2)}, u32[]{:S(2)}) collective-permute-start(bf16[16,1,32,1024]{3,2,0,1:T(8,128)(2,1)S(1)} %dynamic-slice_bitcast_fusion.1), channel_id=1, source_target_pairs={{0,1},{1,0},{2,3},{3,2},{4,5},{5,4},{6,7},{7,6},{8,9},{9,8},{10,11... | collective-permute-start | bytes 3145736 | tf_op jit(solution)/shard_map/ppermute | solution.py:40
  593.6 68.6 %collective-permute-start.83 = (bf16[4,2,32,512]{3,2,1,0:T(8,128)(2,1)}, bf16[4,2,32,512]{3,2,1,0:T(8,128)(2,1)}, u32[]{:S(2)}, u32[]{:S(2)}) collective-permute-start(bf16[4,2,32,512]{3,2,1,0:T(8,128)(2,1)} %dynamic-slice_bitcast_fusion.10), channel_id=1, source_target_pairs={{0,2},{1,3},{2,0},{3,1},{4,6},{5,7},{6,4},{7,5},{8,10},{9,11},{10,... | collective-permute-start | bytes 786440 | tf_op jit(solution)/shard_map/ppermute | solution.py:40
  593.9 69.4 %collective-permute-start.78 = (bf16[4,2,32,512]{3,2,0,1:T(8,128)(2,1)}, bf16[4,2,32,512]{3,2,0,1:T(8,128)(2,1)}, u32[]{:S(2)}, u32[]{:S(2)}) collective-permute-start(bf16[4,2,32,512]{3,2,0,1:T(8,128)(2,1)} %bitcast.555), channel_id=1, source_target_pairs={{0,4},{1,5},{2,6},{3,7},{4,0},{5,1},{6,2},{7,3},{8,12},{9,13},{10,... | collective-permute-start | bytes 786440 | tf_op jit(solution)/shard_map/ppermute | solution.py:40
  595.3 27.0 %collective-permute-start.66 = (bf16[64,2048]{0,1:T(8,128)(2,1)}, bf16[64,2048]{0,1:T(8,128)(2,1)}, u32[]{:S(2)}, u32[]{:S(2)}) collective-permute-start(bf16[64,2048]{0,1:T(8,128)(2,1)} %slice.526), channel_id=1, source_target_pairs={{1,0},{2,1},{3,2},{4,3},{5,4},{6,5},{7,6},{8,7},{9,8},{10,9},{11,1... | collective-permute-start | bytes 786440 | tf_op jit(solution)/shard_map/ppermute | solution.py:36
  604.1 81.4 %collective-permute-start.93 = (bf16[4,2,32,2688]{3,2,1,0:T(8,128)(2,1)}, bf16[4,2,32,2688]{3,2,1,0:T(8,128)(2,1)}, u32[]{:S(2)}, u32[]{:S(2)}) collective-permute-start(bf16[4,2,32,2688]{3,2,1,0:T(8,128)(2,1)} %dynamic-slice_bitcast_fusion), channel_id=1, source_target_pairs={{0,2},{1,3},{2,0},{3,1},{4,6},{5,7},{6,4},{7,5},{8,10},{9,11},{10,... | collective-permute-start | bytes 4128776 | tf_op jit(solution)/shard_map/ppermute | solution.py:40
  607.0 80.5 %collective-permute-start.88 = (bf16[4,2,32,2688]{3,2,0,1:T(8,128)(2,1)}, bf16[4,2,32,2688]{3,2,0,1:T(8,128)(2,1)}, u32[]{:S(2)}, u32[]{:S(2)}) collective-permute-start(bf16[4,2,32,2688]{3,2,0,1:T(8,128)(2,1)} %bitcast.552), channel_id=1, source_target_pairs={{0,4},{1,5},{2,6},{3,7},{4,0},{5,1},{6,2},{7,3},{8,12},{9,13},{10,... | collective-permute-start | bytes 4128776 | tf_op jit(solution)/shard_map/ppermute | solution.py:40
  680.9 51.9 %collective-permute-start.67 = (bf16[16,1,32,3200]{3,2,0,1:T(8,128)(2,1)S(1)}, bf16[16,1,32,3200]{3,2,0,1:T(8,128)(2,1)S(1)}, u32[]{:S(2)}, u32[]{:S(2)}) collective-permute-start(bf16[16,1,32,3200]{3,2,0,1:T(8,128)(2,1)S(1)} %fusion.34), channel_id=1, source_target_pairs={{0,1},{1,0},{2,3},{3,2},{4,5},{5,4},{6,7},{7,6},{8,9},{9,8},{10,11... | collective-permute-start | bytes 9830408 | tf_op jit(solution)/shard_map/ppermute | solution.py:40
  705.2 22.4 %collective-permute-start.96 = (bf16[32,2688]{1,0:T(8,128)(2,1)S(1)}, bf16[32,2688]{1,0:T(8,128)(2,1)S(1)}, u32[]{:S(2)}, u32[]{:S(2)}) collective-permute-start(bf16[32,2688]{1,0:T(8,128)(2,1)S(1)} %get-tuple-element.136), channel_id=1, source_target_pairs={{0,16},{1,17},{2,18},{3,19},{4,20},{5,21},{6,22},{7,23},{8,24},{9,... | collective-permute-start | bytes 516104 | tf_op jit(solution)/shard_map/ppermute | solution.py:40
  705.5 22.2 %collective-permute-start.90 = (bf16[32,2688]{1,0:T(8,128)(2,1)S(1)}, bf16[32,2688]{1,0:T(8,128)(2,1)S(1)}, u32[]{:S(2)}, u32[]{:S(2)}) collective-permute-start(bf16[32,2688]{1,0:T(8,128)(2,1)S(1)} %get-tuple-element.131), channel_id=1, source_target_pairs={{0,8},{1,9},{2,10},{3,11},{4,12},{5,13},{6,14},{7,15},{8,0},{9,1},... | collective-permute-start | bytes 516104 | tf_op jit(solution)/shard_map/ppermute | solution.py:40
  714.2 18.5 %collective-permute-start.91 = (bf16[32,2688]{1,0:T(8,128)(2,1)S(1)}, bf16[32,2688]{1,0:T(8,128)(2,1)S(1)}, u32[]{:S(2)}, u32[]{:S(2)}) collective-permute-start(bf16[32,2688]{1,0:T(8,128)(2,1)S(1)} %get-tuple-element.133), channel_id=1, source_target_pairs={{0,16},{1,17},{2,18},{3,19},{4,20},{5,21},{6,22},{7,23},{8,24},{9,... | collective-permute-start | bytes 516104 | tf_op jit(solution)/shard_map/ppermute | solution.py:40
  734.2 17.2 %collective-permute-start.68 = (bf16[4,2,32,1536]{3,2,0,1:T(8,128)(2,1)S(1)}, bf16[4,2,32,1536]{3,2,0,1:T(8,128)(2,1)S(1)}, u32[]{:S(2)}, u32[]{:S(2)}) collective-permute-start(bf16[4,2,32,1536]{3,2,0,1:T(8,128)(2,1)S(1)} %bitcast.626), channel_id=1, source_target_pairs={{0,4},{1,5},{2,6},{3,7},{4,0},{5,1},{6,2},{7,3},{8,12},{9,13},{10,... | collective-permute-start | bytes 2359304 | tf_op jit(solution)/shard_map/ppermute | solution.py:40
  735.9 21.4 %collective-permute-start.73 = (bf16[4,2,32,1664]{3,2,1,0:T(8,128)(2,1)S(1)}, bf16[4,2,32,1664]{3,2,1,0:T(8,128)(2,1)S(1)}, u32[]{:S(2)}, u32[]{:S(2)}) collective-permute-start(bf16[4,2,32,1664]{3,2,1,0:T(8,128)(2,1)S(1)} %dynamic-slice_bitcast_fusion.2), channel_id=1, source_target_pairs={{0,2},{1,3},{2,0},{3,1},{4,6},{5,7},{6,4},{7,5},{8,10},{9,11},{10,... | collective-permute-start | bytes 2555912 | tf_op jit(solution)/shard_map/ppermute | solution.py:40
  (143 other events, 2389.7 us)

commit v2 on v1

--- a/solution.py
+++ b/solution.py
@@ -53,32 +53,48 @@
     return [list(range(first, count, 8)) for first in range(8)]
 
 
-def gather_rows(shard):
-    count = lax.axis_size("dev")
-    dev_index = lax.axis_index("dev")
-    bits = place_bits(dev_index)
+def gather_far(shard):
+    count = lax.axis_size("dev")
     far = count // 8
-    mine_far = dev_index // 8
-    rows, width = shard.shape
-    full = jnp.zeros((far, 2, 2, 2, rows, width), shard.dtype)
-    for first, last, order in column_halves(width):
+    mine_far = lax.axis_index("dev") // 8
+    halves = []
+    for first, last, _ in column_halves(shard.shape[1]):
         part = shard[:, first:last]
         if far <= 4:
-            held = jnp.zeros((far, rows, last - first), shard.dtype)
+            held = jnp.zeros((far,) + part.shape, shard.dtype)
             held = lax.dynamic_update_slice(held, part[None], (mine_far, 0, 0))
             for step in range(1, far):
                 moved = swapped(part, count, 8 * step)
                 held = lax.dynamic_update_slice(held, moved[None], (mine_far ^ step, 0, 0))
         else:
             held = lax.all_gather(part, "dev", axis=0, axis_index_groups=far_groups(count))
-        pieces = [(0, held)]
-        for mask in order + (1,):
-            pieces = pieces + [(seen | mask, swapped(piece, count, mask)) for seen, piece in pieces]
-        for seen, piece in pieces:
-            spot = {bit: bits[bit] ^ (1 if seen & bit else 0) for bit in (1, 2, 4)}
-            full = lax.dynamic_update_slice(
-                full, piece[:, None, None, None], (0, spot[4], spot[2], spot[1], 0, first)
-            )
+        halves.append([held])
+    return halves
+
+
+def gather_near(halves, stage):
+    count = lax.axis_size("dev")
+    width = sum(pieces[0].shape[-1] for pieces in halves)
+    return [
+        pieces + [swapped(piece, count, order[stage]) for piece in pieces]
+        for pieces, (_, _, order) in zip(halves, column_halves(width))
+    ]
+
+
+def gather_last(halves):
+    count = lax.axis_size("dev")
+    bits = place_bits(lax.axis_index("dev"))
+    far, rows, _ = halves[0][0].shape
+    width = sum(pieces[0].shape[-1] for pieces in halves)
+    full = jnp.zeros((far, 2, 2, 2, rows, width), halves[0][0].dtype)
+    for pieces, (first, _, order) in zip(halves, column_halves(width)):
+        for place, piece in enumerate(pieces):
+            seen = (order[0] if place & 1 else 0) + (order[1] if place & 2 else 0)
+            for core, block in ((0, piece), (1, swapped(piece, count, 1))):
+                spot = {bit: bits[bit] ^ (1 if (seen + core) & bit else 0) for bit in (1, 2, 4)}
+                full = lax.dynamic_update_slice(
+                    full, block[:, None, None, None], (0, spot[4], spot[2], spot[1], 0, first)
+                )
     return full.reshape(count * rows, width)
 
 
@@ -90,26 +106,32 @@
     given = lax.dynamic_slice_in_dim(split, 1 - mine, 1, axis=1)
     taken = swapped(given, count, 1)
     kept = lax.dynamic_slice_in_dim(split, mine, 1, axis=1)
-    return (kept.astype(jnp.float32) + taken.astype(jnp.float32)).astype(jnp.bfloat16)
-
-
-def scatter_rest(half):
-    count = lax.axis_size("dev")
-    dev_index = lax.axis_index("dev")
-    bits = place_bits(dev_index)
+    total = (kept.astype(jnp.float32) + taken.astype(jnp.float32)).astype(jnp.bfloat16)
+    whole = total.reshape(count // 8, 2, 2, rows, grad.shape[1])
+    return [whole[..., first:last] for first, last, _ in column_halves(grad.shape[1])]
+
+
+def scatter_near(parts, stage):
+    count = lax.axis_size("dev")
+    bits = place_bits(lax.axis_index("dev"))
+    width = sum(part.shape[-1] for part in parts)
+    outs = []
+    for part, (_, _, order) in zip(parts, column_halves(width)):
+        mask = order[1 - stage]
+        axis = 1 if mask == 4 or part.ndim == 4 else 2
+        given = lax.dynamic_index_in_dim(part, 1 - bits[mask], axis, keepdims=False)
+        kept = lax.dynamic_index_in_dim(part, bits[mask], axis, keepdims=False)
+        taken = swapped(given, count, mask)
+        outs.append((kept.astype(jnp.float32) + taken.astype(jnp.float32)).astype(jnp.bfloat16))
+    return outs
+
+
+def scatter_far(parts):
+    count = lax.axis_size("dev")
     far = count // 8
-    mine_far = dev_index // 8
-    rows, width = half.shape[2:]
-    whole = half.reshape(far, 2, 2, rows, width)
+    mine_far = lax.axis_index("dev") // 8
     outs = []
-    for first, last, order in column_halves(width):
-        part = whole[..., first:last]
-        for mask in order[::-1]:
-            axis = 1 if mask == 4 or part.ndim == 4 else 2
-            given = lax.dynamic_index_in_dim(part, 1 - bits[mask], axis, keepdims=False)
-            kept = lax.dynamic_index_in_dim(part, bits[mask], axis, keepdims=False)
-            taken = swapped(given, count, mask)
-            part = (kept.astype(jnp.float32) + taken.astype(jnp.float32)).astype(jnp.bfloat16)
+    for part in parts:
         if far <= 4:
             total = lax.dynamic_index_in_dim(part, mine_far, 0, keepdims=False).astype(jnp.float32)
             for step in range(1, far):
@@ -117,7 +139,7 @@
                 total = total + swapped(given, count, 8 * step).astype(jnp.float32)
         else:
             total = lax.psum_scatter(
-                part.reshape(far * rows, last - first),
+                part.reshape(-1, part.shape[-1]),
                 "dev",
                 scatter_dimension=0,
                 tiled=True,
@@ -127,8 +149,8 @@
     return jnp.concatenate(outs, axis=1)
 
 
-def with_column(matrix, vector):
-    return jnp.concatenate([matrix, jnp.pad(vector[:, None], ((0, 0), (0, 127)))], axis=1)
+def tie(*values):
+    return lax.optimization_barrier(values)
 
 
 def layer_norm(values):
@@ -213,20 +235,20 @@
     offsets = jnp.arange(query_block)[:, None] - jnp.arange(window_rows)[None, :] + HALF
     nearby = jnp.abs(offsets) <= HALF
     gains = jnp.pad(jnp.stack([gain_attn, gain_mlp], axis=1), ((0, 0), (0, 126)))
-    qkv_and_gains = gather_rows(jnp.concatenate([w_qkv, gains], axis=1))
+    first_set = gather_near(gather_far(jnp.concatenate([w_qkv, gains], axis=1)), 0)
+    first_set, second_shard = tie(first_set, jnp.concatenate([w_out, w_in], axis=1))
+    second_set = gather_far(second_shard)
+    qkv_and_gains = gather_last(gather_near(first_set, 1))
     full_qkv = qkv_and_gains[:, : 3 * model_width]
     full_gain_attn = qkv_and_gains[:, 3 * model_width]
     full_gain_mlp = qkv_and_gains[:, 3 * model_width + 1]
-    out_and_in = gather_rows(jnp.concatenate([w_out, w_in], axis=1))
-    full_out = out_and_in[:, :model_width]
-    full_in = out_and_in[:, model_width:]
-    down_rows = gather_rows(w_down.T)
     inputs = tokens.astype(jnp.float32)
     normed_attn, inv_attn = layer_norm(inputs)
     h_attn = (normed_attn * full_gain_attn.astype(jnp.float32)).astype(jnp.bfloat16)
-    projected = jnp.dot(h_attn, full_qkv, preferred_element_type=jnp.float32).reshape(
-        tok_rows, 3, head_count, HDIM
-    )
+    projected = jnp.dot(h_attn, full_qkv, preferred_element_type=jnp.float32)
+    projected, second_set = tie(projected, second_set)
+    projected = projected.reshape(tok_rows, 3, head_count, HDIM)
+    second_set = gather_near(second_set, 0)
     queries = apply_rope(projected[:, 0], cosine, sine_table).astype(jnp.bfloat16)
     keys_own = (
         apply_rope(projected[:, 1], cosine, sine_table)
@@ -236,7 +258,7 @@
     values_own = projected[:, 2].astype(jnp.bfloat16).reshape(tok_rows, model_width)
     key_values = padded(jnp.concatenate([keys_own, values_own], axis=1), (("dev", 0),), HALF)
 
-    def block_scores(block_start):
+    def block_scores(block_start, queries, key_values):
         query_tile = queries[block_start : block_start + query_block]
         window = key_values[block_start : block_start + window_rows]
         key_tile = window[:, :model_width].reshape(window_rows, head_count, HDIM)
@@ -258,7 +280,7 @@
     block_outputs = []
     for block_number in range(block_total):
         block_start = block_number * query_block
-        query_tile, key_tile, value_tile, scores = block_scores(block_start)
+        query_tile, key_tile, value_tile, scores = block_scores(block_start, queries, key_values)
         row_peak = jnp.max(scores, axis=-1, keepdims=True)
         exponent = jnp.exp(scores - row_peak)
         row_total = jnp.sum(exponent, axis=-1, keepdims=True)
@@ -267,10 +289,25 @@
         block_outputs.append(
             jnp.einsum(
                 "hqk,khd->qhd", attn_probs, value_tile, preferred_element_type=jnp.float32
-            ).reshape(query_block, model_width)
-        )
-    mixed = jnp.concatenate(block_outputs, axis=0).astype(jnp.bfloat16)
-    residual = inputs + jnp.dot(mixed, full_out, preferred_element_type=jnp.float32)
+            )
+            .reshape(query_block, model_width)
+            .astype(jnp.bfloat16)
+        )
+        if block_number == 0:
+            block_outputs[0], second_set, third_shard, queries = tie(
+                block_outputs[0], second_set, w_down.T, queries
+            )
+            second_set = gather_near(second_set, 1)
+            third_set = gather_far(third_shard)
+    mixed = jnp.concatenate(block_outputs, axis=0)
+    out_and_in = gather_last(second_set)
+    full_out = out_and_in[:, :model_width]
+    full_in = out_and_in[:, model_width:]
+    third_set = gather_near(third_set, 0)
+    branch = jnp.dot(mixed, full_out, preferred_element_type=jnp.float32)
+    branch, third_set = tie(branch, third_set)
+    residual = inputs + branch
+    down_rows = gather_last(gather_near(third_set, 1))
     normed_mlp, inv_mlp = layer_norm(residual)
     h_mlp = (normed_mlp * full_gain_mlp.astype(jnp.float32)).astype(jnp.bfloat16)
     gate_up = jnp.dot(h_mlp, full_in, preferred_element_type=jnp.float32)
@@ -280,32 +317,32 @@
     layer_out = (
         residual + contract_cols(activated, down_rows)
     ).astype(jnp.bfloat16)
-    down_half = scatter_start(contract_rows(cotangent, activated))
+    down_parts = scatter_start(contract_rows(cotangent, activated))
     d_activated = jnp.dot(cotangent, down_rows, preferred_element_type=jnp.float32)
     _, geglu_back = jax.vjp(geglu, gate_part, up_part)
     d_gate, d_up = geglu_back(d_activated)
     d_gate_up = jnp.concatenate([d_gate, d_up], axis=1).astype(jnp.bfloat16)
-    d_gate_up, down_half = lax.optimization_barrier((d_gate_up, down_half))
-    down_part = scatter_rest(down_half).T
-    in_grad = contract_rows(h_mlp, d_gate_up)
+    d_gate_up, down_parts = tie(d_gate_up, down_parts)
+    down_parts = scatter_near(down_parts, 0)
+    in_parts = scatter_start(contract_rows(h_mlp, d_gate_up))
+    d_gate_up, in_parts, down_parts = tie(d_gate_up, in_parts, down_parts)
+    in_parts = scatter_near(in_parts, 0)
+    down_parts = scatter_near(down_parts, 1)
     d_h_mlp = contract_cols(d_gate_up, full_in)
-    mlp_gain_grad = jnp.sum(d_h_mlp * normed_mlp, axis=0)
-    in_half = scatter_start(with_column(in_grad, mlp_gain_grad))
     d_residual = cotangent.astype(jnp.float32) + norm_back(
         d_h_mlp * full_gain_mlp.astype(jnp.float32), normed_mlp, inv_mlp
     )
     d_branch = d_residual.astype(jnp.bfloat16)
-    out_half = scatter_start(contract_rows(mixed, d_branch))
-    d_branch, in_half, out_half = lax.optimization_barrier((d_branch, in_half, out_half))
-    in_sums = scatter_rest(in_half)
-    in_part, mlp_gain_part = in_sums[:, : 2 * hidden_units], in_sums[:, 2 * hidden_units]
-    out_part = scatter_rest(out_half)
+    d_branch, in_parts, down_parts = tie(d_branch, in_parts, down_parts)
+    in_parts = scatter_near(in_parts, 1)
+    down_part = scatter_far(down_parts).T
+    out_parts = scatter_start(contract_rows(mixed, d_branch))
     d_mixed = contract_cols(d_branch, full_out).astype(jnp.bfloat16)
     d_query_list = []
     d_window = jnp.zeros((tok_rows + 2 * HALF, 2 * model_width), jnp.float32)
     for block_number in range(block_total):
         block_start = block_number * query_block
-        query_tile, key_tile, value_tile, scores = block_scores(block_start)
+        query_tile, key_tile, value_tile, scores = block_scores(block_start, queries, key_values)
         attn_probs = jnp.exp(scores - log_totals[block_number])
         grad_tile = d_mixed[block_start : block_start + query_block].reshape(
             query_block, head_count, HDIM
@@ -334,7 +371,16 @@
             [d_keys.reshape(window_rows, model_width), d_values.reshape(window_rows, model_width)],
             axis=1,
         )
+        if block_number == 0:
+            d_mixed, window_grad, in_parts, out_parts = tie(
+                d_mixed, window_grad, in_parts, out_parts
+            )
+            in_sums = scatter_far(in_parts)
+            out_parts = scatter_near(out_parts, 0)
         d_window = d_window.at[block_start : block_start + window_rows].add(window_grad)
+        if block_number == block_total - 1:
+            d_window, in_part, out_parts = tie(d_window, in_sums, out_parts)
+            out_parts = scatter_near(out_parts, 1)
     from_right = passed_along(d_window[:HALF].astype(jnp.bfloat16), "dev", -1).astype(jnp.float32)
     from_left = passed_along(d_window[tok_rows + HALF :].astype(jnp.bfloat16), "dev", 1).astype(
         jnp.float32
@@ -351,14 +397,20 @@
         ],
         axis=1,
     ).astype(jnp.bfloat16)
+    qkv_parts = scatter_start(contract_rows(h_attn, d_projected))
+    out_part = scatter_far(out_parts)
+    d_projected, qkv_parts = tie(d_projected, qkv_parts)
+    qkv_part = scatter_far(scatter_near(scatter_near(qkv_parts, 0), 1))
     d_h_attn = contract_cols(d_projected, full_qkv)
-    attn_gain_grad = jnp.sum(d_h_attn * normed_attn, axis=0)
     tokens_grad = (
         d_residual + norm_back(d_h_attn * full_gain_attn.astype(jnp.float32), normed_attn, inv_attn)
     ).astype(jnp.bfloat16)
-    qkv_grad = contract_rows(h_attn, d_projected)
-    qkv_sums = scatter_rest(scatter_start(with_column(qkv_grad, attn_gain_grad)))
-    qkv_part, attn_gain_part = qkv_sums[:, : 3 * model_width], qkv_sums[:, 3 * model_width]
+    attn_gain_part = jnp.sum(w_qkv.astype(jnp.float32) * qkv_part, axis=1) / gain_attn.astype(
+        jnp.float32
+    )
+    mlp_gain_part = jnp.sum(w_in.astype(jnp.float32) * in_part, axis=1) / gain_mlp.astype(
+        jnp.float32
+    )
     return (
         layer_out,
         tokens_grad,

time: 793 us -> 758 us (0.956)
  waiting for transfers between devices: 254 us -> 221 us
  other arithmetic: 100 us -> 109 us
  starting transfers between devices: 121 us -> 113 us
    ppermute x104, waiting for transfers between devices: 254 us -> 221 us  [swapped(): return lax.ppermute(value, 'dev', [(i, i ^ mask) for i in range(count)])]
    optimization_barrier x0 -> x5, local copies, waits for them, and re-layouts: none -> 11.9 us  [tie(): return lax.optimization_barrier(values)]
    dynamic_update_slice x70 -> x71, local copies, waits for them, and re-layouts: 42.6 us -> 31.6 us  [the longest x48 26.9 us: gather_last(): lax.dynamic_update_slice(full, block[:, None, None, None], (0, spot[4], s...]
    dot_general x3, matrix products: 8.32 us -> 18.4 us  [local(): jnp.einsum('qhd,khd->hqk', grad_tile, value_tile, preferred_element_type=...]
    dot_general x4, matrix products: 40.4 us -> 32 us  [contract_cols(): lax.dot_general(first_mat, second_mat, (((1,), (1,)), ((), ())), preferre...]
    unnamed x172 -> x224, local copies, waits for them, and re-layouts: 15.4 us -> 21.9 us
    another operation x3 -> x4, other arithmetic: 20.6 us -> 21.9 us
  transfers between devices with their start and end apart: 108 -> 108, of which waited for: 50 -> 44; matrix products, arithmetic and copies ran while one was open for 27% -> 33% of each run, Pallas kernels for 0% -> 0%
where the time goes in v2:
time: 758 us; the launch traced here: 748 us
  waiting for transfers between devices  221 us (29%)
  matrix products  171 us (23%)
  local copies, waits for them, and re-layouts  131 us (17%)
  starting transfers between devices  113 us (15%)
  other arithmetic  109 us (14%)
    ppermute x104, waiting for transfers between devices, swapped(): return lax.ppermute(value, 'dev', [(i, i ^ mask) for i in range(count)])  221 us
    ppermute x104, starting transfers between devices, swapped(): return lax.ppermute(value, 'dev', [(i, i ^ mask) for i in range(count)])  106 us
    dot_general x4, matrix products, contract_cols(): lax.dot_general(first_mat, second_mat, (((1,), (1,)), ((), ())), preferre...  32 us
    dot_general x4, matrix products, contract_rows(): lax.dot_general(first_mat, second_mat, (((0,), (0,)), ((), ())), preferre...  30.7 us
    dot_general x1, matrix products, local(): jnp.dot(cotangent, down_rows, preferred_element_type=jnp.float32)  27 us
    dynamic_update_slice x48, local copies, waits for them, and re-layouts, gather_last(): lax.dynamic_update_slice(full, block[:, None, None, None], (0, spot[4], s...  26.9 us
    unnamed x224, local copies, waits for them, and re-layouts  21.9 us
    another operation x4, other arithmetic  21.9 us
  transfers between devices with their start and end apart: 108, of which 44 were waited for; matrix products, arithmetic and copies ran while one was open for 33% of the time, Pallas kernels for 0%

profile of v2, /device:TPU:0, one launch (start us, length us, event | category | flops | bytes accessed | tf_op | source)
XLA Modules:
  0.0 747.9 jit_solution(4247757045380458352)
XLA Ops:
  41.1 5.5 collective-permute-done.20
  49.0 8.7 %collective-permute-done.21 = bf16[32,3072]{1,0:T(8,128)(2,1)S(1)} collective-permute-done((bf16[32,3072]{1,0:T(8,128)(2,1)S(1)}, bf16[32,3072]{1,0:T(8,128)(2,1)S(1)}, u32[]{:S(2)}, u32[]{:S(2)}) %collective-permute-start.21) | collective-permute-done | bytes 196640 | tf_op jit(solution)/shard_map/ppermute | solution.py:40
  60.1 6.2 collective-permute-done.22
  67.4 5.0 collective-permute-done.23
  74.7 7.8 %collective-permute-done.24 = bf16[32,3200]{1,0:T(8,128)(2,1)S(1)} collective-permute-done((bf16[32,3200]{1,0:T(8,128)(2,1)S(1)}, bf16[32,3200]{1,0:T(8,128)(2,1)S(1)}, u32[]{:S(2)}, u32[]{:S(2)}) %collective-permute-start.24) | collective-permute-done | bytes 204832 | tf_op jit(solution)/shard_map/ppermute | solution.py:40
  84.5 5.9 collective-permute-done.25
  94.4 8.7 %collective-permute-done.16 = bf16[4,32,1664]{2,1,0:T(8,128)(2,1)S(1)} collective-permute-done((bf16[4,32,1664]{2,1,0:T(8,128)(2,1)S(1)}, bf16[4,32,1664]{2,1,0:T(8,128)(2,1)S(1)}, u32[]{:S(2)}, u32[]{:S(2)}) %collective-permute-start.16) | collective-permute-done | bytes 426016 | tf_op jit(solution)/shard_map/ppermute | solution.py:40
  103.1 8.7 %collective-permute-done.18 = bf16[4,32,1664]{2,1,0:T(8,128)(2,1)S(1)} collective-permute-done((bf16[4,32,1664]{2,1,0:T(8,128)(2,1)S(1)}, bf16[4,32,1664]{2,1,0:T(8,128)(2,1)S(1)}, u32[]{:S(2)}, u32[]{:S(2)}) %collective-permute-start.18) | collective-permute-done | bytes 426016 | tf_op jit(solution)/shard_map/ppermute | solution.py:40
  117.1 7.7 %fusion.17 = f32[768,3072]{1,0:T(8,128)} fusion(bf16[1024,3200]{1,0:T(8,128)(2,1)S(1)} %bitcast.577, bf16[768,1024]{1,0:T(8,128)(2,1)S(1)} %copy-done.4, f32[1024]{0:T(1024)S(1)} %get-tuple-element.161, f32[768]{0:T(1024)S(1)} %add_rsqrt_fusion.1, f32[768]{0:T(1024)S(1)} %broadcast_multiply_fusion.7), kind=kOutput, calls=%fused_computation.58 | convolution fusion | flops 4835770368 | bytes 17313792 | tf_op jit(solution)/shard_map/dot_general | solution.py:248
  124.8 9.6 %copy.44 = f32[768,3072]{0,1:T(8,128)} copy(f32[768,3072]{1,0:T(8,128)} %fusion.17) | data formatting | bytes 18874368 | tf_op jit(solution)/shard_map/optimization_barrier | solution.py:153
  161.8 6.4 pad_maximum_fusion.6
  175.2 12.3 %collective-permute-done.27 = bf16[4,32,3072]{2,1,0:T(8,128)(2,1)} collective-permute-done((bf16[4,32,3072]{2,1,0:T(8,128)(2,1)}, bf16[4,32,3072]{2,1,0:T(8,128)(2,1)}, u32[]{:S(2)}, u32[]{:S(2)}) %collective-permute-start.27) | collective-permute-done | bytes 786464 | tf_op jit(solution)/shard_map/ppermute | solution.py:40
  197.3 4.2 fusion.78
  208.7 5.9 broadcast_in_dim.381
  230.8 13.0 %collective-permute-done.32 = bf16[4,32,3072]{2,1,0:T(8,128)(2,1)S(1)} collective-permute-done((bf16[4,32,3072]{2,1,0:T(8,128)(2,1)S(1)}, bf16[4,32,3072]{2,1,0:T(8,128)(2,1)S(1)}, u32[]{:S(2)}, u32[]{:S(2)}) %collective-permute-start.32) | collective-permute-done | bytes 786464 | tf_op jit(solution)/shard_map/ppermute | solution.py:40
  245.8 14.1 %collective-permute-done.34 = bf16[4,32,3072]{2,1,0:T(8,128)(2,1)S(1)} collective-permute-done((bf16[4,32,3072]{2,1,0:T(8,128)(2,1)}, bf16[4,32,3072]{2,1,0:T(8,128)(2,1)S(1)}, u32[]{:S(2)}, u32[]{:S(2)}) %collective-permute-start.34) | collective-permute-done | bytes 786464 | tf_op jit(solution)/shard_map/ppermute | solution.py:40
  268.0 13.1 %collective-permute-done.40 = bf16[4,32,3200]{2,1,0:T(8,128)(2,1)S(1)} collective-permute-done((bf16[4,32,3200]{2,1,0:T(8,128)(2,1)S(1)}, bf16[4,32,3200]{2,1,0:T(8,128)(2,1)S(1)}, u32[]{:S(2)}, u32[]{:S(2)}) %collective-permute-start.40) | collective-permute-done | bytes 819232 | tf_op jit(solution)/shard_map/ppermute | solution.py:40
  295.3 15.8 %fusion.2 = f32[768,5248]{1,0:T(8,128)} fusion(bf16[1024,6272]{1,0:T(8,128)(2,1)} %bitcast.558, f32[768,1024]{1,0:T(8,128)S(1)} %get-tuple-element.173, f32[1024]{0:T(1024)S(1)} %get-tuple-element.160, f32[768]{0:T(1024)S(1)} %add_rsqrt_fusion, f32[768]{0:T(1024)S(1)} %broadcast_multiply_fusion.6), kind=kOutput, calls=%fused_computation.5 | convolution fusion | flops 8257536000 | bytes 30025728 | tf_op jit(solution)/shard_map/dot_general | solution.py:313
  324.4 7.1 collective-permute-done.60
  334.5 27.0 %add_convert_fusion.1 = (bf16[768,2624]{1,0:T(8,128)(2,1)}, f32[768,2624]{1,0:T(8,128)}, f32[2624,768]{0,1:T(8,128)}) fusion(f32[768,5248]{1,0:T(8,128)S(1)} %copy-done.9, bf16[768,1024]{1,0:T(8,128)(2,1)} %param.29, bf16[1024,2624]{1,0:T(8,128)(2,1)S(1)} %bitcast.592), kind=kOutput, calls=%fused_computation.11 | convolution fusion | flops 4274307072 | bytes 43220992 | tf_op jit(solution)/shard_map/dot_general | solution.py:321
  361.5 13.9 %fusion.5 = (bf16[768,2624]{1,0:T(8,128)(2,1)}, bf16[768,2624]{1,0:T(8,128)(2,1)S(1)}) fusion(f32[2624,768]{0,1:T(8,128)} %get-tuple-element.252, f32[768,2624]{1,0:T(8,128)} %get-tuple-element.171, f32[768,5248]{1,0:T(8,128)} %fusion.2), kind=kLoop, calls=%fused_computation.10 | loop fusion | flops 12091392 | bytes 40304640 | tf_op jit(solution)/shard_map/convert.33
  377.4 6.3 fusion.19
  383.7 8.2 %copy.74 = bf16[1024,2624]{1,0:T(8,128)(2,1)} copy(bf16[1024,2624]{0,1:T(8,128)(2,1)} %fusion.19) | data formatting | bytes 10747904 | tf_op jit(solution)/shard_map/convert_element_type | solution.py:105
  395.4 8.7 %pad_maximum_fusion = bf16[768,5248]{1,0:T(8,128)(2,1)} fusion(bf16[768,2624]{1,0:T(8,128)(2,1)} %get-tuple-element.176, bf16[768,2624]{1,0:T(8,128)(2,1)} %get-tuple-element.170), kind=kLoop, calls=%fused_computation.26 | loop fusion | flops 16121856 | bytes 16121856 | tf_op jit(solution)/shard_map/concatenate | solution.py:324
  409.9 13.4 %convolution_convert_fusion = bf16[1024,5248]{1,0:T(8,128)(2,1)S(1)} fusion(bf16[768,5248]{1,0:T(8,128)(2,1)} %pad_maximum_fusion, f32[768,1024]{1,0:T(8,128)S(1)} %get-tuple-element.173, f32[1024]{0:T(1024)S(1)} %get-tuple-element.160, f32[768]{0:T(1024)S(1)} %add_rsqrt_fusion, f32[768]{0:T(1024)S(1)} %broadcast_multiply_fusion.6), kind=kOutput, calls=%fused_computation.1 | convolution fusion | flops 8262909952 | bytes 21964800 | tf_op jit(solution)/shard_map/dot_general | solution.py:195
  429.6 5.2 fusion.89
  437.0 8.3 %add_convert_fusion.4 = bf16[768,1024]{1,0:T(8,128)(2,1)} fusion(f32[768,1024]{1,0:T(8,128)S(1)} %get-tuple-element.173, bf16[768,2624]{1,0:T(8,128)(2,1)S(1)} %copy-done.35, bf16[1024,2624]{1,0:T(8,128)(2,1)} %bitcast.593), kind=kOutput, calls=%fused_computation.112 | convolution fusion | flops 4128768000 | bytes 14123008 | tf_op jit(solution)/shard_map/dot_general | solution.py:201
  445.3 6.4 collective-permute-done.64
  453.2 5.4 add_convert_fusion
  465.9 14.3 %multiply_reduce_fusion.6 = (f32[768]{0:T(1024)S(1)}, f32[768]{0:T(1024)S(1)}, f32[768,1024]{1,0:T(8,128)S(1)}) fusion(f32[1024]{0:T(1024)S(1)} %copy-done.86, f32[768]{0:T(1024)S(1)} %copy-done.90, f32[768,1024]{1,0:T(8,128)S(1)} %get-tuple-element.173, f32[768]{0:T(1024)S(1)} %copy-done.81, bf16[768,5248]{1,0:T(8,128)(2,1)} %pad_maximum_fusion, ...), kind=kOutput, calls=%fused_computation.123 | convolution fusion | flops 8259106816 | bytes 25116672 | tf_op jit(solution)/shard_map/dot_general | solution.py:201
  484.6 12.5 %collective-permute-done.66 = bf16[4,2,32,2560]{3,2,0,1:T(8,128)(2,1)} collective-permute-done((bf16[4,2,32,2560]{3,2,0,1:T(8,128)(2,1)}, bf16[4,2,32,2560]{3,2,0,1:T(8,128)(2,1)}, u32[]{:S(2)}, u32[]{:S(2)}) %collective-permute-start.66) | collective-permute-done | bytes 1310752 | tf_op jit(solution)/shard_map/ppermute | solution.py:40
  511.7 5.6 multiply_reduce_fusion.2
  534.7 9.4 %collective-permute-done.70 = bf16[4,32,2560]{2,1,0:T(8,128)(2,1)S(1)} collective-permute-done((bf16[4,32,2560]{2,1,0:T(8,128)(2,1)S(1)}, bf16[4,32,2560]{2,1,0:T(8,128)(2,1)S(1)}, u32[]{:S(2)}, u32[]{:S(2)}) %collective-permute-start.70) | collective-permute-done | bytes 655392 | tf_op jit(solution)/shard_map/ppermute | solution.py:40
  551.4 8.0 %multiply_reduce_fusion = (f32[16,256]{1,0:T(8,128)S(1)}, f32[16,256,384]{2,1,0:T(8,128)}) fusion(f32[16,256,384]{2,1,0:T(8,128)} %copy-done, f32[16,256]{1,0:T(8,128)S(1)} %log_add_fusion, bf16[256,16,64]{0,2,1:T(8,128)(2,1)} %bitcast.594, bf16[384,16,64]{0,2,1:T(8,128)(2,1)} %bitcast.600), kind=kOutput, calls=%fused_computation.34 | convolution fusion | flops 206041088 | bytes 13926400 | tf_op jit(solution)/shard_map/qhd,khd->hqk/dot_general | solution.py:350
  563.0 4.8 multiply_reduce_fusion.1
  589.9 4.3 collective-permute-done.74
  599.1 10.7 %collective-permute-done.77 = bf16[32,2688]{1,0:T(8,128)(2,1)S(1)} collective-permute-done((bf16[32,2688]{1,0:T(8,128)(2,1)S(1)}, bf16[32,2688]{1,0:T(8,128)(2,1)S(1)}, u32[]{:S(2)}, u32[]{:S(2)}) %collective-permute-start.77) | collective-permute-done | bytes 172064 | tf_op jit(solution)/shard_map/ppermute | solution.py:40
  611.6 4.6 collective-permute-done.80
  621.2 4.3 slice.376
  628.2 6.5 scatter-add.21
  634.7 9.8 %collective-permute-start.106 = (bf16[32,1344]{1,0:T(8,128)(2,1)}, bf16[32,1344]{1,0:T(8,128)(2,1)}, u32[]{:S(2)}, u32[]{:S(2)}) collective-permute-start(bf16[32,1344]{1,0:T(8,128)(2,1)} %get-tuple-element.220), channel_id=1, source_target_pairs={{0,16},{1,17},{2,18},{3,19},{4,20},{5,21},{6,22},{7,23},{8,24},{9,... | collective-permute-start | bytes 258056 | tf_op jit(solution)/shard_map/ppermute | solution.py:40
  647.2 6.3 scatter-add.24
  661.1 4.7 fusion.45
  665.7 7.9 %convolution_convert_fusion.1 = bf16[1024,3072]{1,0:T(8,128)(2,1)S(1)} fusion(bf16[768,1024]{1,0:T(8,128)(2,1)S(1)} %copy-done.6, f32[1024]{0:T(1024)S(1)} %copy-done.84, f32[768]{0:T(1024)S(1)} %copy-done.88, f32[768]{0:T(1024)S(1)} %copy-done.79, bf16[768,1024]{0,1:T(8,128)(2,1)} %slice.497, bf16[768,1024]{0,1:T(8,128)(2,1)} %get-tuple-element.225, ...), kind=kOutput, calls=%fused_computation.51 | convolution fusion | flops 4853071872 | bytes 12593152 | tf_op jit(solution)/shard_map/dot_general | solution.py:195
  703.4 5.9 multiply_reduce_fusion.5
  711.5 6.6 collective-permute-done.84
  722.0 6.1 collective-permute-done.85
  740.5 5.5 collective-permute-done.92
  (660 shorter events, 337.8 us)
Async XLA Ops:
  2.5 25.8 %collective-permute-start.4 = (bf16[32,1664]{1,0:T(8,128)(2,1)S(1)}, bf16[32,1664]{1,0:T(8,128)(2,1)S(1)}, u32[]{:S(2)}, u32[]{:S(2)}) collective-permute-start(bf16[32,1664]{1,0:T(8,128)(2,1)S(1)} %get-tuple-element.175), channel_id=1, source_target_pairs={{0,8},{1,9},{2,10},{3,11},{4,12},{5,13},{6,14},{7,15},{8,0},{9,1},... | collective-permute-start | bytes 319496 | tf_op jit(solution)/shard_map/ppermute | solution.py:40
  5.6 22.7 %collective-permute-start.5 = (bf16[32,1664]{1,0:T(8,128)(2,1)S(1)}, bf16[32,1664]{1,0:T(8,128)(2,1)S(1)}, u32[]{:S(2)}, u32[]{:S(2)}) collective-permute-start(bf16[32,1664]{1,0:T(8,128)(2,1)S(1)} %get-tuple-element.175), channel_id=1, source_target_pairs={{0,16},{1,17},{2,18},{3,19},{4,20},{5,21},{6,22},{7,23},{8,24},{9,... | collective-permute-start | bytes 319496 | tf_op jit(solution)/shard_map/ppermute | solution.py:40
  8.2 20.1 %collective-permute-start.6 = (bf16[32,1664]{1,0:T(8,128)(2,1)S(1)}, bf16[32,1664]{1,0:T(8,128)(2,1)S(1)}, u32[]{:S(2)}, u32[]{:S(2)}) collective-permute-start(bf16[32,1664]{1,0:T(8,128)(2,1)S(1)} %get-tuple-element.175), channel_id=1, source_target_pairs={{0,24},{1,25},{2,26},{3,27},{4,28},{5,29},{6,30},{7,31},{8,16},{9,... | collective-permute-start | bytes 319496 | tf_op jit(solution)/shard_map/ppermute | solution.py:40
  37.2 53.2 %collective-permute-start.8 = (bf16[4,32,1536]{2,1,0:T(8,128)(2,1)S(1)}, bf16[4,32,1536]{2,1,0:T(8,128)(2,1)S(1)}, u32[]{:S(2)}, u32[]{:S(2)}) collective-permute-start(bf16[4,32,1536]{2,1,0:T(8,128)(2,1)S(1)} %bitcast_dynamic-update-slice_fusion.60), channel_id=1, source_target_pairs={{0,1},{1,0},{2,3},{3,2},{4,5},{5,4},{6,7},{7,6},{8,9},{9,8},{10,11... | collective-permute-start | bytes 1179656 | tf_op jit(solution)/shard_map/ppermute | solution.py:40
  37.2 56.5 %collective-permute-start.10 = (bf16[4,32,1536]{2,1,0:T(8,128)(2,1)S(1)}, bf16[4,32,1536]{2,1,0:T(8,128)(2,1)S(1)}, u32[]{:S(2)}, u32[]{:S(2)}) collective-permute-start(bf16[4,32,1536]{2,1,0:T(8,128)(2,1)S(1)} %bitcast_dynamic-update-slice_fusion.60), channel_id=1, source_target_pairs={{0,4},{1,5},{2,6},{3,7},{4,0},{5,1},{6,2},{7,3},{8,12},{9,13},{10,... | collective-permute-start | bytes 1179656 | tf_op jit(solution)/shard_map/ppermute | solution.py:40
  38.7 53.4 %collective-permute-start.9 = (bf16[4,32,1536]{2,1,0:T(8,128)(2,1)}, bf16[4,32,1536]{2,1,0:T(8,128)(2,1)S(1)}, u32[]{:S(2)}, u32[]{:S(2)}) collective-permute-start(bf16[4,32,1536]{2,1,0:T(8,128)(2,1)} %collective-permute-done.3), channel_id=1, source_target_pairs={{0,1},{1,0},{2,3},{3,2},{4,5},{5,4},{6,7},{7,6},{8,9},{9,8},{10,11... | collective-permute-start | bytes 1179656 | tf_op jit(solution)/shard_map/ppermute | solution.py:40
  39.0 54.8 %collective-permute-start.12 = (bf16[4,32,1536]{2,1,0:T(8,128)(2,1)}, bf16[4,32,1536]{2,1,0:T(8,128)(2,1)S(1)}, u32[]{:S(2)}, u32[]{:S(2)}) collective-permute-start(bf16[4,32,1536]{2,1,0:T(8,128)(2,1)} %collective-permute-done.3), channel_id=1, source_target_pairs={{0,4},{1,5},{2,6},{3,7},{4,0},{5,1},{6,2},{7,3},{8,12},{9,13},{10,... | collective-permute-start | bytes 1179656 | tf_op jit(solution)/shard_map/ppermute | solution.py:40
  90.4 22.2 %collective-permute-start.14 = (bf16[4,32,1664]{2,1,0:T(8,128)(2,1)S(1)}, bf16[4,32,1664]{2,1,0:T(8,128)(2,1)S(1)}, u32[]{:S(2)}, u32[]{:S(2)}) collective-permute-start(bf16[4,32,1664]{2,1,0:T(8,128)(2,1)S(1)} %bitcast_dynamic-update-slice_fusion.56), channel_id=1, source_target_pairs={{0,1},{1,0},{2,3},{3,2},{4,5},{5,4},{6,7},{7,6},{8,9},{9,8},{10,11... | collective-permute-start | bytes 1277960 | tf_op jit(solution)/shard_map/ppermute | solution.py:40
  92.1 19.7 %collective-permute-start.18 = (bf16[4,32,1664]{2,1,0:T(8,128)(2,1)S(1)}, bf16[4,32,1664]{2,1,0:T(8,128)(2,1)S(1)}, u32[]{:S(2)}, u32[]{:S(2)}) collective-permute-start(bf16[4,32,1664]{2,1,0:T(8,128)(2,1)S(1)} %collective-permute-done.7), channel_id=1, source_target_pairs={{0,2},{1,3},{2,0},{3,1},{4,6},{5,7},{6,4},{7,5},{8,10},{9,11},{10,... | collective-permute-start | bytes 1277960 | tf_op jit(solution)/shard_map/ppermute | solution.py:40
  93.7 18.2 %collective-permute-start.11 = (bf16[4,32,1536]{2,1,0:T(8,128)(2,1)S(1)}, bf16[4,32,1536]{2,1,0:T(8,128)(2,1)S(1)}, u32[]{:S(2)}, u32[]{:S(2)}) collective-permute-start(bf16[4,32,1536]{2,1,0:T(8,128)(2,1)S(1)} %collective-permute-done.10), channel_id=1, source_target_pairs={{0,1},{1,0},{2,3},{3,2},{4,5},{5,4},{6,7},{7,6},{8,9},{9,8},{10,11... | collective-permute-start | bytes 1179656 | tf_op jit(solution)/shard_map/ppermute | solution.py:40
  93.8 18.9 %collective-permute-start.15 = (bf16[4,32,1664]{2,1,0:T(8,128)(2,1)S(1)}, bf16[4,32,1664]{2,1,0:T(8,128)(2,1)S(1)}, u32[]{:S(2)}, u32[]{:S(2)}) collective-permute-start(bf16[4,32,1664]{2,1,0:T(8,128)(2,1)S(1)} %collective-permute-done.7), channel_id=1, source_target_pairs={{0,1},{1,0},{2,3},{3,2},{4,5},{5,4},{6,7},{7,6},{8,9},{9,8},{10,11... | collective-permute-start | bytes 1277960 | tf_op jit(solution)/shard_map/ppermute | solution.py:40
  157.8 29.6 %collective-permute-start.28 = (bf16[4,32,3200]{2,1,0:T(8,128)(2,1)}, bf16[4,32,3200]{2,1,0:T(8,128)(2,1)S(1)}, u32[]{:S(2)}, u32[]{:S(2)}) collective-permute-start(bf16[4,32,3200]{2,1,0:T(8,128)(2,1)} %copy-done.36), channel_id=1, source_target_pairs={{0,4},{1,5},{2,6},{3,7},{4,0},{5,1},{6,2},{7,3},{8,12},{9,13},{10,... | collective-permute-start | bytes 2457608 | tf_op jit(solution)/shard_map/ppermute | solution.py:40
  161.8 25.7 %collective-permute-start.27 = (bf16[4,32,3072]{2,1,0:T(8,128)(2,1)}, bf16[4,32,3072]{2,1,0:T(8,128)(2,1)}, u32[]{:S(2)}, u32[]{:S(2)}) collective-permute-start(bf16[4,32,3072]{2,1,0:T(8,128)(2,1)} %copy-done.40), channel_id=1, source_target_pairs={{0,2},{1,3},{2,0},{3,1},{4,6},{5,7},{6,4},{7,5},{8,10},{9,11},{10,... | collective-permute-start | bytes 2359304 | tf_op jit(solution)/shard_map/ppermute | solution.py:40
  187.5 38.7 %collective-permute-start.46 = (bf16[32,1344]{1,0:T(8,128)(2,1)S(1)}, bf16[32,1344]{1,0:T(8,128)(2,1)S(1)}, u32[]{:S(2)}, u32[]{:S(2)}) collective-permute-start(bf16[32,1344]{1,0:T(8,128)(2,1)S(1)} %slice.357), channel_id=1, source_target_pairs={{0,8},{1,9},{2,10},{3,11},{4,12},{5,13},{6,14},{7,15},{8,0},{9,1},... | collective-permute-start | bytes 258056 | tf_op jit(solution)/shard_map/ppermute | solution.py:40
  188.9 37.2 %collective-permute-start.47 = (bf16[32,1344]{1,0:T(8,128)(2,1)S(1)}, bf16[32,1344]{1,0:T(8,128)(2,1)S(1)}, u32[]{:S(2)}, u32[]{:S(2)}) collective-permute-start(bf16[32,1344]{1,0:T(8,128)(2,1)S(1)} %slice.357), channel_id=1, source_target_pairs={{0,16},{1,17},{2,18},{3,19},{4,20},{5,21},{6,22},{7,23},{8,24},{9,... | collective-permute-start | bytes 258056 | tf_op jit(solution)/shard_map/ppermute | solution.py:40
  189.8 36.4 %collective-permute-start.48 = (bf16[32,1344]{1,0:T(8,128)(2,1)S(1)}, bf16[32,1344]{1,0:T(8,128)(2,1)S(1)}, u32[]{:S(2)}, u32[]{:S(2)}) collective-permute-start(bf16[32,1344]{1,0:T(8,128)(2,1)S(1)} %slice.357), channel_id=1, source_target_pairs={{0,24},{1,25},{2,26},{3,27},{4,28},{5,29},{6,30},{7,31},{8,16},{9,... | collective-permute-start | bytes 258056 | tf_op jit(solution)/shard_map/ppermute | solution.py:40
  191.9 25.1 %collective-permute-start.42 = (bf16[32,1280]{1,0:T(8,128)(2,1)S(1)}, bf16[32,1280]{1,0:T(8,128)(2,1)}, u32[]{:S(2)}, u32[]{:S(2)}) collective-permute-start(bf16[32,1280]{1,0:T(8,128)(2,1)S(1)} %slice.356), channel_id=1, source_target_pairs={{0,8},{1,9},{2,10},{3,11},{4,12},{5,13},{6,14},{7,15},{8,0},{9,1},... | collective-permute-start | bytes 245768 | tf_op jit(solution)/shard_map/ppermute | solution.py:40
  192.4 28.3 %collective-permute-start.43 = (bf16[32,1280]{1,0:T(8,128)(2,1)S(1)}, bf16[32,1280]{1,0:T(8,128)(2,1)S(1)}, u32[]{:S(2)}, u32[]{:S(2)}) collective-permute-start(bf16[32,1280]{1,0:T(8,128)(2,1)S(1)} %slice.356), channel_id=1, source_target_pairs={{0,16},{1,17},{2,18},{3,19},{4,20},{5,21},{6,22},{7,23},{8,24},{9,... | collective-permute-start | bytes 245768 | tf_op jit(solution)/shard_map/ppermute | solution.py:40
  223.3 20.6 %collective-permute-start.32 = (bf16[4,32,3072]{2,1,0:T(8,128)(2,1)S(1)}, bf16[4,32,3072]{2,1,0:T(8,128)(2,1)S(1)}, u32[]{:S(2)}, u32[]{:S(2)}) collective-permute-start(bf16[4,32,3072]{2,1,0:T(8,128)(2,1)S(1)} %copy-done.41), channel_id=1, source_target_pairs={{0,4},{1,5},{2,6},{3,7},{4,0},{5,1},{6,2},{7,3},{8,12},{9,13},{10,... | collective-permute-start | bytes 2359304 | tf_op jit(solution)/shard_map/ppermute | solution.py:40
  226.2 33.8 %collective-permute-start.34 = (bf16[4,32,3072]{2,1,0:T(8,128)(2,1)}, bf16[4,32,3072]{2,1,0:T(8,128)(2,1)S(1)}, u32[]{:S(2)}, u32[]{:S(2)}) collective-permute-start(bf16[4,32,3072]{2,1,0:T(8,128)(2,1)} %collective-permute-done.27), channel_id=1, source_target_pairs={{0,4},{1,5},{2,6},{3,7},{4,0},{5,1},{6,2},{7,3},{8,12},{9,13},{10,... | collective-permute-start | bytes 2359304 | tf_op jit(solution)/shard_map/ppermute | solution.py:40
  226.3 39.9 %collective-permute-start.36 = (bf16[4,32,3200]{2,1,0:T(8,128)(2,1)S(1)}, bf16[4,32,3200]{2,1,0:T(8,128)(2,1)S(1)}, u32[]{:S(2)}, u32[]{:S(2)}) collective-permute-start(bf16[4,32,3200]{2,1,0:T(8,128)(2,1)S(1)} %copy-done.37), channel_id=1, source_target_pairs={{0,1},{1,0},{2,3},{3,2},{4,5},{5,4},{6,7},{7,6},{8,9},{9,8},{10,11... | collective-permute-start | bytes 2457608 | tf_op jit(solution)/shard_map/ppermute | solution.py:40
  226.9 41.1 %collective-permute-start.38 = (bf16[4,32,3200]{2,1,0:T(8,128)(2,1)S(1)}, bf16[4,32,3200]{2,1,0:T(8,128)(2,1)S(1)}, u32[]{:S(2)}, u32[]{:S(2)}) collective-permute-start(bf16[4,32,3200]{2,1,0:T(8,128)(2,1)S(1)} %copy-done.37), channel_id=1, source_target_pairs={{0,2},{1,3},{2,0},{3,1},{4,6},{5,7},{6,4},{7,5},{8,10},{9,11},{10,... | collective-permute-start | bytes 2457608 | tf_op jit(solution)/shard_map/ppermute | solution.py:40
  230.8 52.3 %collective-permute-start.37 = (bf16[4,32,3200]{2,1,0:T(8,128)(2,1)S(1)}, bf16[4,32,3200]{2,1,0:T(8,128)(2,1)S(1)}, u32[]{:S(2)}, u32[]{:S(2)}) collective-permute-start(bf16[4,32,3200]{2,1,0:T(8,128)(2,1)S(1)} %copy-done.66), channel_id=1, source_target_pairs={{0,1},{1,0},{2,3},{3,2},{4,5},{5,4},{6,7},{7,6},{8,9},{9,8},{10,11... | collective-permute-start | bytes 2457608 | tf_op jit(solution)/shard_map/ppermute | solution.py:40
  259.9 21.2 %collective-permute-start.40 = (bf16[4,32,3200]{2,1,0:T(8,128)(2,1)S(1)}, bf16[4,32,3200]{2,1,0:T(8,128)(2,1)S(1)}, u32[]{:S(2)}, u32[]{:S(2)}) collective-permute-start(bf16[4,32,3200]{2,1,0:T(8,128)(2,1)S(1)} %copy-done.66), channel_id=1, source_target_pairs={{0,2},{1,3},{2,0},{3,1},{4,6},{5,7},{6,4},{7,5},{8,10},{9,11},{10,... | collective-permute-start | bytes 2457608 | tf_op jit(solution)/shard_map/ppermute | solution.py:40
  262.2 29.3 %collective-permute-start.45 = (bf16[4,32,1280]{2,1,0:T(8,128)(2,1)}, bf16[4,32,1280]{2,1,0:T(8,128)(2,1)}, u32[]{:S(2)}, u32[]{:S(2)}) collective-permute-start(bf16[4,32,1280]{2,1,0:T(8,128)(2,1)} %bitcast_dynamic-update-slice_fusion.68), channel_id=1, source_target_pairs={{0,2},{1,3},{2,0},{3,1},{4,6},{5,7},{6,4},{7,5},{8,10},{9,11},{10,... | collective-permute-start | bytes 983048 | tf_op jit(solution)/shard_map/ppermute | solution.py:40
  266.2 25.4 %collective-permute-start.49 = (bf16[4,32,1344]{2,1,0:T(8,128)(2,1)S(1)}, bf16[4,32,1344]{2,1,0:T(8,128)(2,1)S(1)}, u32[]{:S(2)}, u32[]{:S(2)}) collective-permute-start(bf16[4,32,1344]{2,1,0:T(8,128)(2,1)S(1)} %bitcast_dynamic-update-slice_fusion.64), channel_id=1, source_target_pairs={{0,4},{1,5},{2,6},{3,7},{4,0},{5,1},{6,2},{7,3},{8,12},{9,13},{10,... | collective-permute-start | bytes 1032200 | tf_op jit(solution)/shard_map/ppermute | solution.py:40
  268.0 17.1 %collective-permute-start.39 = (bf16[4,32,3200]{2,1,0:T(8,128)(2,1)S(1)}, bf16[4,32,3200]{2,1,0:T(8,128)(2,1)S(1)}, u32[]{:S(2)}, u32[]{:S(2)}) collective-permute-start(bf16[4,32,3200]{2,1,0:T(8,128)(2,1)S(1)} %collective-permute-done.38), channel_id=1, source_target_pairs={{0,1},{1,0},{2,3},{3,2},{4,5},{5,4},{6,7},{7,6},{8,9},{9,8},{10,11... | collective-permute-start | bytes 2457608 | tf_op jit(solution)/shard_map/ppermute | solution.py:40
  291.6 21.5 %collective-permute-start.50 = (bf16[4,32,1280]{2,1,0:T(8,128)(2,1)}, bf16[4,32,1280]{2,1,0:T(8,128)(2,1)}, u32[]{:S(2)}, u32[]{:S(2)}) collective-permute-start(bf16[4,32,1280]{2,1,0:T(8,128)(2,1)} %bitcast_dynamic-update-slice_fusion.68), channel_id=1, source_target_pairs={{0,1},{1,0},{2,3},{3,2},{4,5},{5,4},{6,7},{7,6},{8,9},{9,8},{10,11... | collective-permute-start | bytes 983048 | tf_op jit(solution)/shard_map/ppermute | solution.py:40
  292.2 25.7 %collective-permute-start.52 = (bf16[4,32,1280]{2,1,0:T(8,128)(2,1)}, bf16[4,32,1280]{2,1,0:T(8,128)(2,1)}, u32[]{:S(2)}, u32[]{:S(2)}) collective-permute-start(bf16[4,32,1280]{2,1,0:T(8,128)(2,1)} %bitcast_dynamic-update-slice_fusion.68), channel_id=1, source_target_pairs={{0,4},{1,5},{2,6},{3,7},{4,0},{5,1},{6,2},{7,3},{8,12},{9,13},{10,... | collective-permute-start | bytes 983048 | tf_op jit(solution)/shard_map/ppermute | solution.py:40
  293.9 22.1 %collective-permute-start.51 = (bf16[4,32,1280]{2,1,0:T(8,128)(2,1)}, bf16[4,32,1280]{2,1,0:T(8,128)(2,1)}, u32[]{:S(2)}, u32[]{:S(2)}) collective-permute-start(bf16[4,32,1280]{2,1,0:T(8,128)(2,1)} %collective-permute-done.45), channel_id=1, source_target_pairs={{0,1},{1,0},{2,3},{3,2},{4,5},{5,4},{6,7},{7,6},{8,9},{9,8},{10,11... | collective-permute-start | bytes 983048 | tf_op jit(solution)/shard_map/ppermute | solution.py:40
  293.9 26.1 %collective-permute-start.54 = (bf16[4,32,1280]{2,1,0:T(8,128)(2,1)}, bf16[4,32,1280]{2,1,0:T(8,128)(2,1)}, u32[]{:S(2)}, u32[]{:S(2)}) collective-permute-start(bf16[4,32,1280]{2,1,0:T(8,128)(2,1)} %collective-permute-done.45), channel_id=1, source_target_pairs={{0,4},{1,5},{2,6},{3,7},{4,0},{5,1},{6,2},{7,3},{8,12},{9,13},{10,... | collective-permute-start | bytes 983048 | tf_op jit(solution)/shard_map/ppermute | solution.py:40
  294.2 38.9 %collective-permute-start.56 = (bf16[4,32,1344]{2,1,0:T(8,128)(2,1)S(1)}, bf16[4,32,1344]{2,1,0:T(8,128)(2,1)}, u32[]{:S(2)}, u32[]{:S(2)}) collective-permute-start(bf16[4,32,1344]{2,1,0:T(8,128)(2,1)S(1)} %bitcast_dynamic-update-slice_fusion.64), channel_id=1, source_target_pairs={{0,1},{1,0},{2,3},{3,2},{4,5},{5,4},{6,7},{7,6},{8,9},{9,8},{10,11... | collective-permute-start | bytes 1032200 | tf_op jit(solution)/shard_map/ppermute | solution.py:40
  429.0 24.2 %collective-permute-start.63 = (bf16[16,1,32,5248]{3,2,0,1:T(8,128)(2,1)}, bf16[16,1,32,5248]{3,2,0,1:T(8,128)(2,1)}, u32[]{:S(2)}, u32[]{:S(2)}) collective-permute-start(bf16[16,1,32,5248]{3,2,0,1:T(8,128)(2,1)} %dynamic-slice_bitcast_fusion), channel_id=1, source_target_pairs={{0,1},{1,0},{2,3},{3,2},{4,5},{5,4},{6,7},{7,6},{8,9},{9,8},{10,11... | collective-permute-start | bytes 16121864 | tf_op jit(solution)/shard_map/ppermute | solution.py:40
  434.8 18.1 %collective-permute-start.65 = (bf16[4,2,32,1344]{3,2,1,0:T(8,128)(2,1)S(1)}, bf16[4,2,32,1344]{3,2,1,0:T(8,128)(2,1)S(1)}, u32[]{:S(2)}, u32[]{:S(2)}) collective-permute-start(bf16[4,2,32,1344]{3,2,1,0:T(8,128)(2,1)S(1)} %dynamic-slice_bitcast_fusion.7), channel_id=1, source_target_pairs={{0,2},{1,3},{2,0},{3,1},{4,6},{5,7},{6,4},{7,5},{8,10},{9,11},{10,... | collective-permute-start | bytes 2064392 | tf_op jit(solution)/shard_map/ppermute | solution.py:40
  459.4 24.4 %collective-permute-start.69 = (bf16[4,32,1344]{2,1,0:T(8,128)(2,1)S(1)}, bf16[4,32,1344]{2,1,0:T(8,128)(2,1)S(1)}, u32[]{:S(2)}, u32[]{:S(2)}) collective-permute-start(bf16[4,32,1344]{2,1,0:T(8,128)(2,1)S(1)} %dynamic-slice_bitcast_fusion.13), channel_id=1, source_target_pairs={{0,4},{1,5},{2,6},{3,7},{4,0},{5,1},{6,2},{7,3},{8,12},{9,13},{10,... | collective-permute-start | bytes 1032200 | tf_op jit(solution)/shard_map/ppermute | solution.py:40
  461.1 21.8 %collective-permute-start.68 = (bf16[4,32,1280]{2,1,0:T(8,128)(2,1)S(1)}, bf16[4,32,1280]{2,1,0:T(8,128)(2,1)S(1)}, u32[]{:S(2)}, u32[]{:S(2)}) collective-permute-start(bf16[4,32,1280]{2,1,0:T(8,128)(2,1)S(1)} %dynamic-slice_bitcast_fusion.14), channel_id=1, source_target_pairs={{0,2},{1,3},{2,0},{3,1},{4,6},{5,7},{6,4},{7,5},{8,10},{9,11},{10,... | collective-permute-start | bytes 983048 | tf_op jit(solution)/shard_map/ppermute | solution.py:40
  463.1 36.2 %collective-permute-start.67 = (bf16[4,2,32,2688]{3,2,1,0:T(8,128)(2,1)}, bf16[4,2,32,2688]{3,2,1,0:T(8,128)(2,1)}, u32[]{:S(2)}, u32[]{:S(2)}) collective-permute-start(bf16[4,2,32,2688]{3,2,1,0:T(8,128)(2,1)} %dynamic-slice_bitcast_fusion.2), channel_id=1, source_target_pairs={{0,2},{1,3},{2,0},{3,1},{4,6},{5,7},{6,4},{7,5},{8,10},{9,11},{10,... | collective-permute-start | bytes 4128776 | tf_op jit(solution)/shard_map/ppermute | solution.py:40
  465.6 31.5 %collective-permute-start.66 = (bf16[4,2,32,2560]{3,2,0,1:T(8,128)(2,1)}, bf16[4,2,32,2560]{3,2,0,1:T(8,128)(2,1)}, u32[]{:S(2)}, u32[]{:S(2)}) collective-permute-start(bf16[4,2,32,2560]{3,2,0,1:T(8,128)(2,1)} %dynamic-slice_bitcast_fusion.3), channel_id=1, source_target_pairs={{0,4},{1,5},{2,6},{3,7},{4,0},{5,1},{6,2},{7,3},{8,12},{9,13},{10,... | collective-permute-start | bytes 3932168 | tf_op jit(solution)/shard_map/ppermute | solution.py:40
  522.0 152.0 %collective-permute-start.102 = (bf16[32,1280]{1,0:T(8,128)(2,1)}, bf16[32,1280]{1,0:T(8,128)(2,1)}, u32[]{:S(2)}, u32[]{:S(2)}) collective-permute-start(bf16[32,1280]{1,0:T(8,128)(2,1)} %get-tuple-element.221), channel_id=1, source_target_pairs={{0,8},{1,9},{2,10},{3,11},{4,12},{5,13},{6,14},{7,15},{8,0},{9,1},... | collective-permute-start | bytes 245768 | tf_op jit(solution)/shard_map/ppermute | solution.py:40
  522.0 154.3 %collective-permute-start.103 = (bf16[32,1280]{1,0:T(8,128)(2,1)}, bf16[32,1280]{1,0:T(8,128)(2,1)}, u32[]{:S(2)}, u32[]{:S(2)}) collective-permute-start(bf16[32,1280]{1,0:T(8,128)(2,1)} %get-tuple-element.223), channel_id=1, source_target_pairs={{0,16},{1,17},{2,18},{3,19},{4,20},{5,21},{6,22},{7,23},{8,24},{9,... | collective-permute-start | bytes 245768 | tf_op jit(solution)/shard_map/ppermute | solution.py:40
  525.2 20.8 %collective-permute-start.72 = (bf16[16,1,32,1024]{3,2,0,1:T(8,128)(2,1)S(1)}, bf16[16,1,32,1024]{3,2,0,1:T(8,128)(2,1)S(1)}, u32[]{:S(2)}, u32[]{:S(2)}) collective-permute-start(bf16[16,1,32,1024]{3,2,0,1:T(8,128)(2,1)S(1)} %dynamic-slice_bitcast_fusion.4), channel_id=1, source_target_pairs={{0,1},{1,0},{2,3},{3,2},{4,5},{5,4},{6,7},{7,6},{8,9},{9,8},{10,11... | collective-permute-start | bytes 3145736 | tf_op jit(solution)/shard_map/ppermute | solution.py:40
  525.4 19.6 %collective-permute-start.71 = (bf16[4,32,2688]{2,1,0:T(8,128)(2,1)S(1)}, bf16[4,32,2688]{2,1,0:T(8,128)(2,1)S(1)}, u32[]{:S(2)}, u32[]{:S(2)}) collective-permute-start(bf16[4,32,2688]{2,1,0:T(8,128)(2,1)S(1)} %dynamic-slice_bitcast_fusion.8), channel_id=1, source_target_pairs={{0,4},{1,5},{2,6},{3,7},{4,0},{5,1},{6,2},{7,3},{8,12},{9,13},{10,... | collective-permute-start | bytes 2064392 | tf_op jit(solution)/shard_map/ppermute | solution.py:40
  527.1 16.9 %collective-permute-start.70 = (bf16[4,32,2560]{2,1,0:T(8,128)(2,1)S(1)}, bf16[4,32,2560]{2,1,0:T(8,128)(2,1)S(1)}, u32[]{:S(2)}, u32[]{:S(2)}) collective-permute-start(bf16[4,32,2560]{2,1,0:T(8,128)(2,1)S(1)} %dynamic-slice_bitcast_fusion.9), channel_id=1, source_target_pairs={{0,2},{1,3},{2,0},{3,1},{4,6},{5,7},{6,4},{7,5},{8,10},{9,11},{10,... | collective-permute-start | bytes 1966088 | tf_op jit(solution)/shard_map/ppermute | solution.py:40
  596.9 79.4 %collective-permute-start.104 = (bf16[32,1280]{1,0:T(8,128)(2,1)}, bf16[32,1280]{1,0:T(8,128)(2,1)}, u32[]{:S(2)}, u32[]{:S(2)}) collective-permute-start(bf16[32,1280]{1,0:T(8,128)(2,1)} %get-tuple-element.222), channel_id=1, source_target_pairs={{0,24},{1,25},{2,26},{3,27},{4,28},{5,29},{6,30},{7,31},{8,16},{9,... | collective-permute-start | bytes 245768 | tf_op jit(solution)/shard_map/ppermute | solution.py:40
  616.2 61.3 %collective-permute-start.105 = (bf16[32,1344]{1,0:T(8,128)(2,1)}, bf16[32,1344]{1,0:T(8,128)(2,1)}, u32[]{:S(2)}, u32[]{:S(2)}) collective-permute-start(bf16[32,1344]{1,0:T(8,128)(2,1)} %get-tuple-element.218), channel_id=1, source_target_pairs={{0,8},{1,9},{2,10},{3,11},{4,12},{5,13},{6,14},{7,15},{8,0},{9,1},... | collective-permute-start | bytes 258056 | tf_op jit(solution)/shard_map/ppermute | solution.py:40
  634.7 42.8 %collective-permute-start.106 = (bf16[32,1344]{1,0:T(8,128)(2,1)}, bf16[32,1344]{1,0:T(8,128)(2,1)}, u32[]{:S(2)}, u32[]{:S(2)}) collective-permute-start(bf16[32,1344]{1,0:T(8,128)(2,1)} %get-tuple-element.220), channel_id=1, source_target_pairs={{0,16},{1,17},{2,18},{3,19},{4,20},{5,21},{6,22},{7,23},{8,24},{9,... | collective-permute-start | bytes 258056 | tf_op jit(solution)/shard_map/ppermute | solution.py:40
  676.4 23.8 %collective-permute-start.83 = (bf16[16,1,32,3072]{3,2,0,1:T(8,128)(2,1)S(1)}, bf16[16,1,32,3072]{3,2,0,1:T(8,128)(2,1)S(1)}, u32[]{:S(2)}, u32[]{:S(2)}) collective-permute-start(bf16[16,1,32,3072]{3,2,0,1:T(8,128)(2,1)S(1)} %dynamic-slice_bitcast_fusion.1), channel_id=1, source_target_pairs={{0,1},{1,0},{2,3},{3,2},{4,5},{5,4},{6,7},{7,6},{8,9},{9,8},{10,11... | collective-permute-start | bytes 9437192 | tf_op jit(solution)/shard_map/ppermute | solution.py:40
  702.1 19.5 %collective-permute-start.89 = (bf16[4,2,32,1536]{3,2,1,0:T(8,128)(2,1)S(1)}, bf16[4,2,32,1536]{3,2,1,0:T(8,128)(2,1)S(1)}, u32[]{:S(2)}, u32[]{:S(2)}) collective-permute-start(bf16[4,2,32,1536]{3,2,1,0:T(8,128)(2,1)S(1)} %dynamic-slice_bitcast_fusion.5), channel_id=1, source_target_pairs={{0,2},{1,3},{2,0},{3,1},{4,6},{5,7},{6,4},{7,5},{8,10},{9,11},{10,... | collective-permute-start | bytes 2359304 | tf_op jit(solution)/shard_map/ppermute | solution.py:40
  (170 other events, 2850.2 us)

commit v3 on v2

--- a/solution.py
+++ b/solution.py
@@ -246,7 +246,7 @@
     normed_attn, inv_attn = layer_norm(inputs)
     h_attn = (normed_attn * full_gain_attn.astype(jnp.float32)).astype(jnp.bfloat16)
     projected = jnp.dot(h_attn, full_qkv, preferred_element_type=jnp.float32)
-    projected, second_set = tie(projected, second_set)
+    _, second_set = tie(projected[:8, :128], second_set)
     projected = projected.reshape(tok_rows, 3, head_count, HDIM)
     second_set = gather_near(second_set, 0)
     queries = apply_rope(projected[:, 0], cosine, sine_table).astype(jnp.bfloat16)

time: 758 us -> 743 us (0.980)
  waiting for transfers between devices: 221 us -> 212 us
    optimization_barrier x5 -> x4, local copies, waits for them, and re-layouts: 11.9 us -> 2.3 us  [tie(): return lax.optimization_barrier(values)]
    squeeze x1, local copies, waits for them, and re-layouts: 4.12 us -> 13.3 us  [local(): projected[:, 0]]
    ppermute x104, waiting for transfers between devices: 221 us -> 212 us  [swapped(): return lax.ppermute(value, 'dev', [(i, i ^ mask) for i in range(count)])]
    unnamed x224 -> x232, local copies, waits for them, and re-layouts: 21.9 us -> 18.3 us
  transfers between devices with their start and end apart: 108 -> 108, of which waited for: 44 -> 42; matrix products, arithmetic and copies ran while one was open for 33% -> 38% of each run, Pallas kernels for 0% -> 0%
where the time goes in v3:
time: 743 us; the launch traced here: 738 us
  waiting for transfers between devices  212 us (29%)
  matrix products  169 us (23%)
  local copies, waits for them, and re-layouts  135 us (18%)
  other arithmetic  109 us (15%)
  starting transfers between devices  109 us (15%)
    ppermute x104, waiting for transfers between devices, swapped(): return lax.ppermute(value, 'dev', [(i, i ^ mask) for i in range(count)])  212 us
    ppermute x104, starting transfers between devices, swapped(): return lax.ppermute(value, 'dev', [(i, i ^ mask) for i in range(count)])  103 us
    dot_general x4, matrix products, contract_cols(): lax.dot_general(first_mat, second_mat, (((1,), (1,)), ((), ())), preferre...  31.9 us
    dot_general x4, matrix products, contract_rows(): lax.dot_general(first_mat, second_mat, (((0,), (0,)), ((), ())), preferre...  30.7 us
    dot_general x1, matrix products, local(): jnp.dot(cotangent, down_rows, preferred_element_type=jnp.float32)  26.7 us
    dynamic_update_slice x48, local copies, waits for them, and re-layouts, gather_last(): lax.dynamic_update_slice(full, block[:, None, None, None], (0, spot[4], s...  25.8 us
    another operation x4, other arithmetic  21.8 us
    dot_general x3, matrix products, local(): jnp.einsum('qhd,khd->hqk', grad_tile, value_tile, preferred_element_type=...  18.4 us
  transfers between devices with their start and end apart: 108, of which 42 were waited for; matrix products, arithmetic and copies ran while one was open for 38% of the time, Pallas kernels for 0%

profile of v3, /device:TPU:0, one launch (start us, length us, event | category | flops | bytes accessed | tf_op | source)
XLA Modules:
  0.0 737.5 jit_solution(480062896890523540)
XLA Ops:
  22.1 6.3 collective-permute-done.2
  43.0 5.4 collective-permute-done.21
  48.4 11.0 %collective-permute-done.22 = bf16[32,3072]{1,0:T(8,128)(2,1)S(1)} collective-permute-done((bf16[32,3072]{1,0:T(8,128)(2,1)S(1)}, bf16[32,3072]{1,0:T(8,128)(2,1)S(1)}, u32[]{:S(2)}, u32[]{:S(2)}) %collective-permute-start.22) | collective-permute-done | bytes 196640 | tf_op jit(solution)/shard_map/ppermute | solution.py:40
  59.8 8.3 %collective-permute-done.23 = bf16[32,3072]{1,0:T(8,128)(2,1)S(1)} collective-permute-done((bf16[32,3072]{1,0:T(8,128)(2,1)S(1)}, bf16[32,3072]{1,0:T(8,128)(2,1)S(1)}, u32[]{:S(2)}, u32[]{:S(2)}) %collective-permute-start.23) | collective-permute-done | bytes 196640 | tf_op jit(solution)/shard_map/ppermute | solution.py:40
  68.8 5.6 collective-permute-done.24
  76.4 8.1 %collective-permute-done.25 = bf16[32,3200]{1,0:T(8,128)(2,1)S(1)} collective-permute-done((bf16[32,3200]{1,0:T(8,128)(2,1)}, bf16[32,3200]{1,0:T(8,128)(2,1)S(1)}, u32[]{:S(2)}, u32[]{:S(2)}) %collective-permute-start.25) | collective-permute-done | bytes 204832 | tf_op jit(solution)/shard_map/ppermute | solution.py:40
  89.0 8.3 %collective-permute-done.16 = bf16[4,32,1664]{2,1,0:T(8,128)(2,1)S(1)} collective-permute-done((bf16[4,32,1664]{2,1,0:T(8,128)(2,1)S(1)}, bf16[4,32,1664]{2,1,0:T(8,128)(2,1)S(1)}, u32[]{:S(2)}, u32[]{:S(2)}) %collective-permute-start.16) | collective-permute-done | bytes 426016 | tf_op jit(solution)/shard_map/ppermute | solution.py:40
  99.7 6.3 collective-permute-done.18
  108.8 5.9 fusion.17
  114.7 13.3 %slice_bitcast_fusion = (f32[768,16,64]{0,2,1:T(8,128)S(1)}, f32[768,16,64]{0,2,1:T(8,128)}, f32[768,1,16,64]{0,3,2,1:T(8,128)S(1)}) fusion(f32[768,3,16,64]{0,3,2,1:T(8,128)S(1)} %bitcast.546), kind=kLoop, calls=%fused_computation.95 | loop fusion | bytes 15728640 | tf_op jit(solution)/shard_map/squeeze | solution.py:252
  145.4 4.7 collective-permute-start.28
  150.1 7.3 pad_maximum_fusion.6
  164.4 10.5 %collective-permute-done.27 = bf16[4,32,3072]{2,1,0:T(8,128)(2,1)S(1)} collective-permute-done((bf16[4,32,3072]{2,1,0:T(8,128)(2,1)S(1)}, bf16[4,32,3072]{2,1,0:T(8,128)(2,1)S(1)}, u32[]{:S(2)}, u32[]{:S(2)}) %collective-permute-start.27) | collective-permute-done | bytes 786464 | tf_op jit(solution)/shard_map/ppermute | solution.py:40
  186.8 4.2 fusion.78
  198.0 5.9 broadcast_in_dim.381
  223.6 10.3 %collective-permute-done.32 = bf16[4,32,3072]{2,1,0:T(8,128)(2,1)S(1)} collective-permute-done((bf16[4,32,3072]{2,1,0:T(8,128)(2,1)S(1)}, bf16[4,32,3072]{2,1,0:T(8,128)(2,1)S(1)}, u32[]{:S(2)}, u32[]{:S(2)}) %collective-permute-start.32) | collective-permute-done | bytes 786464 | tf_op jit(solution)/shard_map/ppermute | solution.py:40
  235.8 14.4 %collective-permute-done.34 = bf16[4,32,3072]{2,1,0:T(8,128)(2,1)S(1)} collective-permute-done((bf16[4,32,3072]{2,1,0:T(8,128)(2,1)}, bf16[4,32,3072]{2,1,0:T(8,128)(2,1)S(1)}, u32[]{:S(2)}, u32[]{:S(2)}) %collective-permute-start.34) | collective-permute-done | bytes 786464 | tf_op jit(solution)/shard_map/ppermute | solution.py:40
  258.2 13.2 %collective-permute-done.40 = bf16[4,32,3200]{2,1,0:T(8,128)(2,1)S(1)} collective-permute-done((bf16[4,32,3200]{2,1,0:T(8,128)(2,1)S(1)}, bf16[4,32,3200]{2,1,0:T(8,128)(2,1)S(1)}, u32[]{:S(2)}, u32[]{:S(2)}) %collective-permute-start.40) | collective-permute-done | bytes 819232 | tf_op jit(solution)/shard_map/ppermute | solution.py:40
  285.6 15.9 %fusion.2 = f32[768,5248]{1,0:T(8,128)} fusion(bf16[1024,6272]{1,0:T(8,128)(2,1)} %bitcast.558, f32[768,1024]{1,0:T(8,128)S(1)} %get-tuple-element.171, f32[1024]{0:T(1024)S(1)} %get-tuple-element.158, f32[768]{0:T(1024)S(1)} %add_rsqrt_fusion, f32[768]{0:T(1024)S(1)} %broadcast_multiply_fusion.6), kind=kOutput, calls=%fused_computation.5 | convolution fusion | flops 8257536000 | bytes 30025728 | tf_op jit(solution)/shard_map/dot_general | solution.py:313
  314.7 7.1 collective-permute-done.60
  324.8 26.7 %add_convert_fusion.1 = (bf16[768,2624]{1,0:T(8,128)(2,1)}, f32[768,2624]{1,0:T(8,128)}, f32[2624,768]{0,1:T(8,128)}) fusion(f32[768,5248]{1,0:T(8,128)S(1)} %copy-done.7, bf16[768,1024]{1,0:T(8,128)(2,1)} %param.29, bf16[1024,2624]{1,0:T(8,128)(2,1)S(1)} %bitcast.592), kind=kOutput, calls=%fused_computation.11 | convolution fusion | flops 4274307072 | bytes 43220992 | tf_op jit(solution)/shard_map/dot_general | solution.py:321
  351.6 13.9 %fusion.5 = (bf16[768,2624]{1,0:T(8,128)(2,1)}, bf16[768,2624]{1,0:T(8,128)(2,1)S(1)}) fusion(f32[2624,768]{0,1:T(8,128)} %get-tuple-element.250, f32[768,2624]{1,0:T(8,128)} %get-tuple-element.169, f32[768,5248]{1,0:T(8,128)} %fusion.2), kind=kLoop, calls=%fused_computation.10 | loop fusion | flops 12091392 | bytes 40304640 | tf_op jit(solution)/shard_map/convert.33
  367.5 6.3 fusion.19
  373.8 8.1 %copy.74 = bf16[1024,2624]{1,0:T(8,128)(2,1)} copy(bf16[1024,2624]{0,1:T(8,128)(2,1)} %fusion.19) | data formatting | bytes 10747904 | tf_op jit(solution)/shard_map/convert_element_type | solution.py:105
  385.4 8.7 %pad_maximum_fusion = bf16[768,5248]{1,0:T(8,128)(2,1)} fusion(bf16[768,2624]{1,0:T(8,128)(2,1)} %get-tuple-element.174, bf16[768,2624]{1,0:T(8,128)(2,1)} %get-tuple-element.168), kind=kLoop, calls=%fused_computation.26 | loop fusion | flops 16121856 | bytes 16121856 | tf_op jit(solution)/shard_map/concatenate | solution.py:324
  399.9 13.5 %convolution_convert_fusion = bf16[1024,5248]{1,0:T(8,128)(2,1)S(1)} fusion(bf16[768,5248]{1,0:T(8,128)(2,1)} %pad_maximum_fusion, f32[768,1024]{1,0:T(8,128)S(1)} %get-tuple-element.171, f32[1024]{0:T(1024)S(1)} %get-tuple-element.158, f32[768]{0:T(1024)S(1)} %add_rsqrt_fusion, f32[768]{0:T(1024)S(1)} %broadcast_multiply_fusion.6), kind=kOutput, calls=%fused_computation.1 | convolution fusion | flops 8262909952 | bytes 21964800 | tf_op jit(solution)/shard_map/dot_general | solution.py:195
  419.6 5.1 fusion.89
  426.9 8.3 %add_convert_fusion.4 = bf16[768,1024]{1,0:T(8,128)(2,1)} fusion(f32[768,1024]{1,0:T(8,128)S(1)} %get-tuple-element.171, bf16[768,2624]{1,0:T(8,128)(2,1)S(1)} %copy-done.33, bf16[1024,2624]{1,0:T(8,128)(2,1)} %bitcast.593), kind=kOutput, calls=%fused_computation.112 | convolution fusion | flops 4128768000 | bytes 14123008 | tf_op jit(solution)/shard_map/dot_general | solution.py:201
  435.2 6.5 collective-permute-done.64
  443.1 5.4 add_convert_fusion
  456.0 14.2 %multiply_reduce_fusion.6 = (f32[768]{0:T(1024)S(1)}, f32[768]{0:T(1024)S(1)}, f32[768,1024]{1,0:T(8,128)S(1)}) fusion(f32[1024]{0:T(1024)S(1)} %copy-done.90, f32[768]{0:T(1024)S(1)} %copy-done.94, f32[768,1024]{1,0:T(8,128)S(1)} %get-tuple-element.171, f32[768]{0:T(1024)S(1)} %copy-done.85, bf16[768,5248]{1,0:T(8,128)(2,1)} %pad_maximum_fusion, ...), kind=kOutput, calls=%fused_computation.123 | convolution fusion | flops 8259106816 | bytes 25116672 | tf_op jit(solution)/shard_map/dot_general | solution.py:201
  474.8 12.3 %collective-permute-done.66 = bf16[4,2,32,2560]{3,2,0,1:T(8,128)(2,1)} collective-permute-done((bf16[4,2,32,2560]{3,2,0,1:T(8,128)(2,1)}, bf16[4,2,32,2560]{3,2,0,1:T(8,128)(2,1)}, u32[]{:S(2)}, u32[]{:S(2)}) %collective-permute-start.66) | collective-permute-done | bytes 1310752 | tf_op jit(solution)/shard_map/ppermute | solution.py:40
  501.6 5.6 multiply_reduce_fusion.2
  525.0 8.3 %collective-permute-done.70 = bf16[4,32,2560]{2,1,0:T(8,128)(2,1)S(1)} collective-permute-done((bf16[4,32,2560]{2,1,0:T(8,128)(2,1)S(1)}, bf16[4,32,2560]{2,1,0:T(8,128)(2,1)S(1)}, u32[]{:S(2)}, u32[]{:S(2)}) %collective-permute-start.70) | collective-permute-done | bytes 655392 | tf_op jit(solution)/shard_map/ppermute | solution.py:40
  540.6 8.0 %multiply_reduce_fusion = (f32[16,256]{1,0:T(8,128)S(1)}, f32[16,256,384]{2,1,0:T(8,128)}) fusion(f32[16,256,384]{2,1,0:T(8,128)} %copy-done, f32[16,256]{1,0:T(8,128)S(1)} %log_add_fusion, bf16[256,16,64]{0,2,1:T(8,128)(2,1)} %bitcast.594, bf16[384,16,64]{0,2,1:T(8,128)(2,1)} %bitcast.600), kind=kOutput, calls=%fused_computation.34 | convolution fusion | flops 206041088 | bytes 13926400 | tf_op jit(solution)/shard_map/qhd,khd->hqk/dot_general | solution.py:350
  552.2 4.8 multiply_reduce_fusion.1
  587.8 11.4 %collective-permute-done.77 = bf16[32,2688]{1,0:T(8,128)(2,1)S(1)} collective-permute-done((bf16[32,2688]{1,0:T(8,128)(2,1)S(1)}, bf16[32,2688]{1,0:T(8,128)(2,1)S(1)}, u32[]{:S(2)}, u32[]{:S(2)}) %collective-permute-start.77) | collective-permute-done | bytes 172064 | tf_op jit(solution)/shard_map/ppermute | solution.py:40
  611.6 4.3 slice.377
  618.5 6.7 scatter-add.21
  625.1 9.3 %collective-permute-start.106 = (bf16[32,1344]{1,0:T(8,128)(2,1)}, bf16[32,1344]{1,0:T(8,128)(2,1)}, u32[]{:S(2)}, u32[]{:S(2)}) collective-permute-start(bf16[32,1344]{1,0:T(8,128)(2,1)} %get-tuple-element.218), channel_id=1, source_target_pairs={{0,16},{1,17},{2,18},{3,19},{4,20},{5,21},{6,22},{7,23},{8,24},{9,... | collective-permute-start | bytes 258056 | tf_op jit(solution)/shard_map/ppermute | solution.py:40
  637.2 6.3 scatter-add.24
  651.0 4.6 fusion.45
  655.7 7.9 %convolution_convert_fusion.1 = bf16[1024,3072]{1,0:T(8,128)(2,1)S(1)} fusion(bf16[768,1024]{1,0:T(8,128)(2,1)S(1)} %copy-done.4, f32[1024]{0:T(1024)S(1)} %copy-done.88, f32[768]{0:T(1024)S(1)} %copy-done.92, f32[768]{0:T(1024)S(1)} %copy-done.83, bf16[768,1024]{0,1:T(8,128)(2,1)} %slice.498, bf16[768,1024]{0,1:T(8,128)(2,1)} %get-tuple-element.223, ...), kind=kOutput, calls=%fused_computation.51 | convolution fusion | flops 4853071872 | bytes 12593152 | tf_op jit(solution)/shard_map/dot_general | solution.py:195
  673.7 4.1 collective-permute-done.94
  692.9 5.9 multiply_reduce_fusion.5
  700.9 7.0 collective-permute-done.84
  711.5 6.4 collective-permute-done.85
  730.3 5.5 collective-permute-done.92
  (667 shorter events, 326.9 us)
Async XLA Ops:
  2.5 27.6 %collective-permute-start.4 = (bf16[32,1664]{1,0:T(8,128)(2,1)S(1)}, bf16[32,1664]{1,0:T(8,128)(2,1)S(1)}, u32[]{:S(2)}, u32[]{:S(2)}) collective-permute-start(bf16[32,1664]{1,0:T(8,128)(2,1)S(1)} %get-tuple-element.173), channel_id=1, source_target_pairs={{0,8},{1,9},{2,10},{3,11},{4,12},{5,13},{6,14},{7,15},{8,0},{9,1},... | collective-permute-start | bytes 319496 | tf_op jit(solution)/shard_map/ppermute | solution.py:40
  5.6 24.5 %collective-permute-start.5 = (bf16[32,1664]{1,0:T(8,128)(2,1)S(1)}, bf16[32,1664]{1,0:T(8,128)(2,1)S(1)}, u32[]{:S(2)}, u32[]{:S(2)}) collective-permute-start(bf16[32,1664]{1,0:T(8,128)(2,1)S(1)} %get-tuple-element.173), channel_id=1, source_target_pairs={{0,16},{1,17},{2,18},{3,19},{4,20},{5,21},{6,22},{7,23},{8,24},{9,... | collective-permute-start | bytes 319496 | tf_op jit(solution)/shard_map/ppermute | solution.py:40
  8.2 21.9 %collective-permute-start.6 = (bf16[32,1664]{1,0:T(8,128)(2,1)S(1)}, bf16[32,1664]{1,0:T(8,128)(2,1)S(1)}, u32[]{:S(2)}, u32[]{:S(2)}) collective-permute-start(bf16[32,1664]{1,0:T(8,128)(2,1)S(1)} %get-tuple-element.173), channel_id=1, source_target_pairs={{0,24},{1,25},{2,26},{3,27},{4,28},{5,29},{6,30},{7,31},{8,16},{9,... | collective-permute-start | bytes 319496 | tf_op jit(solution)/shard_map/ppermute | solution.py:40
  39.0 45.5 %collective-permute-start.8 = (bf16[4,32,1536]{2,1,0:T(8,128)(2,1)S(1)}, bf16[4,32,1536]{2,1,0:T(8,128)(2,1)S(1)}, u32[]{:S(2)}, u32[]{:S(2)}) collective-permute-start(bf16[4,32,1536]{2,1,0:T(8,128)(2,1)S(1)} %bitcast_dynamic-update-slice_fusion.60), channel_id=1, source_target_pairs={{0,1},{1,0},{2,3},{3,2},{4,5},{5,4},{6,7},{7,6},{8,9},{9,8},{10,11... | collective-permute-start | bytes 1179656 | tf_op jit(solution)/shard_map/ppermute | solution.py:40
  39.0 47.5 %collective-permute-start.10 = (bf16[4,32,1536]{2,1,0:T(8,128)(2,1)S(1)}, bf16[4,32,1536]{2,1,0:T(8,128)(2,1)S(1)}, u32[]{:S(2)}, u32[]{:S(2)}) collective-permute-start(bf16[4,32,1536]{2,1,0:T(8,128)(2,1)S(1)} %bitcast_dynamic-update-slice_fusion.60), channel_id=1, source_target_pairs={{0,4},{1,5},{2,6},{3,7},{4,0},{5,1},{6,2},{7,3},{8,12},{9,13},{10,... | collective-permute-start | bytes 1179656 | tf_op jit(solution)/shard_map/ppermute | solution.py:40
  40.5 45.7 %collective-permute-start.9 = (bf16[4,32,1536]{2,1,0:T(8,128)(2,1)}, bf16[4,32,1536]{2,1,0:T(8,128)(2,1)S(1)}, u32[]{:S(2)}, u32[]{:S(2)}) collective-permute-start(bf16[4,32,1536]{2,1,0:T(8,128)(2,1)} %collective-permute-done.3), channel_id=1, source_target_pairs={{0,1},{1,0},{2,3},{3,2},{4,5},{5,4},{6,7},{7,6},{8,9},{9,8},{10,11... | collective-permute-start | bytes 1179656 | tf_op jit(solution)/shard_map/ppermute | solution.py:40
  40.8 46.2 %collective-permute-start.12 = (bf16[4,32,1536]{2,1,0:T(8,128)(2,1)}, bf16[4,32,1536]{2,1,0:T(8,128)(2,1)S(1)}, u32[]{:S(2)}, u32[]{:S(2)}) collective-permute-start(bf16[4,32,1536]{2,1,0:T(8,128)(2,1)} %collective-permute-done.3), channel_id=1, source_target_pairs={{0,4},{1,5},{2,6},{3,7},{4,0},{5,1},{6,2},{7,3},{8,12},{9,13},{10,... | collective-permute-start | bytes 1179656 | tf_op jit(solution)/shard_map/ppermute | solution.py:40
  84.5 22.1 %collective-permute-start.14 = (bf16[4,32,1664]{2,1,0:T(8,128)(2,1)S(1)}, bf16[4,32,1664]{2,1,0:T(8,128)(2,1)S(1)}, u32[]{:S(2)}, u32[]{:S(2)}) collective-permute-start(bf16[4,32,1664]{2,1,0:T(8,128)(2,1)S(1)} %bitcast_dynamic-update-slice_fusion.56), channel_id=1, source_target_pairs={{0,1},{1,0},{2,3},{3,2},{4,5},{5,4},{6,7},{7,6},{8,9},{9,8},{10,11... | collective-permute-start | bytes 1277960 | tf_op jit(solution)/shard_map/ppermute | solution.py:40
  86.2 20.5 %collective-permute-start.15 = (bf16[4,32,1664]{2,1,0:T(8,128)(2,1)S(1)}, bf16[4,32,1664]{2,1,0:T(8,128)(2,1)S(1)}, u32[]{:S(2)}, u32[]{:S(2)}) collective-permute-start(bf16[4,32,1664]{2,1,0:T(8,128)(2,1)S(1)} %collective-permute-done.7), channel_id=1, source_target_pairs={{0,1},{1,0},{2,3},{3,2},{4,5},{5,4},{6,7},{7,6},{8,9},{9,8},{10,11... | collective-permute-start | bytes 1277960 | tf_op jit(solution)/shard_map/ppermute | solution.py:40
  86.9 19.0 %collective-permute-start.18 = (bf16[4,32,1664]{2,1,0:T(8,128)(2,1)S(1)}, bf16[4,32,1664]{2,1,0:T(8,128)(2,1)S(1)}, u32[]{:S(2)}, u32[]{:S(2)}) collective-permute-start(bf16[4,32,1664]{2,1,0:T(8,128)(2,1)S(1)} %collective-permute-done.7), channel_id=1, source_target_pairs={{0,2},{1,3},{2,0},{3,1},{4,6},{5,7},{6,4},{7,5},{8,10},{9,11},{10,... | collective-permute-start | bytes 1277960 | tf_op jit(solution)/shard_map/ppermute | solution.py:40
  88.6 17.3 %collective-permute-start.13 = (bf16[4,32,1536]{2,1,0:T(8,128)(2,1)S(1)}, bf16[4,32,1536]{2,1,0:T(8,128)(2,1)S(1)}, u32[]{:S(2)}, u32[]{:S(2)}) collective-permute-start(bf16[4,32,1536]{2,1,0:T(8,128)(2,1)S(1)} %collective-permute-done.12), channel_id=1, source_target_pairs={{0,1},{1,0},{2,3},{3,2},{4,5},{5,4},{6,7},{7,6},{8,9},{9,8},{10,11... | collective-permute-start | bytes 1179656 | tf_op jit(solution)/shard_map/ppermute | solution.py:40
  97.2 47.2 %collective-permute-start.26 = (bf16[32,3200]{1,0:T(8,128)(2,1)}, bf16[32,3200]{1,0:T(8,128)(2,1)}, u32[]{:S(2)}, u32[]{:S(2)}) collective-permute-start(bf16[32,3200]{1,0:T(8,128)(2,1)} %slice.342), channel_id=1, source_target_pairs={{0,24},{1,25},{2,26},{3,27},{4,28},{5,29},{6,30},{7,31},{8,16},{9,... | collective-permute-start | bytes 614408 | tf_op jit(solution)/shard_map/ppermute | solution.py:40
  145.4 29.6 %collective-permute-start.28 = (bf16[4,32,3200]{2,1,0:T(8,128)(2,1)S(1)}, bf16[4,32,3200]{2,1,0:T(8,128)(2,1)S(1)}, u32[]{:S(2)}, u32[]{:S(2)}) collective-permute-start(bf16[4,32,3200]{2,1,0:T(8,128)(2,1)S(1)} %bitcast_dynamic-update-slice_fusion.48), channel_id=1, source_target_pairs={{0,4},{1,5},{2,6},{3,7},{4,0},{5,1},{6,2},{7,3},{8,12},{9,13},{10,... | collective-permute-start | bytes 2457608 | tf_op jit(solution)/shard_map/ppermute | solution.py:40
  150.1 24.9 %collective-permute-start.27 = (bf16[4,32,3072]{2,1,0:T(8,128)(2,1)S(1)}, bf16[4,32,3072]{2,1,0:T(8,128)(2,1)S(1)}, u32[]{:S(2)}, u32[]{:S(2)}) collective-permute-start(bf16[4,32,3072]{2,1,0:T(8,128)(2,1)S(1)} %copy-done.41), channel_id=1, source_target_pairs={{0,2},{1,3},{2,0},{3,1},{4,6},{5,7},{6,4},{7,5},{8,10},{9,11},{10,... | collective-permute-start | bytes 2359304 | tf_op jit(solution)/shard_map/ppermute | solution.py:40
  175.6 40.1 %collective-permute-start.46 = (bf16[32,1344]{1,0:T(8,128)(2,1)}, bf16[32,1344]{1,0:T(8,128)(2,1)}, u32[]{:S(2)}, u32[]{:S(2)}) collective-permute-start(bf16[32,1344]{1,0:T(8,128)(2,1)} %slice.358), channel_id=1, source_target_pairs={{0,8},{1,9},{2,10},{3,11},{4,12},{5,13},{6,14},{7,15},{8,0},{9,1},... | collective-permute-start | bytes 258056 | tf_op jit(solution)/shard_map/ppermute | solution.py:40
  175.6 41.3 %collective-permute-start.47 = (bf16[32,1344]{1,0:T(8,128)(2,1)}, bf16[32,1344]{1,0:T(8,128)(2,1)}, u32[]{:S(2)}, u32[]{:S(2)}) collective-permute-start(bf16[32,1344]{1,0:T(8,128)(2,1)} %slice.358), channel_id=1, source_target_pairs={{0,16},{1,17},{2,18},{3,19},{4,20},{5,21},{6,22},{7,23},{8,24},{9,... | collective-permute-start | bytes 258056 | tf_op jit(solution)/shard_map/ppermute | solution.py:40
  178.7 39.5 %collective-permute-start.48 = (bf16[32,1344]{1,0:T(8,128)(2,1)}, bf16[32,1344]{1,0:T(8,128)(2,1)}, u32[]{:S(2)}, u32[]{:S(2)}) collective-permute-start(bf16[32,1344]{1,0:T(8,128)(2,1)} %slice.358), channel_id=1, source_target_pairs={{0,24},{1,25},{2,26},{3,27},{4,28},{5,29},{6,30},{7,31},{8,16},{9,... | collective-permute-start | bytes 258056 | tf_op jit(solution)/shard_map/ppermute | solution.py:40
  180.7 26.5 %collective-permute-start.42 = (bf16[32,1280]{1,0:T(8,128)(2,1)}, bf16[32,1280]{1,0:T(8,128)(2,1)}, u32[]{:S(2)}, u32[]{:S(2)}) collective-permute-start(bf16[32,1280]{1,0:T(8,128)(2,1)} %slice.357), channel_id=1, source_target_pairs={{0,8},{1,9},{2,10},{3,11},{4,12},{5,13},{6,14},{7,15},{8,0},{9,1},... | collective-permute-start | bytes 245768 | tf_op jit(solution)/shard_map/ppermute | solution.py:40
  180.7 29.3 %collective-permute-start.43 = (bf16[32,1280]{1,0:T(8,128)(2,1)}, bf16[32,1280]{1,0:T(8,128)(2,1)}, u32[]{:S(2)}, u32[]{:S(2)}) collective-permute-start(bf16[32,1280]{1,0:T(8,128)(2,1)} %slice.357), channel_id=1, source_target_pairs={{0,16},{1,17},{2,18},{3,19},{4,20},{5,21},{6,22},{7,23},{8,24},{9,... | collective-permute-start | bytes 245768 | tf_op jit(solution)/shard_map/ppermute | solution.py:40
  213.6 20.4 %collective-permute-start.32 = (bf16[4,32,3072]{2,1,0:T(8,128)(2,1)S(1)}, bf16[4,32,3072]{2,1,0:T(8,128)(2,1)S(1)}, u32[]{:S(2)}, u32[]{:S(2)}) collective-permute-start(bf16[4,32,3072]{2,1,0:T(8,128)(2,1)S(1)} %copy-done.42), channel_id=1, source_target_pairs={{0,4},{1,5},{2,6},{3,7},{4,0},{5,1},{6,2},{7,3},{8,12},{9,13},{10,... | collective-permute-start | bytes 2359304 | tf_op jit(solution)/shard_map/ppermute | solution.py:40
  217.0 33.3 %collective-permute-start.34 = (bf16[4,32,3072]{2,1,0:T(8,128)(2,1)}, bf16[4,32,3072]{2,1,0:T(8,128)(2,1)S(1)}, u32[]{:S(2)}, u32[]{:S(2)}) collective-permute-start(bf16[4,32,3072]{2,1,0:T(8,128)(2,1)} %copy-done.66), channel_id=1, source_target_pairs={{0,4},{1,5},{2,6},{3,7},{4,0},{5,1},{6,2},{7,3},{8,12},{9,13},{10,... | collective-permute-start | bytes 2359304 | tf_op jit(solution)/shard_map/ppermute | solution.py:40
  218.2 38.3 %collective-permute-start.36 = (bf16[4,32,3200]{2,1,0:T(8,128)(2,1)S(1)}, bf16[4,32,3200]{2,1,0:T(8,128)(2,1)S(1)}, u32[]{:S(2)}, u32[]{:S(2)}) collective-permute-start(bf16[4,32,3200]{2,1,0:T(8,128)(2,1)S(1)} %copy-done.37), channel_id=1, source_target_pairs={{0,1},{1,0},{2,3},{3,2},{4,5},{5,4},{6,7},{7,6},{8,9},{9,8},{10,11... | collective-permute-start | bytes 2457608 | tf_op jit(solution)/shard_map/ppermute | solution.py:40
  219.4 38.8 %collective-permute-start.38 = (bf16[4,32,3200]{2,1,0:T(8,128)(2,1)S(1)}, bf16[4,32,3200]{2,1,0:T(8,128)(2,1)S(1)}, u32[]{:S(2)}, u32[]{:S(2)}) collective-permute-start(bf16[4,32,3200]{2,1,0:T(8,128)(2,1)S(1)} %copy-done.37), channel_id=1, source_target_pairs={{0,2},{1,3},{2,0},{3,1},{4,6},{5,7},{6,4},{7,5},{8,10},{9,11},{10,... | collective-permute-start | bytes 2457608 | tf_op jit(solution)/shard_map/ppermute | solution.py:40
  223.6 49.7 %collective-permute-start.37 = (bf16[4,32,3200]{2,1,0:T(8,128)(2,1)S(1)}, bf16[4,32,3200]{2,1,0:T(8,128)(2,1)S(1)}, u32[]{:S(2)}, u32[]{:S(2)}) collective-permute-start(bf16[4,32,3200]{2,1,0:T(8,128)(2,1)S(1)} %collective-permute-done.28), channel_id=1, source_target_pairs={{0,1},{1,0},{2,3},{3,2},{4,5},{5,4},{6,7},{7,6},{8,9},{9,8},{10,11... | collective-permute-start | bytes 2457608 | tf_op jit(solution)/shard_map/ppermute | solution.py:40
  250.2 21.2 %collective-permute-start.40 = (bf16[4,32,3200]{2,1,0:T(8,128)(2,1)S(1)}, bf16[4,32,3200]{2,1,0:T(8,128)(2,1)S(1)}, u32[]{:S(2)}, u32[]{:S(2)}) collective-permute-start(bf16[4,32,3200]{2,1,0:T(8,128)(2,1)S(1)} %collective-permute-done.28), channel_id=1, source_target_pairs={{0,2},{1,3},{2,0},{3,1},{4,6},{5,7},{6,4},{7,5},{8,10},{9,11},{10,... | collective-permute-start | bytes 2457608 | tf_op jit(solution)/shard_map/ppermute | solution.py:40
  252.7 29.0 %collective-permute-start.45 = (bf16[4,32,1280]{2,1,0:T(8,128)(2,1)}, bf16[4,32,1280]{2,1,0:T(8,128)(2,1)}, u32[]{:S(2)}, u32[]{:S(2)}) collective-permute-start(bf16[4,32,1280]{2,1,0:T(8,128)(2,1)} %bitcast_dynamic-update-slice_fusion.68), channel_id=1, source_target_pairs={{0,2},{1,3},{2,0},{3,1},{4,6},{5,7},{6,4},{7,5},{8,10},{9,11},{10,... | collective-permute-start | bytes 983048 | tf_op jit(solution)/shard_map/ppermute | solution.py:40
  256.5 25.2 %collective-permute-start.49 = (bf16[4,32,1344]{2,1,0:T(8,128)(2,1)S(1)}, bf16[4,32,1344]{2,1,0:T(8,128)(2,1)S(1)}, u32[]{:S(2)}, u32[]{:S(2)}) collective-permute-start(bf16[4,32,1344]{2,1,0:T(8,128)(2,1)S(1)} %bitcast_dynamic-update-slice_fusion.64), channel_id=1, source_target_pairs={{0,4},{1,5},{2,6},{3,7},{4,0},{5,1},{6,2},{7,3},{8,12},{9,13},{10,... | collective-permute-start | bytes 1032200 | tf_op jit(solution)/shard_map/ppermute | solution.py:40
  281.8 21.6 %collective-permute-start.50 = (bf16[4,32,1280]{2,1,0:T(8,128)(2,1)}, bf16[4,32,1280]{2,1,0:T(8,128)(2,1)}, u32[]{:S(2)}, u32[]{:S(2)}) collective-permute-start(bf16[4,32,1280]{2,1,0:T(8,128)(2,1)} %bitcast_dynamic-update-slice_fusion.68), channel_id=1, source_target_pairs={{0,1},{1,0},{2,3},{3,2},{4,5},{5,4},{6,7},{7,6},{8,9},{9,8},{10,11... | collective-permute-start | bytes 983048 | tf_op jit(solution)/shard_map/ppermute | solution.py:40
  282.4 25.9 %collective-permute-start.52 = (bf16[4,32,1280]{2,1,0:T(8,128)(2,1)}, bf16[4,32,1280]{2,1,0:T(8,128)(2,1)}, u32[]{:S(2)}, u32[]{:S(2)}) collective-permute-start(bf16[4,32,1280]{2,1,0:T(8,128)(2,1)} %bitcast_dynamic-update-slice_fusion.68), channel_id=1, source_target_pairs={{0,4},{1,5},{2,6},{3,7},{4,0},{5,1},{6,2},{7,3},{8,12},{9,13},{10,... | collective-permute-start | bytes 983048 | tf_op jit(solution)/shard_map/ppermute | solution.py:40
  284.0 22.5 %collective-permute-start.51 = (bf16[4,32,1280]{2,1,0:T(8,128)(2,1)}, bf16[4,32,1280]{2,1,0:T(8,128)(2,1)}, u32[]{:S(2)}, u32[]{:S(2)}) collective-permute-start(bf16[4,32,1280]{2,1,0:T(8,128)(2,1)} %collective-permute-done.45), channel_id=1, source_target_pairs={{0,1},{1,0},{2,3},{3,2},{4,5},{5,4},{6,7},{7,6},{8,9},{9,8},{10,11... | collective-permute-start | bytes 983048 | tf_op jit(solution)/shard_map/ppermute | solution.py:40
  284.0 26.3 %collective-permute-start.54 = (bf16[4,32,1280]{2,1,0:T(8,128)(2,1)}, bf16[4,32,1280]{2,1,0:T(8,128)(2,1)}, u32[]{:S(2)}, u32[]{:S(2)}) collective-permute-start(bf16[4,32,1280]{2,1,0:T(8,128)(2,1)} %collective-permute-done.45), channel_id=1, source_target_pairs={{0,4},{1,5},{2,6},{3,7},{4,0},{5,1},{6,2},{7,3},{8,12},{9,13},{10,... | collective-permute-start | bytes 983048 | tf_op jit(solution)/shard_map/ppermute | solution.py:40
  284.4 39.0 %collective-permute-start.56 = (bf16[4,32,1344]{2,1,0:T(8,128)(2,1)S(1)}, bf16[4,32,1344]{2,1,0:T(8,128)(2,1)}, u32[]{:S(2)}, u32[]{:S(2)}) collective-permute-start(bf16[4,32,1344]{2,1,0:T(8,128)(2,1)S(1)} %bitcast_dynamic-update-slice_fusion.64), channel_id=1, source_target_pairs={{0,1},{1,0},{2,3},{3,2},{4,5},{5,4},{6,7},{7,6},{8,9},{9,8},{10,11... | collective-permute-start | bytes 1032200 | tf_op jit(solution)/shard_map/ppermute | solution.py:40
  419.0 24.1 %collective-permute-start.63 = (bf16[16,1,32,5248]{3,2,0,1:T(8,128)(2,1)}, bf16[16,1,32,5248]{3,2,0,1:T(8,128)(2,1)}, u32[]{:S(2)}, u32[]{:S(2)}) collective-permute-start(bf16[16,1,32,5248]{3,2,0,1:T(8,128)(2,1)} %dynamic-slice_bitcast_fusion), channel_id=1, source_target_pairs={{0,1},{1,0},{2,3},{3,2},{4,5},{5,4},{6,7},{7,6},{8,9},{9,8},{10,11... | collective-permute-start | bytes 16121864 | tf_op jit(solution)/shard_map/ppermute | solution.py:40
  424.8 18.1 %collective-permute-start.65 = (bf16[4,2,32,1344]{3,2,1,0:T(8,128)(2,1)S(1)}, bf16[4,2,32,1344]{3,2,1,0:T(8,128)(2,1)S(1)}, u32[]{:S(2)}, u32[]{:S(2)}) collective-permute-start(bf16[4,2,32,1344]{3,2,1,0:T(8,128)(2,1)S(1)} %dynamic-slice_bitcast_fusion.7), channel_id=1, source_target_pairs={{0,2},{1,3},{2,0},{3,1},{4,6},{5,7},{6,4},{7,5},{8,10},{9,11},{10,... | collective-permute-start | bytes 2064392 | tf_op jit(solution)/shard_map/ppermute | solution.py:40
  449.4 24.6 %collective-permute-start.69 = (bf16[4,32,1344]{2,1,0:T(8,128)(2,1)S(1)}, bf16[4,32,1344]{2,1,0:T(8,128)(2,1)S(1)}, u32[]{:S(2)}, u32[]{:S(2)}) collective-permute-start(bf16[4,32,1344]{2,1,0:T(8,128)(2,1)S(1)} %dynamic-slice_bitcast_fusion.13), channel_id=1, source_target_pairs={{0,4},{1,5},{2,6},{3,7},{4,0},{5,1},{6,2},{7,3},{8,12},{9,13},{10,... | collective-permute-start | bytes 1032200 | tf_op jit(solution)/shard_map/ppermute | solution.py:40
  451.1 22.0 %collective-permute-start.68 = (bf16[4,32,1280]{2,1,0:T(8,128)(2,1)S(1)}, bf16[4,32,1280]{2,1,0:T(8,128)(2,1)S(1)}, u32[]{:S(2)}, u32[]{:S(2)}) collective-permute-start(bf16[4,32,1280]{2,1,0:T(8,128)(2,1)S(1)} %dynamic-slice_bitcast_fusion.14), channel_id=1, source_target_pairs={{0,2},{1,3},{2,0},{3,1},{4,6},{5,7},{6,4},{7,5},{8,10},{9,11},{10,... | collective-permute-start | bytes 983048 | tf_op jit(solution)/shard_map/ppermute | solution.py:40
  453.0 36.2 %collective-permute-start.67 = (bf16[4,2,32,2688]{3,2,1,0:T(8,128)(2,1)}, bf16[4,2,32,2688]{3,2,1,0:T(8,128)(2,1)}, u32[]{:S(2)}, u32[]{:S(2)}) collective-permute-start(bf16[4,2,32,2688]{3,2,1,0:T(8,128)(2,1)} %dynamic-slice_bitcast_fusion.2), channel_id=1, source_target_pairs={{0,2},{1,3},{2,0},{3,1},{4,6},{5,7},{6,4},{7,5},{8,10},{9,11},{10,... | collective-permute-start | bytes 4128776 | tf_op jit(solution)/shard_map/ppermute | solution.py:40
  455.6 31.6 %collective-permute-start.66 = (bf16[4,2,32,2560]{3,2,0,1:T(8,128)(2,1)}, bf16[4,2,32,2560]{3,2,0,1:T(8,128)(2,1)}, u32[]{:S(2)}, u32[]{:S(2)}) collective-permute-start(bf16[4,2,32,2560]{3,2,0,1:T(8,128)(2,1)} %dynamic-slice_bitcast_fusion.3), channel_id=1, source_target_pairs={{0,4},{1,5},{2,6},{3,7},{4,0},{5,1},{6,2},{7,3},{8,12},{9,13},{10,... | collective-permute-start | bytes 3932168 | tf_op jit(solution)/shard_map/ppermute | solution.py:40
  511.9 152.1 %collective-permute-start.102 = (bf16[32,1280]{1,0:T(8,128)(2,1)}, bf16[32,1280]{1,0:T(8,128)(2,1)}, u32[]{:S(2)}, u32[]{:S(2)}) collective-permute-start(bf16[32,1280]{1,0:T(8,128)(2,1)} %get-tuple-element.219), channel_id=1, source_target_pairs={{0,8},{1,9},{2,10},{3,11},{4,12},{5,13},{6,14},{7,15},{8,0},{9,1},... | collective-permute-start | bytes 245768 | tf_op jit(solution)/shard_map/ppermute | solution.py:40
  511.9 154.0 %collective-permute-start.103 = (bf16[32,1280]{1,0:T(8,128)(2,1)}, bf16[32,1280]{1,0:T(8,128)(2,1)}, u32[]{:S(2)}, u32[]{:S(2)}) collective-permute-start(bf16[32,1280]{1,0:T(8,128)(2,1)} %get-tuple-element.221), channel_id=1, source_target_pairs={{0,16},{1,17},{2,18},{3,19},{4,20},{5,21},{6,22},{7,23},{8,24},{9,... | collective-permute-start | bytes 245768 | tf_op jit(solution)/shard_map/ppermute | solution.py:40
  514.5 20.8 %collective-permute-start.72 = (bf16[16,1,32,1024]{3,2,0,1:T(8,128)(2,1)S(1)}, bf16[16,1,32,1024]{3,2,0,1:T(8,128)(2,1)S(1)}, u32[]{:S(2)}, u32[]{:S(2)}) collective-permute-start(bf16[16,1,32,1024]{3,2,0,1:T(8,128)(2,1)S(1)} %dynamic-slice_bitcast_fusion.4), channel_id=1, source_target_pairs={{0,1},{1,0},{2,3},{3,2},{4,5},{5,4},{6,7},{7,6},{8,9},{9,8},{10,11... | collective-permute-start | bytes 3145736 | tf_op jit(solution)/shard_map/ppermute | solution.py:40
  514.6 19.6 %collective-permute-start.71 = (bf16[4,32,2688]{2,1,0:T(8,128)(2,1)S(1)}, bf16[4,32,2688]{2,1,0:T(8,128)(2,1)S(1)}, u32[]{:S(2)}, u32[]{:S(2)}) collective-permute-start(bf16[4,32,2688]{2,1,0:T(8,128)(2,1)S(1)} %dynamic-slice_bitcast_fusion.8), channel_id=1, source_target_pairs={{0,4},{1,5},{2,6},{3,7},{4,0},{5,1},{6,2},{7,3},{8,12},{9,13},{10,... | collective-permute-start | bytes 2064392 | tf_op jit(solution)/shard_map/ppermute | solution.py:40
  582.9 17.7 %collective-permute-start.78 = (bf16[32,2688]{1,0:T(8,128)(2,1)S(1)}, bf16[32,2688]{1,0:T(8,128)(2,1)S(1)}, u32[]{:S(2)}, u32[]{:S(2)}) collective-permute-start(bf16[32,2688]{1,0:T(8,128)(2,1)S(1)} %get-tuple-element.205), channel_id=1, source_target_pairs={{0,24},{1,25},{2,26},{3,27},{4,28},{5,29},{6,30},{7,31},{8,16},{9,... | collective-permute-start | bytes 516104 | tf_op jit(solution)/shard_map/ppermute | solution.py:40
  586.5 79.3 %collective-permute-start.104 = (bf16[32,1280]{1,0:T(8,128)(2,1)}, bf16[32,1280]{1,0:T(8,128)(2,1)}, u32[]{:S(2)}, u32[]{:S(2)}) collective-permute-start(bf16[32,1280]{1,0:T(8,128)(2,1)} %get-tuple-element.220), channel_id=1, source_target_pairs={{0,24},{1,25},{2,26},{3,27},{4,28},{5,29},{6,30},{7,31},{8,16},{9,... | collective-permute-start | bytes 245768 | tf_op jit(solution)/shard_map/ppermute | solution.py:40
  605.6 61.3 %collective-permute-start.105 = (bf16[32,1344]{1,0:T(8,128)(2,1)}, bf16[32,1344]{1,0:T(8,128)(2,1)}, u32[]{:S(2)}, u32[]{:S(2)}) collective-permute-start(bf16[32,1344]{1,0:T(8,128)(2,1)} %get-tuple-element.216), channel_id=1, source_target_pairs={{0,8},{1,9},{2,10},{3,11},{4,12},{5,13},{6,14},{7,15},{8,0},{9,1},... | collective-permute-start | bytes 258056 | tf_op jit(solution)/shard_map/ppermute | solution.py:40
  625.1 41.8 %collective-permute-start.106 = (bf16[32,1344]{1,0:T(8,128)(2,1)}, bf16[32,1344]{1,0:T(8,128)(2,1)}, u32[]{:S(2)}, u32[]{:S(2)}) collective-permute-start(bf16[32,1344]{1,0:T(8,128)(2,1)} %get-tuple-element.218), channel_id=1, source_target_pairs={{0,16},{1,17},{2,18},{3,19},{4,20},{5,21},{6,22},{7,23},{8,24},{9,... | collective-permute-start | bytes 258056 | tf_op jit(solution)/shard_map/ppermute | solution.py:40
  665.8 23.8 %collective-permute-start.83 = (bf16[16,1,32,3072]{3,2,0,1:T(8,128)(2,1)S(1)}, bf16[16,1,32,3072]{3,2,0,1:T(8,128)(2,1)S(1)}, u32[]{:S(2)}, u32[]{:S(2)}) collective-permute-start(bf16[16,1,32,3072]{3,2,0,1:T(8,128)(2,1)S(1)} %dynamic-slice_bitcast_fusion.1), channel_id=1, source_target_pairs={{0,1},{1,0},{2,3},{3,2},{4,5},{5,4},{6,7},{7,6},{8,9},{9,8},{10,11... | collective-permute-start | bytes 9437192 | tf_op jit(solution)/shard_map/ppermute | solution.py:40
  691.8 19.4 %collective-permute-start.89 = (bf16[4,2,32,1536]{3,2,1,0:T(8,128)(2,1)S(1)}, bf16[4,2,32,1536]{3,2,1,0:T(8,128)(2,1)S(1)}, u32[]{:S(2)}, u32[]{:S(2)}) collective-permute-start(bf16[4,2,32,1536]{3,2,1,0:T(8,128)(2,1)S(1)} %dynamic-slice_bitcast_fusion.5), channel_id=1, source_target_pairs={{0,2},{1,3},{2,0},{3,1},{4,6},{5,7},{6,4},{7,5},{8,10},{9,11},{10,... | collective-permute-start | bytes 2359304 | tf_op jit(solution)/shard_map/ppermute | solution.py:40
  (174 other events, 2876.9 us)
